TPU v7x, 32 devices: a whole 2x2x4 slice. The times are simulated.
32 devices in a mesh: stream: 4 (over y, x), seq: 8 (over z, core).
Axes of the slice: x: 2, y: 2, z: 4, core: 2. Of those that a mesh axis runs over, the one named last changes fastest.
Arguments:
- conv_input: bfloat16 [4, 32768, 1280], P('stream', 'seq'), may hold values from -6 to 6
- conv_weight: float32 [4, 1280], replicated, may hold values from -3 to 3
- conv_bias: float32 [1280], replicated, may hold values from -1 to 1
- step_size: float32 [4, 16, 32768], P('stream', None, 'seq'), may hold values from 0.0005 to 0.005
- log_decay: float32 [4, 16, 32768], P('stream', None, 'seq'), as said below
- skip_gain: float32 [16], replicated, may hold values from 0.5 to 1.5
- doc_bounds: int32 [4, 32], P('stream'), may hold values from 1 to 32768, as said below
- doc_owner: int32 [4, 32], P('stream'), may hold values from 0 to 3, as said below
Outputs:
- mixed_out: bfloat16 [4, 32768, 1024], P('stream', 'seq')
- handoff_ssm: float32 [4, 8, 4, 2, 16, 64, 128], P('stream', 'seq')
- handoff_conv: bfloat16 [4, 8, 4, 2, 3, 1280], P('stream', 'seq')
Inputs may be any that keep to these rules, and one draw needn't show every extreme that they name: `doc_bounds`: each row rises and never falls; the real documents of a stream end at 32768, after which every entry equals 32768. At most 4 real documents have their last position in one run of 4096 positions starting at a multiple of 4096. `doc_owner`: among the real documents whose last positions lie in one such run of one stream, no owner is named more than 2 times. `log_decay`: never positive.
All inputs are finite; a program needn't handle non-finite values.
Results may differ from a plain program's by a relative error of at most 0.006.
Values may be sent and summed in bfloat16 or wider, within the bound.
No kernel may reach another device: no remote copies, remote signals or barrier semaphores. Data moves between devices by JAX's collectives and lax.ppermute only.
A program may use at most 256 MiB of HBM per device.

v0:
```python
import jax
import jax.numpy as jnp
from jax import lax
from jax.sharding import PartitionSpec as P

P_SIZE = 64
N = 128
SPAN = 256
EMAX = 4
CAP = 2


def shifted(value, axis, steps):
    count = lax.axis_size(axis)
    leading, last = (max(0, -steps), min(count, count - steps))
    return lax.ppermute(value, axis, [(source, source + steps) for source in range(leading, last)])


def split_state(state):
    state_hi = state.astype(jnp.bfloat16)
    state_lo = (state - state_hi.astype(jnp.float32)).astype(jnp.bfloat16)
    return (state_hi, state_lo)


def span_output(
    x_span, b_span, c_span, dt_span, cum_decay, doc_span, prev_doc, state_in, skip_gain
):
    row_count = doc_span.shape[0]
    head_count = dt_span.shape[0]
    scores = jnp.einsum("tn,sn->ts", c_span, b_span, preferred_element_type=jnp.float32)
    position = jnp.arange(row_count)
    causal = (position[:, None] >= position[None, :]) & (doc_span[:, None] == doc_span[None, :])
    spread = cum_decay[:, :, None] - cum_decay[:, None, :]
    weights = jnp.where(
        causal[None],
        jnp.exp(jnp.where(causal[None], spread, 0.0)) * scores[None] * dt_span[:, None, :],
        0.0,
    ).astype(jnp.bfloat16)
    head_rows = x_span.reshape(row_count, head_count, -1)
    inner_part = jnp.einsum("hts,shp->thp", weights, head_rows, preferred_element_type=jnp.float32)
    entry_gate = jnp.where((doc_span == prev_doc)[None, :], jnp.exp(cum_decay), 0.0)
    state_hi, state_lo = split_state(state_in)
    outer_sum = jnp.einsum(
        "tn,hpn->thp", c_span, state_hi, preferred_element_type=jnp.float32
    ) + jnp.einsum("tn,hpn->thp", c_span, state_lo, preferred_element_type=jnp.float32)
    outer_part = outer_sum * entry_gate.T[:, :, None]
    summed = inner_part + outer_part + skip_gain[None, :, None] * head_rows.astype(jnp.float32)
    return summed.reshape(row_count, -1)


def carry_in(end_state, shard_gate, shard):
    head_count = shard_gate.shape[0]
    zeros_state = jnp.zeros(end_state.shape, jnp.float32)
    gates_all = lax.all_gather(shard_gate[None, :], "seq", axis=0, tiled=True)
    count = gates_all.shape[0]
    index_list = jnp.arange(count)
    before_me = (index_list < shard)[:, None]
    through = jnp.where(before_me, gates_all, 1.0)
    suffix = jnp.flip(jnp.cumprod(jnp.flip(through, 0), 0), 0)
    weights = jnp.where(
        before_me, jnp.concatenate([suffix[1:], jnp.ones((1, head_count), jnp.float32)], 0), 0.0
    )
    return zeros_state + jnp.sum(
        weights[:, :, None, None]
        * lax.all_gather(end_state[None].astype(jnp.bfloat16), "seq", axis=0, tiled=True).astype(
            jnp.float32
        ),
        0,
    )


def on_device(
    conv_input, conv_weight, conv_bias, step_size, log_decay, skip_gain, doc_bounds, doc_owner
):
    tok_count = conv_input.shape[1]
    head_count = step_size.shape[1]
    width = head_count * P_SIZE
    lag_rows = conv_weight.shape[0] - 1
    shard = lax.axis_index("seq")
    anchor = shard * tok_count
    rim_rows = shifted(conv_input[0, tok_count - lag_rows :], "seq", 1)
    padded = jnp.concatenate([rim_rows, conv_input[0]], 0)
    end_list = doc_bounds[0]
    owner_row = doc_owner[0]
    places = anchor - lag_rows + jnp.arange(tok_count + lag_rows, dtype=jnp.int32)
    docs_all = jnp.sum((end_list[None, :] <= places[:, None]).astype(jnp.int32), axis=1)
    own_doc = docs_all[lag_rows:]
    mixed_sum = conv_bias[None, :] + conv_weight[0][None, :] * conv_input[0].astype(jnp.float32)
    for lag_step in range(1, lag_rows + 1):
        moved_rows = padded[lag_rows - lag_step : lag_rows - lag_step + tok_count].astype(
            jnp.float32
        )
        same_doc = docs_all[lag_rows - lag_step : lag_rows - lag_step + tok_count] == own_doc
        mixed_sum = mixed_sum + conv_weight[lag_step][None, :] * jnp.where(
            same_doc[:, None], moved_rows, 0.0
        )
    activated = jax.nn.silu(mixed_sum).astype(jnp.bfloat16)
    count = tok_count // SPAN
    x_spans = activated[:, :width].reshape(count, SPAN, width)
    b_spans = activated[:, width : width + N].reshape(count, SPAN, N)
    c_spans = activated[:, width + N :].reshape(count, SPAN, N)
    dt_spans = step_size[0].reshape(head_count, count, SPAN).transpose(1, 0, 2)
    ld_spans = log_decay[0].reshape(head_count, count, SPAN).transpose(1, 0, 2)
    cum_spans = jnp.cumsum(ld_spans, axis=2)
    doc_spans = own_doc.reshape(count, SPAN)
    prev_docs = docs_all[lag_rows - 1 : lag_rows - 1 + tok_count : SPAN]
    end_weight = jnp.where(
        doc_spans[:, None, :] == doc_spans[:, None, -1:],
        jnp.exp(cum_spans[:, :, -1:] - cum_spans) * dt_spans,
        0.0,
    )
    loaded = (
        end_weight.transpose(0, 2, 1)[..., None]
        * x_spans.reshape(count, SPAN, head_count, P_SIZE).astype(jnp.float32)
    ).astype(jnp.bfloat16)
    block_states = jnp.einsum("cshp,csn->chpn", loaded, b_spans, preferred_element_type=jnp.float32)
    gates = jnp.where((doc_spans[:, -1] == prev_docs)[:, None], jnp.exp(cum_spans[:, :, -1]), 0.0)

    def advance(holding, item):
        block_state, gate = item
        return (block_state + gate[:, None, None] * holding, holding)

    end_state, hin_local = lax.scan(
        advance, jnp.zeros((head_count, P_SIZE, N), jnp.float32), (block_states, gates)
    )
    shard_gate = jnp.prod(gates, axis=0)
    lift = jnp.concatenate(
        [jnp.ones((1, head_count), jnp.float32), jnp.cumprod(gates, axis=0)[:-1]], 0
    )

    def span_rows(item):
        x_span, b_span, c_span, dt_span, cum_decay, doc_span, prev_doc, state_in = item
        return span_output(
            x_span, b_span, c_span, dt_span, cum_decay, doc_span, prev_doc, state_in, skip_gain
        )

    carried = carry_in(end_state, shard_gate, shard)
    hin_all = hin_local + lift[:, :, None, None] * carried
    out_rows = lax.map(
        span_rows, (x_spans, b_spans, c_spans, dt_spans, cum_spans, doc_spans, prev_docs, hin_all)
    ).astype(jnp.bfloat16)
    doc_index = jnp.arange(end_list.shape[0], dtype=jnp.int32)
    prior_end = jnp.concatenate([jnp.zeros((1,), jnp.int32), end_list[:-1]])
    real_docs = end_list > prior_end
    last_pos = jnp.clip(end_list - 1, 0, None)
    mine = real_docs & (last_pos >= anchor) & (last_pos < anchor + tok_count)
    earlier_doc = doc_index[None, :] < doc_index[:, None]
    owner_rank = jnp.sum(
        (mine[None, :] & (owner_row[None, :] == owner_row[:, None]) & earlier_doc).astype(
            jnp.int32
        ),
        axis=1,
    )
    order_rank = jnp.cumsum(mine.astype(jnp.int32)) - 1
    owner_count = lax.axis_size("stream")
    owner_ids = jnp.arange(owner_count)
    slot_ids = jnp.arange(CAP)
    ssm_send = jnp.zeros((owner_count, CAP, head_count, P_SIZE, N), jnp.float32)
    conv_send = jnp.zeros((owner_count, CAP, lag_rows, padded.shape[1]), jnp.bfloat16)
    for slot_index in range(EMAX):
        picked = mine & (order_rank == slot_index)
        valid = jnp.any(picked)
        doc_key = jnp.sum(jnp.where(picked, doc_index, 0))
        end_pos = jnp.sum(jnp.where(picked, end_list, 0))
        start_pos = jnp.sum(jnp.where(picked, prior_end, 0))
        target = jnp.sum(jnp.where(picked, owner_row, 0))
        slot_rank = jnp.sum(jnp.where(picked, owner_rank, 0))
        local_pos = jnp.clip(end_pos - 1 - anchor, 0, tok_count - 1)
        block = local_pos // SPAN
        offset = local_pos % SPAN
        x_span = lax.dynamic_index_in_dim(x_spans, block, 0, keepdims=False)
        b_span = lax.dynamic_index_in_dim(b_spans, block, 0, keepdims=False)
        dt_span = lax.dynamic_index_in_dim(dt_spans, block, 0, keepdims=False)
        cum_decay = lax.dynamic_index_in_dim(cum_spans, block, 0, keepdims=False)
        doc_span = lax.dynamic_index_in_dim(doc_spans, block, 0, keepdims=False)
        prev_doc = lax.dynamic_index_in_dim(prev_docs, block, 0, keepdims=False)
        state_in = lax.dynamic_index_in_dim(hin_all, block, 0, keepdims=False)
        kept_rows = (jnp.arange(SPAN) <= offset) & (doc_span == doc_key)
        scaled = jnp.where(
            kept_rows[None, :], jnp.exp(cum_decay[:, offset][:, None] - cum_decay) * dt_span, 0.0
        )
        slot_load = (
            scaled.T[:, :, None] * x_span.reshape(SPAN, head_count, P_SIZE).astype(jnp.float32)
        ).astype(jnp.bfloat16)
        final_state = jnp.einsum(
            "shp,sn->hpn", slot_load, b_span, preferred_element_type=jnp.float32
        )
        final_state = (
            final_state
            + jnp.where(prev_doc == doc_key, jnp.exp(cum_decay[:, offset]), 0.0)[:, None, None]
            * state_in
        )
        tail_rows = lax.dynamic_slice_in_dim(padded, local_pos + 1, lag_rows, 0)
        tail_pos = anchor + local_pos - (lag_rows - 1) + jnp.arange(lag_rows, dtype=jnp.int32)
        tail = jnp.where((tail_pos >= start_pos)[:, None], tail_rows, jnp.zeros_like(tail_rows))
        chosen = (owner_ids[:, None] == target) & (slot_ids[None, :] == slot_rank) & valid
        ssm_send = jnp.where(chosen[:, :, None, None, None], final_state[None, None], ssm_send)
        conv_send = jnp.where(chosen[:, :, None, None], tail[None, None], conv_send)
    got_ssm, got_conv = (
        lax.all_to_all(ssm_send, "stream", split_axis=0, concat_axis=0, tiled=True),
        lax.all_to_all(
            conv_send.astype(jnp.float32), "stream", split_axis=0, concat_axis=0, tiled=True
        ),
    )
    return (
        out_rows.reshape(1, tok_count, width),
        got_ssm[None, None],
        got_conv.astype(jnp.bfloat16)[None, None],
    )


def solution(mesh):
    in_specs = (
        P("stream", "seq", None),
        P(),
        P(),
        P("stream", None, "seq"),
        P("stream", None, "seq"),
        P(),
        P("stream", None),
        P("stream", None),
    )
    out_specs = (
        P("stream", "seq", None),
        P("stream", "seq", None, None, None, None, None),
        P("stream", "seq", None, None, None, None),
    )
    return jax.shard_map(
        on_device, mesh=mesh, in_specs=in_specs, out_specs=out_specs, check_vma=False
    )
```

profile of v0, /device:TPU:0, one launch (start us, length us, event | category | flops | bytes accessed | tf_op | source)
XLA Modules:
  0.0 396.7 jit_solution(17613506967836219099)
XLA Ops:
  7.9 2.3 collective-permute-start
  16.7 1.7 select_reduce_fusion.3
  23.4 9.1 %reduce-window.19 = f32[16,16,2,128]{3,1,2,0:T(8,128)S(1)} reduce-window(f32[16,16,2,128]{3,1,2,0:T(8,128)S(1)} %copy_bitcast_fusion.1, f32[]{:T(128)} %constant.285.clone.1), window={size=1x1x1x128 pad=0_0x0_0x0_0x127_0}, to_apply=%region_1.2 | reduce-window | flops 8323072 | bytes 524292 | tf_op jit(solution)/shard_map/reduce-window
  36.0 2.5 and_reduce_fusion.3
  49.2 17.2 %all-reduce.2 = f32[128]{0:T(128)S(1)} all-reduce(f32[128]{0:T(128)S(1)} %dynamic-update-slice), channel_id=2, replica_groups=mesh['stream'=4,'seq'=8] {'seq'}, use_global_device_ids=true, to_apply=%add.2 | all-reduce | flops 128 | bytes 1024
  66.5 28.8 %multiply_convert_fusion = bf16[4096,1280]{1,0:T(8,128)(2,1)S(1)} fusion(bf16[4096,1280]{1,0:T(8,128)(2,1)} %bitcast.256, bf16[3,1280]{1,0:T(4,128)(2,1)S(1)} %collective-permute-done, f32[1280]{0:T(1024)S(1)} %get-tuple-element.170, f32[1280]{0:T(1024)S(1)} %get-tuple-element.171, f32[1280]{0:T(1024)S(1)} %get-tuple-element.169, ...), kind=kLoop, calls=%fused_computation.51 | loop fusion | flops 152043520 | bytes 21017088 | tf_op jit(solution)/shard_map/convert_element_type | solution.py:97
  95.3 9.1 %slice_convert_fusion = (f32[4096,1024]{1,0:T(8,128)}, bf16[4096,1024]{1,0:T(8,128)(2,1)}) fusion(bf16[4096,1280]{1,0:T(8,128)(2,1)S(1)} %multiply_convert_fusion), kind=kLoop, calls=%fused_computation.224 | loop fusion | flops 4194304 | bytes 33554432 | tf_op jit(solution)/shard_map/convert_element_type | solution.py:114
  105.6 17.5 %copy.97 = f32[4096,1024]{0,1:T(8,128)} copy(f32[4096,1024]{1,0:T(8,128)} %get-tuple-element.250) | data formatting | bytes 33554432 | tf_op jit(solution)/shard_map/convert_element_type | solution.py:114
  123.1 11.0 %copy.123 = f32[128,8,16,256]{3,2,1,0:T(8,128)S(1)} copy(f32[128,8,16,256]{3,1,2,0:T(8,128)} %bitcast.252) | data formatting | bytes 33554432
  134.0 2.4 multiply_convert_fusion.1
  136.5 6.2 %fusion.33 = f32[16,16,64,128]{3,2,1,0:T(8,128)} fusion(bf16[16,256,128,1]{2,1,3,0:T(8,128)(2,1)S(1)} %bitcast.260, bf16[16,256,16,64]{1,0,3,2:T(8,128)(2,1)S(1)} %multiply_convert_fusion.1), kind=kOutput, calls=%fused_computation.60 | convolution fusion | flops 1073741824 | bytes 17825792 | tf_op jit(solution)/shard_map/cshp,csn->chpn/dot_general | solution.py:116
  142.7 32.4 %while.24 = (s32[]{:T(128)}, f32[16,64,128]{2,1,0:T(8,128)S(1)}, f32[16,16,64,128]{3,2,1,0:T(8,128)}, f32[16,16,64,128]{3,2,1,0:T(8,128)}, f32[16,16]{1,0:T(8,128)S(1)}, /*index=5*/s32[]{:T(128)}, s32[]{:T(128)}) while((s32[]{:T(128)}, f32[16,64,128]{2,1,0:T(8,128)S(1)}, f32[16,16,64,128]{3,2,1,0:T(8,128)}, ...), condition=%wide.region_4.5_spmd.clone, body=%wide.region_3.4_spmd.clone.sunk | while | flops 524291 | bytes 2622240 | solution.py:123
  191.5 3.7 all-to-all-start.1
  195.2 4.1 %multiply_convert_fusion.5 = (bf16[1,256,1024]{2,1,0:T(8,128)(2,1)}, bf16[1,256,1024]{2,1,0:T(8,128)(2,1)}, bf16[1,256,1024]{2,1,0:T(8,128)(2,1)}, bf16[1,256,1024]{2,1,0:T(8,128)(2,1)}) fusion(f32[1,256,1024]{2,1,0:T(8,128)S(1)} %copy.105, bf16[16,256,1024]{2,1,0:T(8,128)(2,1)} %bitcast.258, s32[]{:T(128)S(6)} %select_n.320, f32[1,256,1024]{2,1,0:T(8,128)} %copy.111, ...), kind=kLoop, calls=%fused_computation.73 | loop fusion | flops 3145728 | bytes 8388624 | tf_op jit(solution)/shard_map/convert_element_type | solution.py:184
  204.3 2.1 fusion.35
  206.4 4.1 %multiply_add_fusion = f32[16,16,64,128]{3,2,1,0:T(8,128)S(1)} fusion(f32[16,16,64,128]{3,2,1,0:T(8,128)} %get-tuple-element.88, f32[16,64,128]{2,1,0:T(8,128)S(1)} %fusion.35, f32[16,16]{1,0:T(8,128)S(1)} %concatenate.27), kind=kLoop, calls=%fused_computation.62 | loop fusion | flops 4194304 | bytes 17302528 | tf_op jit(solution)/shard_map/add | solution.py:138
  211.5 2.3 copy-done
  214.1 3.2 select_select_fusion
  217.3 4.9 %all-to-all-start = ((f32[4,2,16,64,128]{4,3,2,1,0:T(8,128)}), f32[4,2,16,64,128]{4,3,2,1,0:T(8,128)}, u32[]{:S(2)}, u32[]{:S(2)}) async-start(f32[4,2,16,64,128]{4,3,2,1,0:T(8,128)} %select_select_fusion), calls=%async_computation | async-start | bytes 8388608 | tf_op jit(solution)/shard_map/all_to_all | solution.py:200
  222.3 150.0 %while.23 = (s32[]{:T(128)}, bf16[16,256,1024]{1,2,0:T(8,128)(2,1)}, bf16[16,256,1024]{2,1,0:T(8,128)(2,1)}, s32[16,256]{1,0:T(8,128)S(1)}, f32[16,16,256]{2,1,0...) while((s32[]{:T(128)}, ...), condition=%wide.region_10.11_spmd, body=%wide.region_9.10_spmd.sunk | while | flops 294064384 | bytes 10755285 | solution.py:139
  238.7 1.4 fusion.109
  285.6 1.4 fusion.109
  372.2 12.2 %copy.100 = bf16[16,256,1024]{2,1,0:T(8,128)(2,1)} copy(bf16[16,256,1024]{1,2,0:T(8,128)(2,1)} %get-tuple-element.90) | data formatting | bytes 16777216 | tf_op jit(solution)/shard_map/convert_element_type | solution.py:141
  384.5 4.8 %copy.163 = f32[1,1,4,2,16,64,128]{6,5,4,3,2,1,0:T(8,128)} copy(f32[1,1,4,2,16,64,128]{6,5,4,3,2,1,0:T(8,128)} %bitcast.66) | data formatting | bytes 8388608
  (344 shorter events, 220.6 us)
Async XLA Ops:
  7.2 197.1 %all-gather.4.cloned.1.call-start = ((), (), s32[]{:S(2)}) async-start(), calls=%async_computation.2 | async-start | bytes 2359296 | tf_op jit(solution)/shard_map/all_gather | solution.py:65
  7.9 58.5 %collective-permute-start = (bf16[3,1280]{1,0:T(4,128)(2,1)S(1)}, bf16[3,1280]{1,0:T(4,128)(2,1)S(1)}, u32[]{:S(2)}, u32[]{:S(2)}) collective-permute-start(bf16[3,1280]{1,0:T(4,128)(2,1)S(1)} %slice_bitcast_fusion), channel_id=1, source_target_pairs={{0,1},{1,2},{2,3},{3,4},{4,5},{5,6},{6,7},{8,9},{9,10},{10,11},{11... | collective-permute-start | bytes 23048 | tf_op jit(solution)/shard_map/ppermute | solution.py:16
  32.6 15.2 %copy-start.4 = (u32[32]{0:T(128)S(1)}, u32[32]{0:T(128)}, u32[]{:S(2)}) copy-start(u32[32]{0:T(128)} %constant.317) | copy-start | bytes 388
  32.6 33.9 %copy-start.3 = (f32[1280]{0:T(1024)S(1)}, f32[1280]{0:T(1024)}, u32[]{:S(2)}) copy-start(f32[1280]{0:T(1024)} %param.14) | copy-start | bytes 15364
  175.8 19.4 %copy-start.1 = (f32[1,256,1024]{2,1,0:T(8,128)S(1)}, f32[1,256,1024]{2,1,0:T(8,128)}, u32[]{:S(2)}) copy-start(f32[1,256,1024]{2,1,0:T(8,128)} %copy.107) | copy-start | bytes 3145732
  191.5 12.8 %all-to-all-start.1 = ((bf16[4,2,3,1280]{3,1,2,0:T(2,128)(2,1)}), bf16[4,2,3,1280]{3,1,2,0:T(2,128)(2,1)S(1)}, u32[]{:S(2)}, u32[]{:S(2)}) async-start(bf16[4,2,3,1280]{3,1,2,0:T(2,128)(2,1)} %fusion.44), calls=%async_computation.1 | async-start | bytes 122880 | tf_op jit(solution)/shard_map/all_to_all | solution.py:201
  210.6 3.2 copy-start
  211.5 10.8 %copy-start.2 = (f32[16]{0:T(128)S(1)}, f32[16]{0:T(128)}, u32[]{:S(2)}) copy-start(f32[16]{0:T(128)} %param.17) | copy-start | bytes 196
  217.3 167.2 %all-to-all-start = ((f32[4,2,16,64,128]{4,3,2,1,0:T(8,128)}), f32[4,2,16,64,128]{4,3,2,1,0:T(8,128)}, u32[]{:S(2)}, u32[]{:S(2)}) async-start(f32[4,2,16,64,128]{4,3,2,1,0:T(8,128)} %select_select_fusion), calls=%async_computation | async-start | bytes 8388608 | tf_op jit(solution)/shard_map/all_to_all | solution.py:200
Sparse Core Ops, SparseCore 0:
  176.0 27.3 all-gather.3
where the time goes:
time: 402 us; the launch traced here: 397 us
  other arithmetic  132 us (33%)
  local copies, waits for them, and re-layouts  123 us (31%)
  matrix products  89.1 us (22%)
  between operations  23 us (6%)
  blocking collectives  17.2 us (4%)
  starting transfers between devices  11 us (3%)
    dynamic_slice x48, local copies, waits for them, and re-layouts, on_device(): lax.map(span_rows, (x_spans, b_spans, c_spans, dt_spans, cum_spans, doc_s...  29.9 us
    convert_element_type x1, other arithmetic, on_device(): activated = jax.nn.silu(mixed_sum).astype(jnp.bfloat16)  28.8 us
    dot_general x16, matrix products, span_output(): jnp.einsum('tn,hpn->thp', c_span, state_lo, preferred_element_type=jnp.fl...  23.1 us
    dot_general x16, matrix products, span_output(): jnp.einsum('tn,hpn->thp', c_span, state_hi, preferred_element_type=jnp.fl...  22 us
    unnamed x18, local copies, waits for them, and re-layouts  21.6 us
    dot_general x16, matrix products, span_output(): jnp.einsum('hts,shp->thp', weights, head_rows, preferred_element_type=jnp...  20.2 us
    add x16, other arithmetic, advance(): return (block_state + gate[:, None, None] * holding, holding)  18.5 us
    convert_element_type x1, local copies, waits for them, and re-layouts, on_device(): x_spans.reshape(count, SPAN, head_count, P_SIZE).astype(jnp.float32)  17.5 us
  transfers between devices with their start and end apart: 4, of which 0 were waited for; matrix products, arithmetic and copies ran while one was open for 55% of the time, Pallas kernels for 0%

commit v1 on v0

v1 whole, which is shorter than its diff:
```python
import functools

import jax
import jax.numpy as jnp
from jax import lax
from jax.experimental import pallas as pl
from jax.experimental.pallas import tpu as pltpu
from jax.sharding import PartitionSpec as P

P_SIZE = 64
N = 128
EMAX = 4
CAP = 2
CHUNK = 128
BLOCK = 256
FAR = 1 << 30
LOG2E = 1.4426950408889634
PAY = 144
TAIL = 32
VMEM = 56 * 1024 * 1024

F32 = jnp.float32
BF16 = jnp.bfloat16


def shifted(value, axis, steps):
    count = lax.axis_size(axis)
    leading, last = (max(0, -steps), min(count, count - steps))
    return lax.ppermute(value, axis, [(source, source + steps) for source in range(leading, last)])


def iota(shape, axis):
    return lax.broadcasted_iota(jnp.int32, shape, axis)


def outer_dot(left, right):
    return lax.dot_general(left, right, (((0,), (0,)), ((), ())), preferred_element_type=F32)


def halves(value):
    high = value.astype(BF16)
    low = (value - high.astype(F32)).astype(BF16)
    return jnp.concatenate([high, low], axis=0)


def thirds(value):
    high = value.astype(BF16)
    rest = value - high.astype(F32)
    mid = rest.astype(BF16)
    low = (rest - mid.astype(F32)).astype(BF16)
    return jnp.concatenate([high, mid, low], axis=0)


def spread_row(column, rep):
    return jnp.sum(rep * column, axis=0, keepdims=True)


def last_start(meta, place):
    start = meta[0]
    for slot in range(EMAX):
        end = meta[1 + slot]
        start = jnp.where(end <= place, end, start)
    return start


def next_end(meta, place):
    end = FAR
    for slot in reversed(range(EMAX)):
        end = jnp.where(meta[1 + slot] > place, meta[1 + slot], end)
    return end


def starts_of(meta, rows):
    start = jnp.full(rows.shape, meta[0], jnp.int32)
    for slot in range(EMAX):
        end = meta[1 + slot]
        start = jnp.where(rows >= end, end, start)
    return start


def read_docs(bounds, owners, meta, count, anchor, span):
    for slot in range(EMAX):
        meta[1 + slot] = FAR
        meta[5 + slot] = 0
    for owner in range(count.shape[0]):
        count[owner] = 0

    def one(index, carry):
        found, prior, start = carry
        end = bounds[0, index]
        owner = owners[0, index]
        mine = (end > prior) & (end > anchor) & (end <= anchor + span) & (found < EMAX)

        @pl.when(mine)
        def _():
            meta[1 + found] = end - anchor
            rank = count[owner]
            meta[5 + found] = jnp.where(rank < CAP, owner * CAP + rank, -1)
            count[owner] = rank + 1

        return found + mine.astype(jnp.int32), end, jnp.where(end <= anchor, end, start)

    zero = jnp.int32(0)
    _, _, start = lax.fori_loop(0, bounds.shape[1], one, (zero, zero, zero))
    meta[0] = start - anchor


def states_kernel(
    shard_ref, bounds, owners, x_ref, rim_ref, dt_ref, ld_ref, w_ref, bias_ref, rep_ref, rep16_ref, tri_ref,
    act_ref, cum_ref, carry_ref, sin_ref, pay_ref, fin_ref, first_ref, meta,
    state, edge, edge16, total, count,
):
    step = pl.program_id(0)
    heads = dt_ref.shape[0]
    width = rep_ref.shape[1]
    span = pl.num_programs(0) * BLOCK

    @pl.when(step == 0)
    def _():
        read_docs(bounds, owners, meta, count, shard_ref[0] * span, span)
        state[...] = jnp.zeros_like(state)
        total[...] = jnp.zeros_like(total)
        fin_ref[...] = jnp.zeros_like(fin_ref)
        first_ref[...] = jnp.zeros_like(first_ref)
        edge16[...] = rim_ref[...]
        edge[...] = rim_ref[...].astype(F32)[8:]

    for part in range(BLOCK // CHUNK):
        low = part * CHUNK
        rows = slice(low, low + CHUNK)
        begin = step * BLOCK + low
        place = iota((CHUNK, 128), 0) + begin
        back = place - starts_of(meta, place)
        keep = [(back >= lag).astype(F32) for lag in range(1, 4)]
        for tile in range(x_ref.shape[1] // 128):
            cols = slice(tile * 128, tile * 128 + 128)
            here = x_ref[rows, cols].astype(F32)
            wide = jnp.concatenate([edge[:, cols], here], axis=0)
            mixed = bias_ref[:, cols] + w_ref[0:1, cols] * here
            for lag in range(1, 4):
                moved = wide[8 - lag : 8 - lag + CHUNK]
                mixed = mixed + (w_ref[lag : lag + 1, cols] * keep[lag - 1]) * moved
            act_ref[rows, cols] = (mixed + mixed * jnp.tanh(mixed)).astype(BF16)
            edge[:, cols] = here[CHUNK - 8 :]

        summed = jnp.dot(
            thirds(ld_ref[:, rows] * LOG2E), tri_ref[...], preferred_element_type=F32
        )
        cum = summed[:heads] + summed[heads : 2 * heads] + summed[2 * heads :]
        cum_ref[:, rows] = cum
        dt = dt_ref[:, rows]
        lane = iota((heads, CHUNK), 1) + begin
        open_end = jnp.where(meta[0] < 0, meta[1], -1)
        carry_ref[:, rows] = jnp.where(lane < open_end, jnp.exp2(total[...] + cum), 0.0)
        x_act = act_ref[rows, :width]
        b_act = act_ref[rows, width : width + N]
        sin_ref[part] = state[...].astype(BF16)

        def finish(slot, _):
            end = meta[1 + slot]
            start = jnp.where(slot > 0, meta[jnp.maximum(slot, 1)], meta[0])
            at_end = jnp.sum(jnp.where(lane == end - 1, cum, 0.0), axis=1, keepdims=True)
            inside = (lane < end) & (lane >= start)
            weight = jnp.where(inside, jnp.exp2(jnp.minimum(at_end - cum, 0.0)) * dt, 0.0)
            load = (outer_dot(halves(weight), rep16_ref[...]) * x_act.astype(F32)).astype(BF16)
            local = outer_dot(b_act, load)
            through = jnp.where(start < begin, jnp.exp2(at_end), 0.0)
            final = local + spread_row(through, rep_ref[...]) * state[...]
            target = meta[5 + slot]

            @pl.when(target >= 0)
            def _():
                fin_ref[target, :width] = final.T.astype(BF16)

            opened = jnp.where(start < 0, jnp.exp2(total[:, :1] + at_end), 0.0)

            @pl.when(slot == 0)
            def _():
                first_ref[...] = jnp.broadcast_to(
                    spread_row(opened, rep_ref[...]), first_ref.shape
                )

            tail = jnp.zeros((TAIL, 128), F32)
            row = iota((TAIL, CHUNK), 0)
            col = iota((TAIL, CHUNK), 1) + begin
            row16 = iota((TAIL, 16), 0)
            col16 = iota((TAIL, 16), 1) + begin - 16
            for tile in range(x_ref.shape[1] // 128):
                cols = slice(tile * 128, tile * 128 + 128)
                want = end - 3 + row - 3 * tile
                pick = (col == want) & (col >= start) & (row >= 3 * tile) & (row < 3 * tile + 3)
                want16 = end - 3 + row16 - 3 * tile
                pick16 = (col16 == want16) & (col16 >= start) & (row16 >= 3 * tile) & (row16 < 3 * tile + 3)
                tail = tail + jnp.dot(
                    pick.astype(F32).astype(BF16), x_ref[rows, cols], preferred_element_type=F32
                ) + jnp.dot(
                    pick16.astype(F32).astype(BF16), edge16[:, cols], preferred_element_type=F32
                )

            @pl.when(target >= 0)
            def _():
                fin_ref[target, width : width + TAIL] = tail.astype(BF16)

            return 0

        done = jnp.int32(0)
        upto = jnp.int32(0)
        for slot in range(EMAX):
            done = done + (meta[1 + slot] <= begin).astype(jnp.int32)
            upto = upto + (meta[1 + slot] <= begin + CHUNK).astype(jnp.int32)
        lax.fori_loop(done, upto, finish, 0)
        edge16[...] = x_ref[low + CHUNK - 16 : low + CHUNK, :]

        start = last_start(meta, begin + CHUNK - 1)
        last = cum[:, CHUNK - 1 :]
        weight = jnp.where(lane >= start, jnp.exp2(last - cum) * dt, 0.0)
        load = (outer_dot(halves(weight), rep16_ref[...]) * x_act.astype(F32)).astype(BF16)
        through = spread_row(jnp.where(start < begin, jnp.exp2(last), 0.0), rep_ref[...])
        state[...] = through * state[...] + outer_dot(b_act, load)
        total[...] = total[...] + last

    @pl.when(step == pl.num_programs(0) - 1)
    def _():
        start = last_start(meta, span - 1)
        gate = spread_row(jnp.where(start < 0, jnp.exp2(total[:, :1]), 0.0), rep_ref[...])
        gate = jnp.broadcast_to(gate, (16, width))
        high = gate.astype(BF16).astype(F32)
        pay_ref[:N] = state[...].astype(BF16)
        pay_ref[N:] = jnp.where(iota((16, width), 0) == 0, high, gate - high).astype(BF16)


def output_kernel(meta, act_ref, dt_ref, cum_ref, sin_ref, gain_ref, rep16_ref, out_ref):
    step = pl.program_id(0)
    heads = dt_ref.shape[0]
    width = out_ref.shape[1]
    for part in range(BLOCK // CHUNK):
        low = part * CHUNK
        rows = slice(low, low + CHUNK)
        begin = step * BLOCK + low
        cum = cum_ref[:, rows]
        back = cum - jnp.log2(dt_ref[:, rows])
        ahead = cum.T
        b_act = act_ref[rows, width : width + N]
        c_act = act_ref[rows, width + N : width + 2 * N]
        place = iota((CHUNK, CHUNK), 0) + begin
        other = iota((CHUNK, CHUNK), 1) + begin
        scores = lax.dot_general(c_act, b_act, (((1,), (1,)), ((), ())), preferred_element_type=F32)
        scores = jnp.where((other <= place) & (other >= starts_of(meta, place)), scores, 0.0)
        lane = iota((heads, CHUNK), 1) + begin
        before = jnp.where(last_start(meta, begin) < begin, next_end(meta, begin), -1)
        entry = halves(jnp.where(lane < before, jnp.exp2(cum), 0.0))
        left_half = iota((CHUNK, 128), 1) < P_SIZE
        for pair in range(heads // 2):
            cols = slice(pair * 128, pair * 128 + 128)
            mixes = []
            for head in (2 * pair, 2 * pair + 1):
                spread = jnp.minimum(ahead[:, head : head + 1] - back[head : head + 1, :], 0.0)
                mixes.append((jnp.exp2(spread) * scores).astype(BF16))
            x_act = act_ref[rows, cols]
            zero = jnp.zeros_like(x_act)
            split = jnp.concatenate(
                [jnp.where(left_half, x_act, zero), jnp.where(left_half, zero, x_act)], axis=0
            )
            inner = jnp.dot(jnp.concatenate(mixes, axis=1), split, preferred_element_type=F32)
            outer = jnp.dot(c_act, sin_ref[part, :, cols], preferred_element_type=F32)
            scale = outer_dot(entry, rep16_ref[:, cols])
            value = inner + scale * outer + gain_ref[:, cols] * x_act.astype(F32)
            out_ref[rows, cols] = value.astype(BF16)


def carry_kernel(shard_ref, meta, gathered, first_ref, fin_in, carried_ref, fin_ref, held):
    del meta
    width = first_ref.shape[1]
    held[...] = jnp.zeros_like(held)

    def one(index, _):
        gates = gathered[index, N:].astype(F32)
        held[...] = (gates[0:1] + gates[1:2]) * held[...] + gathered[index, :N].astype(F32)
        return 0

    lax.fori_loop(0, shard_ref[0], one, 0)
    carried_ref[...] = held[...].astype(BF16)
    fin_ref[0, :width] = (
        fin_in[0, :width].astype(F32) + (first_ref[0:1] * held[...]).T
    ).astype(BF16)
    fin_ref[0, width:] = fin_in[0, width:]


def correct_kernel(meta, base_ref, c_ref, carry_ref, carried_ref, rep16_ref, out_ref):
    step = pl.program_id(0)
    touched = (meta[0] < 0) & (meta[1] > step * BLOCK)

    @pl.when(touched)
    def _():
        entry = halves(carry_ref[...])
        width = out_ref.shape[1]
        for tile in range(width // 256):
            cols = slice(tile * 256, tile * 256 + 256)
            outer = jnp.dot(c_ref[...], carried_ref[:, cols], preferred_element_type=F32)
            scale = outer_dot(entry, rep16_ref[:, cols])
            out_ref[:, cols] = (base_ref[:, cols].astype(F32) + scale * outer).astype(BF16)

    @pl.when(jnp.logical_not(touched))
    def _():
        out_ref[...] = base_ref[...]


def params():
    return pltpu.CompilerParams(vmem_limit_bytes=VMEM, dimension_semantics=("arbitrary",))


def whole(shape):
    return pl.BlockSpec(shape, lambda *_: (0,) * len(shape))


def on_device(
    conv_input, conv_weight, conv_bias, step_size, log_decay, skip_gain, doc_bounds, doc_owner
):
    span, channels = conv_input.shape[1:]
    heads = step_size.shape[1]
    width = heads * P_SIZE
    steps = span // BLOCK
    chunks = span // CHUNK
    owners = lax.axis_size("stream")
    slots = owners * CAP
    rows = width + TAIL
    shard = lax.axis_index("seq").astype(jnp.int32).reshape(1)
    rows_in = conv_input[0]
    rim = shifted(rows_in[span - 16 :], "seq", 1)
    rep = (jnp.arange(width)[None, :] // P_SIZE == jnp.arange(heads)[:, None]).astype(F32)
    rep16 = jnp.concatenate([rep, rep], 0).astype(BF16)
    ticks = jnp.arange(CHUNK)
    tri = (ticks[:, None] <= ticks[None, :]).astype(BF16)
    smem = pl.BlockSpec(memory_space=pltpu.SMEM)
    per_head = pl.BlockSpec((heads, BLOCK), lambda i, *_: (0, i))
    act, cum, carry, sin, pay, fin, first, meta = pl.pallas_call(
        states_kernel,
        grid=(steps,),
        in_specs=[
            smem, smem, smem,
            pl.BlockSpec((BLOCK, channels), lambda i: (i, 0)),
            whole((16, channels)),
            per_head, per_head,
            whole((4, channels)), whole((1, channels)),
            whole((heads, width)), whole((2 * heads, width)), whole((CHUNK, CHUNK)),
        ],
        out_specs=[
            pl.BlockSpec((BLOCK, channels), lambda i: (i, 0)),
            per_head, per_head,
            pl.BlockSpec((BLOCK // CHUNK, N, width), lambda i: (i, 0, 0)),
            whole((PAY, width)), whole((slots, rows, N)), whole((8, width)),
            smem,
        ],
        out_shape=[
            jax.ShapeDtypeStruct((span, channels), BF16),
            jax.ShapeDtypeStruct((heads, span), F32),
            jax.ShapeDtypeStruct((heads, span), F32),
            jax.ShapeDtypeStruct((chunks, N, width), BF16),
            jax.ShapeDtypeStruct((PAY, width), BF16),
            jax.ShapeDtypeStruct((slots, rows, N), BF16),
            jax.ShapeDtypeStruct((8, width), F32),
            jax.ShapeDtypeStruct((16,), jnp.int32),
        ],
        scratch_shapes=[
            pltpu.VMEM((N, width), F32),
            pltpu.VMEM((8, channels), F32),
            pltpu.VMEM((16, channels), BF16),
            pltpu.VMEM((heads, CHUNK), F32),
            pltpu.SMEM((owners,), jnp.int32),
        ],
        compiler_params=params(),
        cost_estimate=pl.CostEstimate(
            flops=2 * span * width * N * 2, bytes_accessed=40 << 20, transcendentals=span * channels
        ),
        name="states",
    )(
        shard, doc_bounds, doc_owner, rows_in, rim, step_size[0], log_decay[0],
        conv_weight * 0.5, conv_bias[None] * 0.5, rep, rep16, tri,
    )

    gathered = lax.all_gather(pay[None], "seq", axis=0, tiled=True)

    gain = jnp.repeat(skip_gain, P_SIZE)[None]
    prefetch = functools.partial(pltpu.PrefetchScalarGridSpec, num_scalar_prefetch=1)
    base = pl.pallas_call(
        output_kernel,
        grid_spec=prefetch(
            grid=(steps,),
            in_specs=[
                pl.BlockSpec((BLOCK, channels), lambda i, *_: (i, 0)),
                per_head, per_head,
                pl.BlockSpec((BLOCK // CHUNK, N, width), lambda i, *_: (i, 0, 0)),
                whole((1, width)), whole((2 * heads, width)),
            ],
            out_specs=pl.BlockSpec((BLOCK, width), lambda i, *_: (i, 0)),
        ),
        out_shape=jax.ShapeDtypeStruct((span, width), BF16),
        compiler_params=params(),
        cost_estimate=pl.CostEstimate(
            flops=2 * span * width * N * 4, bytes_accessed=30 << 20, transcendentals=span * CHUNK * heads
        ),
        name="outputs",
    )(meta, act, step_size[0], cum, sin, gain, rep16)

    carried, fin = pl.pallas_call(
        carry_kernel,
        grid_spec=pltpu.PrefetchScalarGridSpec(
            num_scalar_prefetch=2,
            grid=(1,),
            in_specs=[
                whole(gathered.shape), whole((8, width)),
                pl.BlockSpec((1, rows, N), lambda i, shard_ref, meta: (meta[5], 0, 0)),
            ],
            out_specs=[
                whole((N, width)),
                pl.BlockSpec((1, rows, N), lambda i, shard_ref, meta: (meta[5], 0, 0)),
            ],
            scratch_shapes=[pltpu.VMEM((N, width), F32)],
        ),
        out_shape=[
            jax.ShapeDtypeStruct((N, width), BF16),
            jax.ShapeDtypeStruct((slots, rows, N), BF16),
        ],
        input_output_aliases={4: 1},
        compiler_params=params(),
        name="carry",
    )(shard, meta, gathered, first, fin)

    got = lax.all_to_all(
        fin.reshape(owners, CAP, rows, N), "stream", split_axis=0, concat_axis=0, tiled=True
    )

    out = pl.pallas_call(
        correct_kernel,
        grid_spec=prefetch(
            grid=(steps,),
            in_specs=[
                pl.BlockSpec((BLOCK, width), lambda i, *_: (i, 0)),
                pl.BlockSpec((BLOCK, N), lambda i, *_: (i, width // N + 1)),
                per_head,
                whole((N, width)), whole((2 * heads, width)),
            ],
            out_specs=pl.BlockSpec((BLOCK, width), lambda i, *_: (i, 0)),
        ),
        out_shape=jax.ShapeDtypeStruct((span, width), BF16),
        input_output_aliases={1: 0},
        compiler_params=params(),
        cost_estimate=pl.CostEstimate(
            flops=2 * span * width * N, bytes_accessed=18 << 20, transcendentals=0
        ),
        name="correct",
    )(meta, base, act, carry, carried, rep16)

    ssm = got[:, :, :width].astype(F32).reshape(1, 1, owners, CAP, heads, P_SIZE, N)
    tiles = channels // N
    conv = got[:, :, width : width + 3 * tiles].reshape(owners, CAP, tiles, 3, N)
    conv = conv.transpose(0, 1, 3, 2, 4).reshape(1, 1, owners, CAP, 3, channels)
    return out[None], ssm, conv


def solution(mesh):
    in_specs = (
        P("stream", "seq", None),
        P(),
        P(),
        P("stream", None, "seq"),
        P("stream", None, "seq"),
        P(),
        P("stream", None),
        P("stream", None),
    )
    out_specs = (
        P("stream", "seq", None),
        P("stream", "seq", None, None, None, None, None),
        P("stream", "seq", None, None, None, None),
    )
    return jax.shard_map(
        on_device, mesh=mesh, in_specs=in_specs, out_specs=out_specs, check_vma=False
    )
```

time: 402 us -> 151 us (0.38)
  the two profiles are of different devices: /device:TPU:0 before, /device:TPU:11 now
where the time goes in v1:
time: 151 us; the launch traced here: 149 us
  Pallas kernels  83.1 us (55%)
  waiting for transfers between devices  34.4 us (23%)
  between operations  14.1 us (9%)
  starting transfers between devices  7.65 us (5%)
  other arithmetic  6.42 us (4%)
  local copies, waits for them, and re-layouts  3.61 us (2%)
    pallas_call x1, Pallas kernels, on_device(): pl.pallas_call(states_kernel, grid=(steps,), in_specs=[smem, smem, smem,...  39.8 us
    all_gather x1, waiting for transfers between devices, on_device(): gathered = lax.all_gather(pay[None], 'seq', axis=0, tiled=True)  34.4 us
    pallas_call x1, Pallas kernels, on_device(): pl.pallas_call(output_kernel, grid_spec=prefetch(grid=(steps,), in_specs=...  23.8 us
    pallas_call x1, Pallas kernels, on_device(): pl.pallas_call(correct_kernel, grid_spec=prefetch(grid=(steps,), in_specs...  16 us
    all_to_all x1, starting transfers between devices, on_device(): lax.all_to_all(fin.reshape(owners, CAP, rows, N), 'stream', split_axis=0,...  3.86 us
    ppermute x1, starting transfers between devices, shifted(): lax.ppermute(value, axis, [(source, source + steps) for source in range(l...  3.75 us
    pallas_call x1, Pallas kernels, on_device(): pl.pallas_call(carry_kernel, grid_spec=pltpu.PrefetchScalarGridSpec(num_s...  3.51 us
  transfers between devices with their start and end apart: 3, of which 1 were waited for; matrix products, arithmetic and copies ran while one was open for 4% of the time, Pallas kernels for 27%

profile of v1, /device:TPU:11, one launch (start us, length us, event | category | flops | bytes accessed | tf_op | source)
XLA Modules:
  0.0 149.3 jit_solution(10353157448172217536)
XLA Ops:
  7.2 0.0 all-gather.3.cloned.1.call-start
  7.2 0.8 slice_bitcast_fusion
  8.0 3.8 %collective-permute-start = (bf16[16,1280]{1,0:T(8,128)(2,1)S(1)}, bf16[16,1280]{1,0:T(8,128)(2,1)S(1)}, u32[]{:S(2)}, u32[]{:S(2)}) collective-permute-start(bf16[16,1280]{1,0:T(8,128)(2,1)S(1)} %slice_bitcast_fusion), channel_id=1, source_target_pairs={{0,1},{1,2},{2,3},{3,4},{4,5},{5,6},{6,7},{8,9},{9,10},{10,11},{11... | collective-permute-start | bytes 122888 | tf_op jit(solution)/shard_map/ppermute | solution.py:29
  11.8 0.7 broadcast_multiply_fusion.1
  12.5 1.3 broadcast_multiply_fusion.w_ref
  13.8 0.6 fusion.2
  14.4 0.6 pad_maximum_fusion.rep16_ref
  15.1 0.6 fusion.1.tri_ref
  15.7 0.6 mul.18.bias_ref
  16.3 0.0 collective-permute-done.rim_ref
  16.3 0.6 copy-done
  16.9 39.8 %states.1 = (bf16[4096,1280]{1,0:T(8,128)(2,1)}, f32[16,4096]{1,0:T(8,128)}, f32[16,4096]{1,0:T(8,128)}, bf16[32,128,1024]{2,1,0:T(8,128)(2,1)}, bf16[144,1024]{...) custom-call(s32[1]{0:T(128)} %bitcast.shard_ref, s32[1,32]{1,0:T(1,128)} %bounds.1, ...), custom_call_target="tpu_custom_call" | custom-call | flops 2147483648 | bytes 41943040 | tf_op jit(solution)/shard_map/states/pallas_call | solution.py:336
  56.7 0.0 all-gather.3.cloned.1.call-update
  56.7 34.4 %all-gather.3.cloned.1.call-done = bf16[1152,1024]{1,0:T(8,128)(2,1)} async-done(((bf16[144,1024]{1,0:T(8,128)(2,1)}), bf16[1152,1024]{1,0:T(8,128)(2,1)}) %all-gather.3.cloned.1.call-update) | async-done | bytes 2359312 | tf_op jit(solution)/shard_map/all_gather | solution.py:381
  91.1 3.5 %carry.1 = (bf16[128,1024]{1,0:T(8,128)(2,1)}, bf16[8,1056,128]{2,1,0:T(8,128)(2,1)}) custom-call(s32[1]{0:T(128)} %bitcast.shard_ref, s32[16]{0:T(128)} %get-tuple-element.13.meta, bf16[8,144,1024]{2,1,0:T(8,128)(2,1)} %bitcast.20, f32[8,1024]{1,0:T(8,128)} %get-tuple-element.19.first_ref, ...), custom_call_target="tpu_custom_call", output_to_operand_aliasing={{1}: (4, {})} | custom-call | tf_op jit(solution)/shard_map/carry/pallas_call | solution.py:405
  94.6 3.9 %all-to-all-start = ((bf16[4,2,1056,128]{3,2,1,0:T(8,128)(2,1)}), bf16[4,2,1056,128]{3,2,1,0:T(8,128)(2,1)S(1)}, u32[]{:S(2)}, u32[]{:S(2)}) async-start(bf16[4,2,1056,128]{3,2,1,0:T(8,128)(2,1)} %bitcast.18), calls=%async_computation | async-start | bytes 4325376 | tf_op jit(solution)/shard_map/all_to_all | solution.py:429
  98.5 0.1 broadcast_in_dim.6
  98.5 0.7 broadcast_in_dim_reshape.3.gain_ref
  99.2 23.8 %outputs.1.base_ref = bf16[4096,1024]{1,0:T(8,128)(2,1)} custom-call(s32[16]{0:T(128)} %get-tuple-element.13.meta, bf16[4096,1280]{1,0:T(8,128)(2,1)} %get-tuple-element.14.act_ref.c_ref, f32[16,4096]{1,0:T(8,128)} %bitcast.22, f32[16,4096]{1,0:T(8,128)} %get-tuple-element.15.cum_ref, bf16[32,128,1024]{2,1,0:T(8,128)(2,1)} %get-tuple-element.16.sin_ref, ...), custom_call_target="tpu_custom_call" | custom-call | flops 4294967296 | bytes 31457280 | tf_op jit(solution)/shard_map/outputs/pallas_call | solution.py:385
  123.0 16.0 %correct.1 = bf16[4096,1024]{1,0:T(8,128)(2,1)} custom-call(s32[16]{0:T(128)} %get-tuple-element.13.meta, bf16[4096,1024]{1,0:T(8,128)(2,1)} %outputs.1.base_ref, bf16[4096,1280]{1,0:T(8,128)(2,1)} %get-tuple-element.14.act_ref.c_ref, f32[16,4096]{1,0:T(8,128)} %get-tuple-element.17.carry_ref, ...), custom_call_target="tpu_custom_call", output_to_operand_aliasing={{}: (1, {})} | custom-call | flops 1073741824 | bytes 18874368 | tf_op jit(solution)/shard_map/correct/pallas_call | solution.py:433
  139.0 0.0 all-to-all-done
  139.1 0.7 reshape.68
  139.8 0.1 slice.16
  139.9 2.5 %convert.8 = f32[1,1,4,2,16,64,128]{6,5,4,3,2,1,0:T(8,128)} convert(bf16[1,1,4,2,16,64,128]{6,5,4,3,2,1,0:T(8,128)(2,1)S(1)} %bitcast.19) | non-fusion elementwise | flops 1048576 | bytes 6291456 | tf_op jit(solution)/shard_map/reshape | solution.py:454
  (7 shorter events, 0.1 us)
Async XLA Ops:
  7.2 83.9 %all-gather.3.cloned.1.call-start = ((), (), s32[]{:S(2)}) async-start(), calls=%async_computation.1 | async-start | bytes 2654208 | tf_op jit(solution)/shard_map/all_gather | solution.py:381
  8.0 8.3 %collective-permute-start = (bf16[16,1280]{1,0:T(8,128)(2,1)S(1)}, bf16[16,1280]{1,0:T(8,128)(2,1)S(1)}, u32[]{:S(2)}, u32[]{:S(2)}) collective-permute-start(bf16[16,1280]{1,0:T(8,128)(2,1)S(1)} %slice_bitcast_fusion), channel_id=1, source_target_pairs={{0,1},{1,2},{2,3},{3,4},{4,5},{5,6},{6,7},{8,9},{9,10},{10,11},{11... | collective-permute-start | bytes 122888 | tf_op jit(solution)/shard_map/ppermute | solution.py:29
  16.3 0.6 copy-start
  16.9 81.6 %copy-start.1 = (f32[16]{0:T(128)S(1)}, f32[16]{0:T(128)}, u32[]{:S(2)}) copy-start(f32[16]{0:T(128)} %param.13) | copy-start | bytes 196
  94.6 44.4 %all-to-all-start = ((bf16[4,2,1056,128]{3,2,1,0:T(8,128)(2,1)}), bf16[4,2,1056,128]{3,2,1,0:T(8,128)(2,1)S(1)}, u32[]{:S(2)}, u32[]{:S(2)}) async-start(bf16[4,2,1056,128]{3,2,1,0:T(8,128)(2,1)} %bitcast.18), calls=%async_computation | async-start | bytes 4325376 | tf_op jit(solution)/shard_map/all_to_all | solution.py:429
Sparse Core Ops, SparseCore 0:
  56.8 34.1 all-gather.2

commit v2 on v1

--- a/solution.py
+++ b/solution.py
@@ -2,6 +2,7 @@
 
 import jax
 import jax.numpy as jnp
+import numpy as np
 from jax import lax
 from jax.experimental import pallas as pl
 from jax.experimental.pallas import tpu as pltpu
@@ -12,7 +13,7 @@
 EMAX = 4
 CAP = 2
 CHUNK = 128
-BLOCK = 256
+BLOCK = 512
 FAR = 1 << 30
 LOG2E = 1.4426950408889634
 PAY = 144
@@ -105,15 +106,36 @@
     meta[0] = start - anchor
 
 
+def conv_rows(x_ref, edge16, moves, weights, act_ref, part, choice):
+    low = part * CHUNK
+    rows = slice(low, low + CHUNK)
+    pick = moves[choice]
+    for tile in range(x_ref.shape[1] // 256):
+        cols = slice(tile * 256, tile * 256 + 256)
+        if part:
+            wide = x_ref[low - 16 : low + CHUNK, cols]
+        else:
+            wide = jnp.concatenate([edge16[:, cols], x_ref[rows, cols]], axis=0)
+        moved = jnp.dot(pick, wide, preferred_element_type=F32)
+        moved = moved.reshape(CHUNK // 8, 3, 8, 256)
+        mixed = weights[4:5, cols] + weights[0:1, cols] * x_ref[rows, cols].astype(F32)
+        for lag in range(1, 4):
+            mixed = mixed + weights[lag : lag + 1, cols] * moved[:, lag - 1].reshape(CHUNK, 256)
+        act_ref[rows, cols] = (mixed + mixed * jnp.tanh(mixed)).astype(BF16)
+
+
 def states_kernel(
-    shard_ref, bounds, owners, x_ref, rim_ref, dt_ref, ld_ref, w_ref, bias_ref, rep_ref, rep16_ref, tri_ref,
+    shard_ref, bounds, owners, x_ref, rim_ref, dt_ref, ld_ref, w_ref, bias_ref,
+    rep_ref, rep16_ref, tri_ref, move_ref, slot_ref,
     act_ref, cum_ref, carry_ref, sin_ref, pay_ref, fin_ref, first_ref, meta,
-    state, edge, edge16, total, count,
+    state, edge16, total, totals, weights, moves, count,
 ):
     step = pl.program_id(0)
     heads = dt_ref.shape[0]
     width = rep_ref.shape[1]
     span = pl.num_programs(0) * BLOCK
+    parts = BLOCK // CHUNK
+    first = step * BLOCK
 
     @pl.when(step == 0)
     def _():
@@ -123,101 +145,117 @@
         fin_ref[...] = jnp.zeros_like(fin_ref)
         first_ref[...] = jnp.zeros_like(first_ref)
         edge16[...] = rim_ref[...]
-        edge[...] = rim_ref[...].astype(F32)[8:]
-
-    for part in range(BLOCK // CHUNK):
+        weights[0:4] = 0.5 * w_ref[...]
+        weights[4:5] = 0.5 * bias_ref[...]
+        moves[0] = move_ref[...]
+
+    choices = []
+    for part in range(parts):
+        begin = first + part * CHUNK
+        near = (meta[0] > begin - 3) & (meta[0] < begin + CHUNK)
+        for slot in range(EMAX):
+            near = near | ((meta[1 + slot] > begin - 3) & (meta[1 + slot] < begin + CHUNK))
+
+        @pl.when(near)
+        def _():
+            tick = slot_ref[...] // 4 + begin
+            kept = (tick - starts_of(meta, tick) >= slot_ref[...] % 4).astype(F32)
+            moves[1 + part, :, :128] = (kept * move_ref[:, :128].astype(F32)).astype(BF16)
+            moves[1 + part, :, 128:] = (kept[:, :16] * move_ref[:, 128:].astype(F32)).astype(BF16)
+
+        choices.append(jnp.where(near, 1 + part, 0))
+
+    conv_rows(x_ref, edge16, moves, weights, act_ref, 0, choices[0])
+    running = total[...]
+    for part in range(parts):
         low = part * CHUNK
         rows = slice(low, low + CHUNK)
-        begin = step * BLOCK + low
-        place = iota((CHUNK, 128), 0) + begin
-        back = place - starts_of(meta, place)
-        keep = [(back >= lag).astype(F32) for lag in range(1, 4)]
-        for tile in range(x_ref.shape[1] // 128):
-            cols = slice(tile * 128, tile * 128 + 128)
-            here = x_ref[rows, cols].astype(F32)
-            wide = jnp.concatenate([edge[:, cols], here], axis=0)
-            mixed = bias_ref[:, cols] + w_ref[0:1, cols] * here
-            for lag in range(1, 4):
-                moved = wide[8 - lag : 8 - lag + CHUNK]
-                mixed = mixed + (w_ref[lag : lag + 1, cols] * keep[lag - 1]) * moved
-            act_ref[rows, cols] = (mixed + mixed * jnp.tanh(mixed)).astype(BF16)
-            edge[:, cols] = here[CHUNK - 8 :]
-
+        begin = first + low
+        if part + 1 < parts:
+            conv_rows(x_ref, edge16, moves, weights, act_ref, part + 1, choices[part + 1])
         summed = jnp.dot(
             thirds(ld_ref[:, rows] * LOG2E), tri_ref[...], preferred_element_type=F32
         )
         cum = summed[:heads] + summed[heads : 2 * heads] + summed[2 * heads :]
         cum_ref[:, rows] = cum
-        dt = dt_ref[:, rows]
         lane = iota((heads, CHUNK), 1) + begin
         open_end = jnp.where(meta[0] < 0, meta[1], -1)
-        carry_ref[:, rows] = jnp.where(lane < open_end, jnp.exp2(total[...] + cum), 0.0)
-        x_act = act_ref[rows, :width]
-        b_act = act_ref[rows, width : width + N]
-        sin_ref[part] = state[...].astype(BF16)
-
-        def finish(slot, _):
-            end = meta[1 + slot]
-            start = jnp.where(slot > 0, meta[jnp.maximum(slot, 1)], meta[0])
-            at_end = jnp.sum(jnp.where(lane == end - 1, cum, 0.0), axis=1, keepdims=True)
-            inside = (lane < end) & (lane >= start)
-            weight = jnp.where(inside, jnp.exp2(jnp.minimum(at_end - cum, 0.0)) * dt, 0.0)
-            load = (outer_dot(halves(weight), rep16_ref[...]) * x_act.astype(F32)).astype(BF16)
-            local = outer_dot(b_act, load)
-            through = jnp.where(start < begin, jnp.exp2(at_end), 0.0)
-            final = local + spread_row(through, rep_ref[...]) * state[...]
-            target = meta[5 + slot]
-
-            @pl.when(target >= 0)
-            def _():
-                fin_ref[target, :width] = final.T.astype(BF16)
-
-            opened = jnp.where(start < 0, jnp.exp2(total[:, :1] + at_end), 0.0)
-
-            @pl.when(slot == 0)
-            def _():
-                first_ref[...] = jnp.broadcast_to(
-                    spread_row(opened, rep_ref[...]), first_ref.shape
-                )
-
-            tail = jnp.zeros((TAIL, 128), F32)
-            row = iota((TAIL, CHUNK), 0)
-            col = iota((TAIL, CHUNK), 1) + begin
-            row16 = iota((TAIL, 16), 0)
-            col16 = iota((TAIL, 16), 1) + begin - 16
-            for tile in range(x_ref.shape[1] // 128):
-                cols = slice(tile * 128, tile * 128 + 128)
-                want = end - 3 + row - 3 * tile
-                pick = (col == want) & (col >= start) & (row >= 3 * tile) & (row < 3 * tile + 3)
-                want16 = end - 3 + row16 - 3 * tile
-                pick16 = (col16 == want16) & (col16 >= start) & (row16 >= 3 * tile) & (row16 < 3 * tile + 3)
-                tail = tail + jnp.dot(
-                    pick.astype(F32).astype(BF16), x_ref[rows, cols], preferred_element_type=F32
-                ) + jnp.dot(
-                    pick16.astype(F32).astype(BF16), edge16[:, cols], preferred_element_type=F32
-                )
-
-            @pl.when(target >= 0)
-            def _():
-                fin_ref[target, width : width + TAIL] = tail.astype(BF16)
-
-            return 0
-
-        done = jnp.int32(0)
-        upto = jnp.int32(0)
-        for slot in range(EMAX):
-            done = done + (meta[1 + slot] <= begin).astype(jnp.int32)
-            upto = upto + (meta[1 + slot] <= begin + CHUNK).astype(jnp.int32)
-        lax.fori_loop(done, upto, finish, 0)
-        edge16[...] = x_ref[low + CHUNK - 16 : low + CHUNK, :]
-
+        carry_ref[:, rows] = jnp.where(lane < open_end, jnp.exp2(running + cum), 0.0)
+        totals[part] = running
         start = last_start(meta, begin + CHUNK - 1)
         last = cum[:, CHUNK - 1 :]
-        weight = jnp.where(lane >= start, jnp.exp2(last - cum) * dt, 0.0)
-        load = (outer_dot(halves(weight), rep16_ref[...]) * x_act.astype(F32)).astype(BF16)
+        weight = jnp.where(lane >= start, jnp.exp2(last - cum) * dt_ref[:, rows], 0.0)
+        weight = weight.T.astype(BF16)
         through = spread_row(jnp.where(start < begin, jnp.exp2(last), 0.0), rep_ref[...])
-        state[...] = through * state[...] + outer_dot(b_act, load)
-        total[...] = total[...] + last
+        b_turned = act_ref[rows, width : width + N].T
+        for tile in range(width // 256):
+            cols = slice(tile * 256, tile * 256 + 256)
+            held = state[:, cols]
+            sin_ref[part, :, cols] = held.astype(BF16)
+            scale = jnp.dot(weight, rep16_ref[:heads, cols], preferred_element_type=F32)
+            load = scale.astype(BF16) * act_ref[rows, cols]
+            grown = jnp.dot(b_turned, load, preferred_element_type=F32)
+            state[:, cols] = through[:, cols] * held + grown
+        running = running + last
+    total[...] = running
+
+    def finish(slot, _):
+        end = meta[1 + slot]
+        start = jnp.where(slot > 0, meta[jnp.maximum(slot, 1)], meta[0])
+        part = (end - 1 - first) // CHUNK
+        low = pl.multiple_of(part * CHUNK, CHUNK)
+        begin = first + low
+        lane = iota((heads, CHUNK), 1) + begin
+        cum = cum_ref[:, pl.ds(low, CHUNK)]
+        at_end = jnp.sum(jnp.where(lane == end - 1, cum, 0.0), axis=1, keepdims=True)
+        inside = (lane < end) & (lane >= start)
+        weight = jnp.exp2(jnp.minimum(at_end - cum, 0.0)) * dt_ref[:, pl.ds(low, CHUNK)]
+        weight = jnp.where(inside, weight, 0.0).T.astype(BF16)
+        scale = jnp.dot(weight, rep16_ref[:heads], preferred_element_type=F32)
+        load = scale.astype(BF16) * act_ref[pl.ds(low, CHUNK), :width]
+        local = outer_dot(act_ref[pl.ds(low, CHUNK), width : width + N], load)
+        through = spread_row(jnp.where(start < begin, jnp.exp2(at_end), 0.0), rep_ref[...])
+        final = local + through * sin_ref[part].astype(F32)
+        target = meta[5 + slot]
+        opened = jnp.where(start < 0, jnp.exp2(totals[part][:, :1] + at_end), 0.0)
+
+        @pl.when(slot == 0)
+        def _():
+            first_ref[...] = jnp.broadcast_to(spread_row(opened, rep_ref[...]), first_ref.shape)
+
+        tail = jnp.zeros((TAIL, 128), F32)
+        row = iota((TAIL, CHUNK), 0)
+        col = iota((TAIL, CHUNK), 1) + begin
+        row16 = iota((TAIL, 16), 0)
+        col16 = iota((TAIL, 16), 1) + begin - 16
+        before = pl.multiple_of(jnp.maximum(low - 16, 0), 16)
+        for tile in range(x_ref.shape[1] // 128):
+            cols = slice(tile * 128, tile * 128 + 128)
+            mine = (row >= 3 * tile) & (row < 3 * tile + 3)
+            pick = (col == end - 3 + row - 3 * tile) & (col >= start) & mine
+            mine16 = (row16 >= 3 * tile) & (row16 < 3 * tile + 3)
+            pick16 = (col16 == end - 3 + row16 - 3 * tile) & (col16 >= start) & mine16
+            rim = jnp.where(low > 0, x_ref[pl.ds(before, 16), cols].astype(F32), edge16[:, cols].astype(F32))
+            tail = tail + jnp.dot(
+                pick.astype(F32).astype(BF16), x_ref[pl.ds(low, CHUNK), cols], preferred_element_type=F32
+            ) + jnp.dot(
+                pick16.astype(F32).astype(BF16), rim.astype(BF16), preferred_element_type=F32
+            )
+
+        @pl.when(target >= 0)
+        def _():
+            fin_ref[target, :width] = final.T.astype(BF16)
+            fin_ref[target, width : width + TAIL] = tail.astype(BF16)
+
+        return 0
+
+    done = jnp.int32(0)
+    upto = jnp.int32(0)
+    for slot in range(EMAX):
+        done = done + (meta[1 + slot] <= first).astype(jnp.int32)
+        upto = upto + (meta[1 + slot] <= first + BLOCK).astype(jnp.int32)
+    lax.fori_loop(done, upto, finish, 0)
+    edge16[...] = x_ref[BLOCK - 16 :, :]
 
     @pl.when(step == pl.num_programs(0) - 1)
     def _():
@@ -248,23 +286,29 @@
         scores = jnp.where((other <= place) & (other >= starts_of(meta, place)), scores, 0.0)
         lane = iota((heads, CHUNK), 1) + begin
         before = jnp.where(last_start(meta, begin) < begin, next_end(meta, begin), -1)
-        entry = halves(jnp.where(lane < before, jnp.exp2(cum), 0.0))
+        entry = jnp.where(lane < before, jnp.exp2(cum), 0.0)
+        entry = jnp.concatenate([entry, entry - entry.astype(BF16).astype(F32)], axis=0).T.astype(BF16)
         left_half = iota((CHUNK, 128), 1) < P_SIZE
-        for pair in range(heads // 2):
-            cols = slice(pair * 128, pair * 128 + 128)
-            mixes = []
-            for head in (2 * pair, 2 * pair + 1):
-                spread = jnp.minimum(ahead[:, head : head + 1] - back[head : head + 1, :], 0.0)
-                mixes.append((jnp.exp2(spread) * scores).astype(BF16))
-            x_act = act_ref[rows, cols]
-            zero = jnp.zeros_like(x_act)
-            split = jnp.concatenate(
-                [jnp.where(left_half, x_act, zero), jnp.where(left_half, zero, x_act)], axis=0
-            )
-            inner = jnp.dot(jnp.concatenate(mixes, axis=1), split, preferred_element_type=F32)
+        for quad in range(heads // 4):
+            cols = slice(quad * 256, quad * 256 + 256)
             outer = jnp.dot(c_act, sin_ref[part, :, cols], preferred_element_type=F32)
-            scale = outer_dot(entry, rep16_ref[:, cols])
-            value = inner + scale * outer + gain_ref[:, cols] * x_act.astype(F32)
+            scale = jnp.dot(entry, rep16_ref[:, cols], preferred_element_type=F32)
+            sums = []
+            for pair in (2 * quad, 2 * quad + 1):
+                mixes = []
+                for head in (2 * pair, 2 * pair + 1):
+                    spread = jnp.minimum(ahead[:, head : head + 1] - back[head : head + 1, :], 0.0)
+                    mixes.append((jnp.exp2(spread) * scores).astype(BF16))
+                x_pair = act_ref[rows, pair * 128 : pair * 128 + 128]
+                zero = jnp.zeros_like(x_pair)
+                split = jnp.concatenate(
+                    [jnp.where(left_half, x_pair, zero), jnp.where(left_half, zero, x_pair)], axis=0
+                )
+                sums.append(
+                    jnp.dot(jnp.concatenate(mixes, axis=1), split, preferred_element_type=F32)
+                )
+            inner = jnp.concatenate(sums, axis=1)
+            value = inner + scale * outer + gain_ref[:, cols] * act_ref[rows, cols].astype(F32)
             out_ref[rows, cols] = value.astype(BF16)
 
 
@@ -292,13 +336,16 @@
 
     @pl.when(touched)
     def _():
-        entry = halves(carry_ref[...])
+        entry = carry_ref[...]
+        entry = jnp.concatenate([entry, entry - entry.astype(BF16).astype(F32)], axis=0).T.astype(BF16)
         width = out_ref.shape[1]
         for tile in range(width // 256):
             cols = slice(tile * 256, tile * 256 + 256)
-            outer = jnp.dot(c_ref[...], carried_ref[:, cols], preferred_element_type=F32)
-            scale = outer_dot(entry, rep16_ref[:, cols])
-            out_ref[:, cols] = (base_ref[:, cols].astype(F32) + scale * outer).astype(BF16)
+            for part in range(BLOCK // CHUNK):
+                rows = slice(part * CHUNK, part * CHUNK + CHUNK)
+                outer = jnp.dot(c_ref[rows, :], carried_ref[:, cols], preferred_element_type=F32)
+                scale = jnp.dot(entry[rows], rep16_ref[:, cols], preferred_element_type=F32)
+                out_ref[rows, cols] = (base_ref[rows, cols].astype(F32) + scale * outer).astype(BF16)
 
     @pl.when(jnp.logical_not(touched))
     def _():
@@ -327,10 +374,15 @@
     shard = lax.axis_index("seq").astype(jnp.int32).reshape(1)
     rows_in = conv_input[0]
     rim = shifted(rows_in[span - 16 :], "seq", 1)
-    rep = (jnp.arange(width)[None, :] // P_SIZE == jnp.arange(heads)[:, None]).astype(F32)
-    rep16 = jnp.concatenate([rep, rep], 0).astype(BF16)
-    ticks = jnp.arange(CHUNK)
+    rep = (np.arange(width)[None, :] // P_SIZE == np.arange(heads)[:, None]).astype(np.float32)
+    rep16 = np.concatenate([rep, rep], 0).astype(BF16)
+    ticks = np.arange(CHUNK)
     tri = (ticks[:, None] <= ticks[None, :]).astype(BF16)
+    order = np.arange(3 * CHUNK)
+    tick, lag = 8 * (order // 24) + order % 8, order % 24 // 8 + 1
+    source = np.arange(CHUNK + 16)
+    move = (source[None, :] - 16 == (tick - lag)[:, None]).astype(BF16)
+    slot = np.broadcast_to((4 * tick + lag)[:, None], (3 * CHUNK, 128)).astype(np.int32)
     smem = pl.BlockSpec(memory_space=pltpu.SMEM)
     per_head = pl.BlockSpec((heads, BLOCK), lambda i, *_: (0, i))
     act, cum, carry, sin, pay, fin, first, meta = pl.pallas_call(
@@ -343,6 +395,7 @@
             per_head, per_head,
             whole((4, channels)), whole((1, channels)),
             whole((heads, width)), whole((2 * heads, width)), whole((CHUNK, CHUNK)),
+            whole(move.shape), whole(slot.shape),
         ],
         out_specs=[
             pl.BlockSpec((BLOCK, channels), lambda i: (i, 0)),
@@ -363,9 +416,11 @@
         ],
         scratch_shapes=[
             pltpu.VMEM((N, width), F32),
-            pltpu.VMEM((8, channels), F32),
             pltpu.VMEM((16, channels), BF16),
             pltpu.VMEM((heads, CHUNK), F32),
+            pltpu.VMEM((BLOCK // CHUNK, heads, CHUNK), F32),
+            pltpu.VMEM((8, channels), F32),
+            pltpu.VMEM((1 + BLOCK // CHUNK,) + move.shape, BF16),
             pltpu.SMEM((owners,), jnp.int32),
         ],
         compiler_params=params(),
@@ -375,7 +430,7 @@
         name="states",
     )(
         shard, doc_bounds, doc_owner, rows_in, rim, step_size[0], log_decay[0],
-        conv_weight * 0.5, conv_bias[None] * 0.5, rep, rep16, tri,
+        conv_weight, conv_bias[None], rep, rep16, tri, move, slot,
     )
 
     gathered = lax.all_gather(pay[None], "seq", axis=0, tiled=True)
@@ -402,6 +457,7 @@
         name="outputs",
     )(meta, act, step_size[0], cum, sin, gain, rep16)
 
+    gathered, base = lax.optimization_barrier((gathered, base))
     carried, fin = pl.pallas_call(
         carry_kernel,
         grid_spec=pltpu.PrefetchScalarGridSpec(

time: 151 us -> 130 us (0.86)
  the two profiles are of different devices: /device:TPU:11 before, /device:TPU:0 now
where the time goes in v2:
time: 130 us; the launch traced here: 129 us
  Pallas kernels  74.4 us (57%)
  waiting for transfers between devices  27.7 us (21%)
  between operations  14.1 us (11%)
  starting transfers between devices  6.03 us (5%)
  local copies, waits for them, and re-layouts  4.32 us (3%)
  other arithmetic  2.48 us (2%)
    pallas_call x1, Pallas kernels, on_device(): pl.pallas_call(states_kernel, grid=(steps,), in_specs=[smem, smem, smem,...  40.4 us
    pallas_call x1, Pallas kernels, on_device(): pl.pallas_call(output_kernel, grid_spec=prefetch(grid=(steps,), in_specs=...  20.3 us
    all_to_all x1, waiting for transfers between devices, on_device(): lax.all_to_all(fin.reshape(owners, CAP, rows, N), 'stream', split_axis=0,...  15.9 us
    all_gather x1, waiting for transfers between devices, on_device(): gathered = lax.all_gather(pay[None], 'seq', axis=0, tiled=True)  11.7 us
    pallas_call x1, Pallas kernels, on_device(): pl.pallas_call(correct_kernel, grid_spec=prefetch(grid=(steps,), in_specs...  10.3 us
    all_to_all x1, starting transfers between devices, on_device(): lax.all_to_all(fin.reshape(owners, CAP, rows, N), 'stream', split_axis=0,...  3.64 us
    pallas_call x1, Pallas kernels, on_device(): pl.pallas_call(carry_kernel, grid_spec=pltpu.PrefetchScalarGridSpec(num_s...  3.34 us
  transfers between devices with their start and end apart: 3, of which 2 were waited for; matrix products, arithmetic and copies ran while one was open for 2% of the time, Pallas kernels for 24%

profile of v2, /device:TPU:0, one launch (start us, length us, event | category | flops | bytes accessed | tf_op | source)
XLA Modules:
  0.0 129.0 jit_solution(10597293483669513146)
XLA Ops:
  7.2 0.0 copy-start.1
  7.2 0.0 all-gather.3.cloned.1.call-start
  7.2 0.8 slice_bitcast_fusion
  8.0 2.3 %collective-permute-start = (bf16[16,1280]{1,0:T(8,128)(2,1)S(1)}, bf16[16,1280]{1,0:T(8,128)(2,1)S(1)}, u32[]{:S(2)}, u32[]{:S(2)}) collective-permute-start(bf16[16,1280]{1,0:T(8,128)(2,1)S(1)} %slice_bitcast_fusion), channel_id=1, source_target_pairs={{0,1},{1,2},{2,3},{3,4},{4,5},{5,6},{6,7},{8,9},{9,10},{10,11},{11... | collective-permute-start | bytes 122888 | tf_op jit(solution)/shard_map/ppermute | solution.py:30
  10.4 1.3 %broadcast_in_dim.12.bias_ref = f32[1,1280]{1,0:T(1,128)} reshape(f32[1280]{0:T(1024)} %param.15) | data formatting | bytes 10240 | tf_op jit(solution)/shard_map/broadcast_in_dim | solution.py:433
  11.7 0.0 collective-permute-done.rim_ref
  11.7 0.0 copy-start
  11.7 0.6 copy-done
  12.3 40.4 %states.1 = (bf16[4096,1280]{1,0:T(8,128)(2,1)}, f32[16,4096]{1,0:T(8,128)}, f32[16,4096]{1,0:T(8,128)}, bf16[32,128,1024]{2,1,0:T(8,128)(2,1)}, bf16[144,1024]{...) custom-call(s32[1]{0:T(128)} %bitcast.shard_ref, s32[1,32]{1,0:T(1,128)} %bounds.1, ...), custom_call_target="tpu_custom_call" | custom-call | flops 2147483648 | bytes 41943040 | tf_op jit(solution)/shard_map/states/pallas_call | solution.py:388
  52.7 0.0 all-gather.3.cloned.1.call-update
  52.7 0.0 copy-done.1
  52.7 0.1 broadcast_in_dim.14
  52.8 0.7 broadcast_in_dim_reshape.3.gain_ref
  53.5 20.3 %outputs.1.base_ref = bf16[4096,1024]{1,0:T(8,128)(2,1)} custom-call(s32[16]{0:T(128)} %get-tuple-element.15.meta, bf16[4096,1280]{1,0:T(8,128)(2,1)} %get-tuple-element.17.act_ref.c_ref, f32[16,4096]{1,0:T(8,128)} %bitcast.22, f32[16,4096]{1,0:T(8,128)} %get-tuple-element.18.cum_ref, bf16[32,128,1024]{2,1,0:T(8,128)(2,1)} %get-tuple-element.19.sin_ref, ...), custom_call_target="tpu_custom_call" | custom-call | flops 4294967296 | bytes 31457280 | tf_op jit(solution)/shard_map/outputs/pallas_call | solution.py:440
  73.8 11.7 %all-gather.3.cloned.1.call-done = bf16[1152,1024]{1,0:T(8,128)(2,1)} async-done(((bf16[144,1024]{1,0:T(8,128)(2,1)}), bf16[1152,1024]{1,0:T(8,128)(2,1)}) %all-gather.3.cloned.1.call-update) | async-done | bytes 2359312 | tf_op jit(solution)/shard_map/all_gather | solution.py:436
  85.5 3.3 %carry.1 = (bf16[128,1024]{1,0:T(8,128)(2,1)}, bf16[8,1056,128]{2,1,0:T(8,128)(2,1)}) custom-call(s32[1]{0:T(128)} %bitcast.shard_ref, s32[16]{0:T(128)} %get-tuple-element.15.meta, bf16[8,144,1024]{2,1,0:T(8,128)(2,1)} %bitcast.20, f32[8,1024]{1,0:T(8,128)} %get-tuple-element.23.first_ref, ...), custom_call_target="tpu_custom_call", output_to_operand_aliasing={{1}: (4, {})} | custom-call | tf_op jit(solution)/shard_map/carry/pallas_call | solution.py:461
  88.9 3.6 %all-to-all-start = ((bf16[4,2,1056,128]{3,2,1,0:T(8,128)(2,1)}), bf16[4,2,1056,128]{3,2,1,0:T(8,128)(2,1)S(1)}, u32[]{:S(2)}, u32[]{:S(2)}) async-start(bf16[4,2,1056,128]{3,2,1,0:T(8,128)(2,1)} %bitcast.18), calls=%async_computation | async-start | bytes 4325376 | tf_op jit(solution)/shard_map/all_to_all | solution.py:485
  92.5 10.3 %correct.1 = bf16[4096,1024]{1,0:T(8,128)(2,1)} custom-call(s32[16]{0:T(128)} %get-tuple-element.15.meta, bf16[4096,1024]{1,0:T(8,128)(2,1)} %outputs.1.base_ref, bf16[4096,1280]{1,0:T(8,128)(2,1)} %get-tuple-element.17.act_ref.c_ref, f32[16,4096]{1,0:T(8,128)} %get-tuple-element.21.carry_ref, ...), custom_call_target="tpu_custom_call", output_to_operand_aliasing={{}: (1, {})} | custom-call | flops 1073741824 | bytes 18874368 | tf_op jit(solution)/shard_map/correct/pallas_call | solution.py:489
  102.8 15.9 %all-to-all-done = bf16[4,2,1056,128]{3,2,1,0:T(8,128)(2,1)S(1)} async-done(((bf16[4,2,1056,128]{3,2,1,0:T(8,128)(2,1)}), bf16[4,2,1056,128]{3,2,1,0:T(8,128)(2,1)S(1)}, u32[]{:S(2)}, u32[]{:S(2)}) %all-to-all-start) | async-done | bytes 2162720 | tf_op jit(solution)/shard_map/all_to_all | solution.py:485
  118.8 0.1 slice.16
  118.9 2.5 %convert.1 = f32[1,1,4,2,16,64,128]{6,5,4,3,2,1,0:T(8,128)} convert(bf16[1,1,4,2,16,64,128]{6,5,4,3,2,1,0:T(8,128)(2,1)S(1)} %bitcast.19) | non-fusion elementwise | flops 1048576 | bytes 6291456 | tf_op jit(solution)/shard_map/reshape | solution.py:510
  121.5 0.7 reshape.30
  (3 shorter events, 0.1 us)
Async XLA Ops:
  7.2 45.6 %copy-start.1 = (f32[16]{0:T(128)S(1)}, f32[16]{0:T(128)}, u32[]{:S(2)}) copy-start(f32[16]{0:T(128)} %param.18) | copy-start | bytes 196
  7.2 78.4 %all-gather.3.cloned.1.call-start = ((), (), s32[]{:S(2)}) async-start(), calls=%async_computation.1 | async-start | bytes 2654208 | tf_op jit(solution)/shard_map/all_gather | solution.py:436
  8.0 3.7 %collective-permute-start = (bf16[16,1280]{1,0:T(8,128)(2,1)S(1)}, bf16[16,1280]{1,0:T(8,128)(2,1)S(1)}, u32[]{:S(2)}, u32[]{:S(2)}) collective-permute-start(bf16[16,1280]{1,0:T(8,128)(2,1)S(1)} %slice_bitcast_fusion), channel_id=1, source_target_pairs={{0,1},{1,2},{2,3},{3,4},{4,5},{5,6},{6,7},{8,9},{9,10},{10,11},{11... | collective-permute-start | bytes 122888 | tf_op jit(solution)/shard_map/ppermute | solution.py:30
  11.7 0.6 copy-start
  88.9 29.9 %all-to-all-start = ((bf16[4,2,1056,128]{3,2,1,0:T(8,128)(2,1)}), bf16[4,2,1056,128]{3,2,1,0:T(8,128)(2,1)S(1)}, u32[]{:S(2)}, u32[]{:S(2)}) async-start(bf16[4,2,1056,128]{3,2,1,0:T(8,128)(2,1)} %bitcast.18), calls=%async_computation | async-start | bytes 4325376 | tf_op jit(solution)/shard_map/all_to_all | solution.py:485
Sparse Core Ops, SparseCore 0:
  52.9 32.6 all-gather.2

commit v3 on v2

--- a/solution.py
+++ b/solution.py
@@ -267,8 +267,9 @@
         pay_ref[N:] = jnp.where(iota((16, width), 0) == 0, high, gate - high).astype(BF16)
 
 
-def output_kernel(meta, act_ref, dt_ref, cum_ref, sin_ref, gain_ref, rep16_ref, out_ref):
-    step = pl.program_id(0)
+def output_kernel(origin, held, meta, act_ref, dt_ref, cum_ref, sin_ref, gain_ref, rep16_ref, *refs):
+    out_ref = refs[held]
+    step = origin + pl.program_id(0)
     heads = dt_ref.shape[0]
     width = out_ref.shape[1]
     for part in range(BLOCK // CHUNK):
@@ -312,9 +313,31 @@
             out_ref[rows, cols] = value.astype(BF16)
 
 
-def carry_kernel(shard_ref, meta, gathered, first_ref, fin_in, carried_ref, fin_ref, held):
-    del meta
-    width = first_ref.shape[1]
+def gates_of(pay_ref, cols):
+    gates = pay_ref[N:, cols].astype(F32)
+    return gates[0:1] + gates[1:2]
+
+
+def pair_kernel(shard_ref, own_ref, got_ref, half_ref):
+    side = half_ref.shape[1]
+
+    def join(early, late, cols):
+        after = gates_of(late, cols)
+        gate = jnp.broadcast_to(after * gates_of(early, cols), (PAY - N, side))
+        high = gate.astype(BF16).astype(F32)
+        half_ref[:N] = (late[:N, cols].astype(F32) + after * early[:N, cols].astype(F32)).astype(BF16)
+        half_ref[N:] = jnp.where(iota((PAY - N, side), 0) == 0, high, gate - high).astype(BF16)
+
+    @pl.when(shard_ref[0] % 2 == 0)
+    def _():
+        join(own_ref, got_ref, slice(0, side))
+
+    @pl.when(shard_ref[0] % 2 == 1)
+    def _():
+        join(got_ref, own_ref, slice(side, 2 * side))
+
+
+def prefix_kernel(shard_ref, gathered, prefix_ref, held):
     held[...] = jnp.zeros_like(held)
 
     def one(index, _):
@@ -322,12 +345,28 @@
         held[...] = (gates[0:1] + gates[1:2]) * held[...] + gathered[index, :N].astype(F32)
         return 0
 
-    lax.fori_loop(0, shard_ref[0], one, 0)
-    carried_ref[...] = held[...].astype(BF16)
-    fin_ref[0, :width] = (
-        fin_in[0, :width].astype(F32) + (first_ref[0:1] * held[...]).T
-    ).astype(BF16)
-    fin_ref[0, width:] = fin_in[0, width:]
+    lax.fori_loop(0, shard_ref[0] // 2, one, 0)
+    prefix_ref[...] = held[...].astype(BF16)
+
+
+def carry_kernel(shard_ref, meta, mine_ref, other_ref, early_ref, first_ref, carried_ref, send_ref):
+    side = mine_ref.shape[1]
+    lower, upper = slice(0, side), slice(side, 2 * side)
+
+    @pl.when(shard_ref[0] % 2 == 0)
+    def _():
+        carried_ref[:, lower] = mine_ref[...]
+        carried_ref[:, upper] = other_ref[...]
+
+    @pl.when(shard_ref[0] % 2 == 1)
+    def _():
+        for cols, part in ((lower, other_ref), (upper, mine_ref)):
+            carried_ref[:, cols] = (
+                early_ref[:N, cols].astype(F32) + gates_of(early_ref, cols) * part[...].astype(F32)
+            ).astype(BF16)
+
+    send_ref[...] = jnp.zeros_like(send_ref)
+    send_ref[meta[5] // CAP] = (first_ref[0:1] * carried_ref[...].astype(F32)).T.astype(BF16)
 
 
 def correct_kernel(meta, base_ref, c_ref, carry_ref, carried_ref, rep16_ref, out_ref):
@@ -341,11 +380,9 @@
         width = out_ref.shape[1]
         for tile in range(width // 256):
             cols = slice(tile * 256, tile * 256 + 256)
-            for part in range(BLOCK // CHUNK):
-                rows = slice(part * CHUNK, part * CHUNK + CHUNK)
-                outer = jnp.dot(c_ref[rows, :], carried_ref[:, cols], preferred_element_type=F32)
-                scale = jnp.dot(entry[rows], rep16_ref[:, cols], preferred_element_type=F32)
-                out_ref[rows, cols] = (base_ref[rows, cols].astype(F32) + scale * outer).astype(BF16)
+            outer = jnp.dot(c_ref[...], carried_ref[:, cols], preferred_element_type=F32)
+            scale = jnp.dot(entry, rep16_ref[:, cols], preferred_element_type=F32)
+            out_ref[:, cols] = (base_ref[:, cols].astype(F32) + scale * outer).astype(BF16)
 
     @pl.when(jnp.logical_not(touched))
     def _():
@@ -433,58 +470,83 @@
         conv_weight, conv_bias[None], rep, rep16, tri, move, slot,
     )
 
-    gathered = lax.all_gather(pay[None], "seq", axis=0, tiled=True)
-
     gain = jnp.repeat(skip_gain, P_SIZE)[None]
     prefetch = functools.partial(pltpu.PrefetchScalarGridSpec, num_scalar_prefetch=1)
-    base = pl.pallas_call(
-        output_kernel,
-        grid_spec=prefetch(
-            grid=(steps,),
-            in_specs=[
-                pl.BlockSpec((BLOCK, channels), lambda i, *_: (i, 0)),
-                per_head, per_head,
-                pl.BlockSpec((BLOCK // CHUNK, N, width), lambda i, *_: (i, 0, 0)),
-                whole((1, width)), whole((2 * heads, width)),
-            ],
-            out_specs=pl.BlockSpec((BLOCK, width), lambda i, *_: (i, 0)),
-        ),
-        out_shape=jax.ShapeDtypeStruct((span, width), BF16),
-        compiler_params=params(),
-        cost_estimate=pl.CostEstimate(
-            flops=2 * span * width * N * 4, bytes_accessed=30 << 20, transcendentals=span * CHUNK * heads
-        ),
-        name="outputs",
-    )(meta, act, step_size[0], cum, sin, gain, rep16)
-
-    gathered, base = lax.optimization_barrier((gathered, base))
-    carried, fin = pl.pallas_call(
-        carry_kernel,
-        grid_spec=pltpu.PrefetchScalarGridSpec(
-            num_scalar_prefetch=2,
-            grid=(1,),
-            in_specs=[
-                whole(gathered.shape), whole((8, width)),
-                pl.BlockSpec((1, rows, N), lambda i, shard_ref, meta: (meta[5], 0, 0)),
-            ],
-            out_specs=[
-                whole((N, width)),
-                pl.BlockSpec((1, rows, N), lambda i, shard_ref, meta: (meta[5], 0, 0)),
-            ],
-            scratch_shapes=[pltpu.VMEM((N, width), F32)],
-        ),
-        out_shape=[
-            jax.ShapeDtypeStruct((N, width), BF16),
-            jax.ShapeDtypeStruct((slots, rows, N), BF16),
-        ],
-        input_output_aliases={4: 1},
-        compiler_params=params(),
-        name="carry",
-    )(shard, meta, gathered, first, fin)
-
+
+    def outputs(first, last, base):
+        hold = [] if base is None else [base]
+        return pl.pallas_call(
+            functools.partial(output_kernel, first, bool(hold)),
+            grid_spec=prefetch(
+                grid=(last - first,),
+                in_specs=[
+                    pl.BlockSpec((BLOCK, channels), lambda i, *_: (first + i, 0)),
+                    pl.BlockSpec((heads, BLOCK), lambda i, *_: (0, first + i)),
+                    pl.BlockSpec((heads, BLOCK), lambda i, *_: (0, first + i)),
+                    pl.BlockSpec((BLOCK // CHUNK, N, width), lambda i, *_: (first + i, 0, 0)),
+                    whole((1, width)), whole((2 * heads, width)),
+                ] + [pl.BlockSpec(memory_space=pl.ANY)] * len(hold),
+                out_specs=pl.BlockSpec((BLOCK, width), lambda i, *_: (first + i, 0)),
+            ),
+            out_shape=jax.ShapeDtypeStruct((span, width), BF16),
+            input_output_aliases={7: 0} if hold else {},
+            compiler_params=params(),
+            cost_estimate=pl.CostEstimate(
+                flops=2 * (last - first) * BLOCK * width * N * 4,
+                bytes_accessed=(last - first) * (4 << 20),
+                transcendentals=(last - first) * BLOCK * CHUNK * heads,
+            ),
+            name="outputs",
+        )(meta, act, step_size[0], cum, sin, gain, rep16, *hold)
+
+    side = width // 2
+    count = lax.axis_size("seq")
+    pairs = [(index, index ^ 1) for index in range(count)]
+    early = lax.ppermute(pay, "seq", pairs)
+    base = outputs(0, 1, None)
+    early, base = lax.optimization_barrier((early, base))
+    half = pl.pallas_call(
+        pair_kernel,
+        in_specs=[smem, whole((PAY, width)), whole((PAY, width))],
+        out_specs=whole((PAY, side)),
+        out_shape=jax.ShapeDtypeStruct((PAY, side), BF16),
+        compiler_params=pltpu.CompilerParams(vmem_limit_bytes=VMEM),
+        name="pair",
+    )(shard, pay, early)
+    half, fin = lax.optimization_barrier((half, fin))
+    gathered = lax.all_gather(
+        half[None], "seq", axis=0, tiled=True,
+        axis_index_groups=[list(range(0, count, 2)), list(range(1, count, 2))],
+    )
     got = lax.all_to_all(
         fin.reshape(owners, CAP, rows, N), "stream", split_axis=0, concat_axis=0, tiled=True
     )
+    base = outputs(1, steps - 2, base)
+    gathered, base = lax.optimization_barrier((gathered, base))
+    mine = pl.pallas_call(
+        prefix_kernel,
+        in_specs=[smem, whole(gathered.shape)],
+        out_specs=whole((N, side)),
+        out_shape=jax.ShapeDtypeStruct((N, side), BF16),
+        scratch_shapes=[pltpu.VMEM((N, side), F32)],
+        compiler_params=pltpu.CompilerParams(vmem_limit_bytes=VMEM),
+        name="prefix",
+    )(shard, gathered)
+    other = lax.ppermute(mine, "seq", pairs)
+    base = outputs(steps - 2, steps, base)
+    other, base = lax.optimization_barrier((other, base))
+    carried, send = pl.pallas_call(
+        carry_kernel,
+        in_specs=[smem, smem, whole((N, side)), whole((N, side)), whole((PAY, width)), whole((8, width))],
+        out_specs=[whole((N, width)), whole((owners, width, N))],
+        out_shape=[
+            jax.ShapeDtypeStruct((N, width), BF16),
+            jax.ShapeDtypeStruct((owners, width, N), BF16),
+        ],
+        compiler_params=pltpu.CompilerParams(vmem_limit_bytes=VMEM),
+        name="carry",
+    )(shard, meta, mine, other, early, first)
+    more = lax.all_to_all(send, "stream", split_axis=0, concat_axis=0, tiled=True)
 
     out = pl.pallas_call(
         correct_kernel,
@@ -507,7 +569,9 @@
         name="correct",
     )(meta, base, act, carry, carried, rep16)
 
-    ssm = got[:, :, :width].astype(F32).reshape(1, 1, owners, CAP, heads, P_SIZE, N)
+    more = jnp.concatenate([more[:, None], jnp.zeros((owners, CAP - 1, width, N), BF16)], axis=1)
+    ssm = got[:, :, :width].astype(F32) + more.astype(F32)
+    ssm = ssm.reshape(1, 1, owners, CAP, heads, P_SIZE, N)
     tiles = channels // N
     conv = got[:, :, width : width + 3 * tiles].reshape(owners, CAP, tiles, 3, N)
     conv = conv.transpose(0, 1, 3, 2, 4).reshape(1, 1, owners, CAP, 3, channels)

time: 130 us -> 153 us (1.18)
  blocking collectives: 0 us -> 40.1 us
  between operations: 14.1 us -> 0.71 us
  waiting for transfers between devices: 27.7 us -> 14.6 us
  Pallas kernels: 74.4 us -> 83.2 us
  local copies, waits for them, and re-layouts: 4.32 us -> 7.9 us
  other arithmetic: 2.48 us -> 0.28 us
    all_to_all x0 -> x1, blocking collectives: none -> 22.3 us  [on_device(): lax.all_to_all(send, 'stream', split_axis=0, concat_axis=0, tiled=True)]
    all_gather x0 -> x1, blocking collectives: none -> 17.8 us  [on_device(): lax.all_gather(half[None], 'seq', axis=0, tiled=True, axis_index_groups=[...]
    all_gather x1 -> x0, waiting for transfers between devices: 11.7 us -> none  [on_device(): gathered = lax.all_gather(pay[None], 'seq', axis=0, tiled=True)]
    pallas_call x2 -> x6, Pallas kernels: 23.7 us -> 32.8 us  [the longest x3 26.9 us: outputs(): pl.pallas_call(functools.partial(output_kernel, first, bool(hold)), grid_...]
    unnamed x4 -> x9, local copies, waits for them, and re-layouts: 0.62 us -> 4.34 us
    reshape x1 -> x0, other arithmetic: 2.48 us -> none  [on_device(): got[:, :, :width].astype(F32).reshape(1, 1, owners, CAP, heads, P_SIZE, N)]
  transfers between devices with their start and end apart: 3 -> 4, of which waited for: 2 -> 1; matrix products, arithmetic and copies ran while one was open for 2% -> 1% of each run, Pallas kernels for 24% -> 15%
where the time goes in v3:
time: 153 us
  Pallas kernels  83.2 us (54%)
  blocking collectives  40.1 us (26%)
  waiting for transfers between devices  14.6 us (10%)
  local copies, waits for them, and re-layouts  7.9 us (5%)
  starting transfers between devices  6.04 us (4%)
    pallas_call x1, Pallas kernels, on_device(): pl.pallas_call(states_kernel, grid=(steps,), in_specs=[smem, smem, smem,...  40.1 us
    pallas_call x3, Pallas kernels, outputs(): pl.pallas_call(functools.partial(output_kernel, first, bool(hold)), grid_...  26.9 us
    all_to_all x1, blocking collectives, on_device(): lax.all_to_all(send, 'stream', split_axis=0, concat_axis=0, tiled=True)  22.3 us
    all_gather x1, blocking collectives, on_device(): lax.all_gather(half[None], 'seq', axis=0, tiled=True, axis_index_groups=[...  17.8 us
    all_to_all x1, waiting for transfers between devices, on_device(): lax.all_to_all(fin.reshape(owners, CAP, rows, N), 'stream', split_axis=0,...  14.6 us
    pallas_call x1, Pallas kernels, on_device(): pl.pallas_call(correct_kernel, grid_spec=prefetch(grid=(steps,), in_specs...  10.3 us
    unnamed x9, local copies, waits for them, and re-layouts  4.34 us
    all_to_all x1, starting transfers between devices, on_device(): lax.all_to_all(fin.reshape(owners, CAP, rows, N), 'stream', split_axis=0,...  3.62 us
  transfers between devices with their start and end apart: 4, of which 1 were waited for; matrix products, arithmetic and copies ran while one was open for 1% of the time, Pallas kernels for 15%

profile of v3, /device:TPU:0, one launch (start us, length us, event | category | flops | bytes accessed | tf_op | source)
XLA Modules:
  0.0 152.9 jit_solution(16558057940641741418)
XLA Ops:
  0.6 0.8 slice_bitcast_fusion
  1.4 2.3 %collective-permute-start = (bf16[16,1280]{1,0:T(8,128)(2,1)S(1)}, bf16[16,1280]{1,0:T(8,128)(2,1)S(1)}, u32[]{:S(2)}, u32[]{:S(2)}) collective-permute-start(bf16[16,1280]{1,0:T(8,128)(2,1)S(1)} %slice_bitcast_fusion), channel_id=1, source_target_pairs={{0,1},{1,2},{2,3},{3,4},{4,5},{5,6},{6,7},{8,9},{9,10},{10,11},{11... | collective-permute-start | bytes 122888 | tf_op jit(solution)/shard_map/ppermute | solution.py:30
  3.8 1.3 broadcast_in_dim.16.bias_ref
  5.1 0.6 copy-done.2
  5.7 40.1 %states.1 = (bf16[4096,1280]{1,0:T(8,128)(2,1)}, f32[16,4096]{1,0:T(8,128)}, f32[16,4096]{1,0:T(8,128)}, bf16[32,128,1024]{2,1,0:T(8,128)(2,1)}, bf16[144,1024]{...) custom-call(s32[1]{0:T(128)} %bitcast.shard_ref, s32[1,32]{1,0:T(1,128)} %bounds.1, ...), custom_call_target="tpu_custom_call" | custom-call | flops 2147483648 | bytes 41943040 | tf_op jit(solution)/shard_map/states/pallas_call | solution.py:425
  45.8 0.1 collective-permute-start.1
  45.9 0.1 broadcast_in_dim.17
  46.0 0.7 broadcast_in_dim_reshape.3.gain_ref
  46.7 5.4 %outputs.3.refs_0_ = bf16[4096,1024]{1,0:T(8,128)(2,1)} custom-call(s32[16]{0:T(128)} %get-tuple-element.21.meta, bf16[4096,1280]{1,0:T(8,128)(2,1)} %get-tuple-element.23.act_ref.c_ref, f32[16,4096]{1,0:T(8,128)} %bitcast.20, f32[16,4096]{1,0:T(8,128)} %get-tuple-element.24.cum_ref, bf16[32,128,1024]{2,1,0:T(8,128)(2,1)} %get-tuple-element.25.sin_ref, ...), custom_call_target="tpu_custom_call" | custom-call | flops 536870912 | bytes 4194304 | tf_op jit(solution)/shard_map/outputs/pallas_call | solution.py:478
  52.1 0.7 copy-done
  52.8 1.8 %pair.1 = bf16[144,512]{1,0:T(8,128)(2,1)} custom-call(s32[1]{0:T(128)} %bitcast.shard_ref, bf16[144,1024]{1,0:T(8,128)(2,1)} %get-tuple-element.22.own_ref, bf16[144,1024]{1,0:T(8,128)(2,1)} %copy-done), custom_call_target="tpu_custom_call" | custom-call | tf_op jit(solution)/shard_map/pair/pallas_call | solution.py:508
  54.6 17.8 %all-gather = bf16[576,512]{1,0:T(8,128)(2,1)} all-gather(bf16[144,512]{1,0:T(8,128)(2,1)} %pair.1), channel_id=2, replica_groups={{0,2,4,6},{1,3,5,7},{8,10,12,14},{9,11,13,15},{16,18,20,22},{17,19,21,2..., dimensions={0}, use_global_device_ids=true | all-gather | bytes 737280 | tf_op jit(solution)/shard_map/all_gather | solution.py:517
  72.4 13.9 %outputs.4.refs_0_ = bf16[4096,1024]{1,0:T(8,128)(2,1)} custom-call(s32[16]{0:T(128)} %get-tuple-element.21.meta, bf16[4096,1280]{1,0:T(8,128)(2,1)} %get-tuple-element.23.act_ref.c_ref, f32[16,4096]{1,0:T(8,128)} %bitcast.21, f32[16,4096]{1,0:T(8,128)} %get-tuple-element.24.cum_ref, ...), custom_call_target="tpu_custom_call", output_to_operand_aliasing={{}: (7, {})} | custom-call | flops 2684354560 | bytes 20971520 | tf_op jit(solution)/shard_map/outputs/pallas_call | solution.py:478
  86.3 1.7 %prefix.1.mine_ref = bf16[128,512]{1,0:T(8,128)(2,1)} custom-call(s32[1]{0:T(128)} %bitcast.shard_ref, bf16[4,144,512]{2,1,0:T(8,128)(2,1)} %bitcast.24), custom_call_target="tpu_custom_call" | custom-call | tf_op jit(solution)/shard_map/prefix/pallas_call | solution.py:526
  88.1 7.6 %outputs.5.base_ref = bf16[4096,1024]{1,0:T(8,128)(2,1)} custom-call(s32[16]{0:T(128)} %get-tuple-element.21.meta, bf16[4096,1280]{1,0:T(8,128)(2,1)} %get-tuple-element.23.act_ref.c_ref, f32[16,4096]{1,0:T(8,128)} %bitcast.22, f32[16,4096]{1,0:T(8,128)} %get-tuple-element.24.cum_ref, ...), custom_call_target="tpu_custom_call", output_to_operand_aliasing={{}: (7, {})} | custom-call | flops 1073741824 | bytes 8388608 | tf_op jit(solution)/shard_map/outputs/pallas_call | solution.py:478
  95.6 0.7 copy-done.1
  96.3 2.4 %carry.1 = (bf16[128,1024]{1,0:T(8,128)(2,1)}, bf16[4,1024,128]{2,1,0:T(8,128)(2,1)}) custom-call(s32[1]{0:T(128)} %bitcast.shard_ref, s32[16]{0:T(128)} %get-tuple-element.21.meta, bf16[128,512]{1,0:T(8,128)(2,1)} %prefix.1.mine_ref, bf16[128,512]{1,0:T(8,128)(2,1)} %copy-done.1, bf16[144,1024]{1,0:T(8,128)(2,1)} %copy-done, ...), custom_call_target="tpu_custom_call" | custom-call | tf_op jit(solution)/shard_map/carry/pallas_call | solution.py:538
  98.7 22.3 %all_to_all.10 = bf16[4,1024,128]{2,1,0:T(8,128)(2,1)S(1)} all-to-all(bf16[4,1024,128]{2,1,0:T(8,128)(2,1)} %get-tuple-element.38), channel_id=1, replica_groups=mesh['stream'=4,'seq'=8] {'stream'}, dimensions={0} | all-to-all | bytes 2097152 | tf_op jit(solution)/shard_map/all_to_all | solution.py:549
  121.0 3.6 %all-to-all-start = ((bf16[4,2,1056,128]{3,2,1,0:T(8,128)(2,1)}), bf16[4,2,1056,128]{3,2,1,0:T(8,128)(2,1)S(1)}, u32[]{:S(2)}, u32[]{:S(2)}) async-start(bf16[4,2,1056,128]{3,2,1,0:T(8,128)(2,1)} %bitcast.25), calls=%async_computation | async-start | bytes 4325376 | tf_op jit(solution)/shard_map/all_to_all | solution.py:521
  124.6 10.3 %correct.1 = bf16[4096,1024]{1,0:T(8,128)(2,1)} custom-call(s32[16]{0:T(128)} %get-tuple-element.21.meta, bf16[4096,1024]{1,0:T(8,128)(2,1)} %outputs.5.base_ref, bf16[4096,1280]{1,0:T(8,128)(2,1)} %get-tuple-element.23.act_ref.c_ref, f32[16,4096]{1,0:T(8,128)} %get-tuple-element.33.carry_ref, ...), custom_call_target="tpu_custom_call", output_to_operand_aliasing={{}: (1, {})} | custom-call | flops 1073741824 | bytes 18874368 | tf_op jit(solution)/shard_map/correct/pallas_call | solution.py:551
  135.0 14.6 %all-to-all-done = bf16[4,2,1056,128]{3,2,1,0:T(8,128)(2,1)S(1)} async-done(((bf16[4,2,1056,128]{3,2,1,0:T(8,128)(2,1)}), bf16[4,2,1056,128]{3,2,1,0:T(8,128)(2,1)S(1)}, u32[]{:S(2)}, u32[]{:S(2)}) %all-to-all-start) | async-done | bytes 2162720 | tf_op jit(solution)/shard_map/all_to_all | solution.py:521
  149.6 0.3 convert_add_fusion
  149.9 2.3 %copy.28 = f32[1,1,4,2,16,64,128]{6,5,4,3,2,1,0:T(8,128)} copy(f32[1,1,4,2,16,64,128]{6,5,4,2,3,1,0:T(8,128)S(1)} %bitcast.17) | data formatting | bytes 8388608
  152.3 0.7 reshape.26
  (12 shorter events, 0.1 us)
Async XLA Ops:
  1.4 3.7 %collective-permute-start = (bf16[16,1280]{1,0:T(8,128)(2,1)S(1)}, bf16[16,1280]{1,0:T(8,128)(2,1)S(1)}, u32[]{:S(2)}, u32[]{:S(2)}) collective-permute-start(bf16[16,1280]{1,0:T(8,128)(2,1)S(1)} %slice_bitcast_fusion), channel_id=1, source_target_pairs={{0,1},{1,2},{2,3},{3,4},{4,5},{5,6},{6,7},{8,9},{9,10},{10,11},{11... | collective-permute-start | bytes 122888 | tf_op jit(solution)/shard_map/ppermute | solution.py:30
  5.1 0.6 copy-start.2
  5.7 40.2 %copy-start.3 = (f32[16]{0:T(128)S(1)}, f32[16]{0:T(128)}, u32[]{:S(2)}) copy-start(f32[16]{0:T(128)} %param.18) | copy-start | bytes 196
  45.8 6.2 %collective-permute-start.1 = (bf16[144,1024]{1,0:T(8,128)(2,1)}, bf16[144,1024]{1,0:T(8,128)(2,1)S(1)}, u32[]{:S(2)}, u32[]{:S(2)}) collective-permute-start(bf16[144,1024]{1,0:T(8,128)(2,1)} %get-tuple-element.22.own_ref), channel_id=1, source_target_pairs={{0,1},{1,0},{2,3},{3,2},{4,5},{5,4},{6,7},{7,6},{8,9},{9,8},{10,11... | collective-permute-start | bytes 884744 | tf_op jit(solution)/shard_map/ppermute | solution.py:505
  52.1 0.7 copy-start
  88.1 7.6 %collective-permute-start.2 = (bf16[128,512]{1,0:T(8,128)(2,1)}, bf16[128,512]{1,0:T(8,128)(2,1)S(1)}, u32[]{:S(2)}, u32[]{:S(2)}) collective-permute-start(bf16[128,512]{1,0:T(8,128)(2,1)} %prefix.1.mine_ref), channel_id=1, source_target_pairs={{0,1},{1,0},{2,3},{3,2},{4,5},{5,4},{6,7},{7,6},{8,9},{9,8},{10,11... | collective-permute-start | bytes 393224 | tf_op jit(solution)/shard_map/ppermute | solution.py:535
  95.6 0.7 copy-start.1
  121.0 28.6 %all-to-all-start = ((bf16[4,2,1056,128]{3,2,1,0:T(8,128)(2,1)}), bf16[4,2,1056,128]{3,2,1,0:T(8,128)(2,1)S(1)}, u32[]{:S(2)}, u32[]{:S(2)}) async-start(bf16[4,2,1056,128]{3,2,1,0:T(8,128)(2,1)} %bitcast.25), calls=%async_computation | async-start | bytes 4325376 | tf_op jit(solution)/shard_map/all_to_all | solution.py:521

commit v4 on v3

--- a/solution.py
+++ b/solution.py
@@ -18,7 +18,7 @@
 LOG2E = 1.4426950408889634
 PAY = 144
 TAIL = 32
-VMEM = 56 * 1024 * 1024
+MIB = 1024 * 1024
 
 F32 = jnp.float32
 BF16 = jnp.bfloat16
@@ -106,7 +106,7 @@
     meta[0] = start - anchor
 
 
-def conv_rows(x_ref, edge16, moves, weights, act_ref, part, choice):
+def conv_rows(x_ref, edge16, moves, weights, act_ref, first, part, choice):
     low = part * CHUNK
     rows = slice(low, low + CHUNK)
     pick = moves[choice]
@@ -121,7 +121,7 @@
         mixed = weights[4:5, cols] + weights[0:1, cols] * x_ref[rows, cols].astype(F32)
         for lag in range(1, 4):
             mixed = mixed + weights[lag : lag + 1, cols] * moved[:, lag - 1].reshape(CHUNK, 256)
-        act_ref[rows, cols] = (mixed + mixed * jnp.tanh(mixed)).astype(BF16)
+        act_ref[pl.ds(first + low, CHUNK), cols] = (mixed + mixed * jnp.tanh(mixed)).astype(BF16)
 
 
 def states_kernel(
@@ -135,7 +135,7 @@
     width = rep_ref.shape[1]
     span = pl.num_programs(0) * BLOCK
     parts = BLOCK // CHUNK
-    first = step * BLOCK
+    first = pl.multiple_of(step * BLOCK, BLOCK)
 
     @pl.when(step == 0)
     def _():
@@ -165,35 +165,36 @@
 
         choices.append(jnp.where(near, 1 + part, 0))
 
-    conv_rows(x_ref, edge16, moves, weights, act_ref, 0, choices[0])
+    conv_rows(x_ref, edge16, moves, weights, act_ref, first, 0, choices[0])
     running = total[...]
     for part in range(parts):
         low = part * CHUNK
         rows = slice(low, low + CHUNK)
         begin = first + low
         if part + 1 < parts:
-            conv_rows(x_ref, edge16, moves, weights, act_ref, part + 1, choices[part + 1])
+            conv_rows(x_ref, edge16, moves, weights, act_ref, first, part + 1, choices[part + 1])
         summed = jnp.dot(
             thirds(ld_ref[:, rows] * LOG2E), tri_ref[...], preferred_element_type=F32
         )
         cum = summed[:heads] + summed[heads : 2 * heads] + summed[2 * heads :]
-        cum_ref[:, rows] = cum
+        there = pl.ds(begin, CHUNK)
+        cum_ref[:, there] = cum
         lane = iota((heads, CHUNK), 1) + begin
         open_end = jnp.where(meta[0] < 0, meta[1], -1)
-        carry_ref[:, rows] = jnp.where(lane < open_end, jnp.exp2(running + cum), 0.0)
+        carry_ref[:, there] = jnp.where(lane < open_end, jnp.exp2(running + cum), 0.0)
         totals[part] = running
         start = last_start(meta, begin + CHUNK - 1)
         last = cum[:, CHUNK - 1 :]
         weight = jnp.where(lane >= start, jnp.exp2(last - cum) * dt_ref[:, rows], 0.0)
         weight = weight.T.astype(BF16)
         through = spread_row(jnp.where(start < begin, jnp.exp2(last), 0.0), rep_ref[...])
-        b_turned = act_ref[rows, width : width + N].T
+        b_turned = act_ref[there, width : width + N].T
         for tile in range(width // 256):
             cols = slice(tile * 256, tile * 256 + 256)
             held = state[:, cols]
             sin_ref[part, :, cols] = held.astype(BF16)
             scale = jnp.dot(weight, rep16_ref[:heads, cols], preferred_element_type=F32)
-            load = scale.astype(BF16) * act_ref[rows, cols]
+            load = scale.astype(BF16) * act_ref[there, cols]
             grown = jnp.dot(b_turned, load, preferred_element_type=F32)
             state[:, cols] = through[:, cols] * held + grown
         running = running + last
@@ -206,14 +207,15 @@
         low = pl.multiple_of(part * CHUNK, CHUNK)
         begin = first + low
         lane = iota((heads, CHUNK), 1) + begin
-        cum = cum_ref[:, pl.ds(low, CHUNK)]
+        there = pl.ds(pl.multiple_of(begin, CHUNK), CHUNK)
+        cum = cum_ref[:, there]
         at_end = jnp.sum(jnp.where(lane == end - 1, cum, 0.0), axis=1, keepdims=True)
         inside = (lane < end) & (lane >= start)
         weight = jnp.exp2(jnp.minimum(at_end - cum, 0.0)) * dt_ref[:, pl.ds(low, CHUNK)]
         weight = jnp.where(inside, weight, 0.0).T.astype(BF16)
         scale = jnp.dot(weight, rep16_ref[:heads], preferred_element_type=F32)
-        load = scale.astype(BF16) * act_ref[pl.ds(low, CHUNK), :width]
-        local = outer_dot(act_ref[pl.ds(low, CHUNK), width : width + N], load)
+        load = scale.astype(BF16) * act_ref[there, :width]
+        local = outer_dot(act_ref[there, width : width + N], load)
         through = spread_row(jnp.where(start < begin, jnp.exp2(at_end), 0.0), rep_ref[...])
         final = local + through * sin_ref[part].astype(F32)
         target = meta[5 + slot]
@@ -272,12 +274,13 @@
     step = origin + pl.program_id(0)
     heads = dt_ref.shape[0]
     width = out_ref.shape[1]
-    for part in range(BLOCK // CHUNK):
-        low = part * CHUNK
-        rows = slice(low, low + CHUNK)
-        begin = step * BLOCK + low
+    parts = BLOCK // CHUNK
+    for part in range(parts):
+        begin = pl.multiple_of(step * BLOCK + part * CHUNK, CHUNK)
+        rows = pl.ds(begin, CHUNK)
+        here = slice(part * CHUNK, part * CHUNK + CHUNK)
         cum = cum_ref[:, rows]
-        back = cum - jnp.log2(dt_ref[:, rows])
+        back = cum - jnp.log2(dt_ref[:, here])
         ahead = cum.T
         b_act = act_ref[rows, width : width + N]
         c_act = act_ref[rows, width + N : width + 2 * N]
@@ -337,19 +340,16 @@
         join(got_ref, own_ref, slice(side, 2 * side))
 
 
-def prefix_kernel(shard_ref, gathered, prefix_ref, held):
-    held[...] = jnp.zeros_like(held)
-
-    def one(index, _):
-        gates = gathered[index, N:].astype(F32)
-        held[...] = (gates[0:1] + gates[1:2]) * held[...] + gathered[index, :N].astype(F32)
-        return 0
-
-    lax.fori_loop(0, shard_ref[0] // 2, one, 0)
-    prefix_ref[...] = held[...].astype(BF16)
-
-
-def carry_kernel(shard_ref, meta, mine_ref, other_ref, early_ref, first_ref, carried_ref, send_ref):
+def prefix_kernel(*refs):
+    prefix_ref = refs[-1]
+    side = prefix_ref.shape[1]
+    total = jnp.zeros((N, side), F32)
+    for ref in refs[:-1]:
+        total = gates_of(ref, slice(0, side)) * total + ref[:N].astype(F32)
+    prefix_ref[...] = total.astype(BF16)
+
+
+def carry_kernel(shard_ref, stream_ref, meta, mine_ref, other_ref, early_ref, first_ref, carried_ref, *sends):
     side = mine_ref.shape[1]
     lower, upper = slice(0, side), slice(side, 2 * side)
 
@@ -365,32 +365,36 @@
                 early_ref[:N, cols].astype(F32) + gates_of(early_ref, cols) * part[...].astype(F32)
             ).astype(BF16)
 
-    send_ref[...] = jnp.zeros_like(send_ref)
-    send_ref[meta[5] // CAP] = (first_ref[0:1] * carried_ref[...].astype(F32)).T.astype(BF16)
-
-
-def correct_kernel(meta, base_ref, c_ref, carry_ref, carried_ref, rep16_ref, out_ref):
-    step = pl.program_id(0)
-    touched = (meta[0] < 0) & (meta[1] > step * BLOCK)
+    value = (first_ref[0:1] * carried_ref[...].astype(F32)).T.astype(BF16)
+    apart = (meta[5] // CAP) ^ stream_ref[0]
+    for index, ref in enumerate(sends):
+        ref[...] = jnp.where(apart == index, value, jnp.zeros_like(value))
+
+
+def correct_kernel(meta, base_ref, act_ref, carry_ref, carried_ref, rep16_ref, out_ref):
+    width = out_ref.shape[1]
+    begin = pl.multiple_of(pl.program_id(0) * BLOCK, BLOCK)
+    rows = pl.ds(begin, BLOCK)
+    touched = (meta[0] < 0) & (meta[1] > begin)
 
     @pl.when(touched)
     def _():
-        entry = carry_ref[...]
+        entry = carry_ref[:, rows]
         entry = jnp.concatenate([entry, entry - entry.astype(BF16).astype(F32)], axis=0).T.astype(BF16)
-        width = out_ref.shape[1]
+        c_act = act_ref[rows, width + N : width + 2 * N]
         for tile in range(width // 256):
             cols = slice(tile * 256, tile * 256 + 256)
-            outer = jnp.dot(c_ref[...], carried_ref[:, cols], preferred_element_type=F32)
+            outer = jnp.dot(c_act, carried_ref[:, cols], preferred_element_type=F32)
             scale = jnp.dot(entry, rep16_ref[:, cols], preferred_element_type=F32)
-            out_ref[:, cols] = (base_ref[:, cols].astype(F32) + scale * outer).astype(BF16)
+            out_ref[:, cols] = (base_ref[rows, cols].astype(F32) + scale * outer).astype(BF16)
 
     @pl.when(jnp.logical_not(touched))
     def _():
-        out_ref[...] = base_ref[...]
-
-
-def params():
-    return pltpu.CompilerParams(vmem_limit_bytes=VMEM, dimension_semantics=("arbitrary",))
+        out_ref[...] = base_ref[rows, :]
+
+
+def params(mib):
+    return pltpu.CompilerParams(vmem_limit_bytes=mib * MIB)
 
 
 def whole(shape):
@@ -421,6 +425,8 @@
     move = (source[None, :] - 16 == (tick - lag)[:, None]).astype(BF16)
     slot = np.broadcast_to((4 * tick + lag)[:, None], (3 * CHUNK, 128)).astype(np.int32)
     smem = pl.BlockSpec(memory_space=pltpu.SMEM)
+    resident = pl.BlockSpec(memory_space=pltpu.VMEM)
+    stream = lax.axis_index("stream").astype(jnp.int32).reshape(1)
     per_head = pl.BlockSpec((heads, BLOCK), lambda i, *_: (0, i))
     act, cum, carry, sin, pay, fin, first, meta = pl.pallas_call(
         states_kernel,
@@ -435,16 +441,15 @@
             whole(move.shape), whole(slot.shape),
         ],
         out_specs=[
-            pl.BlockSpec((BLOCK, channels), lambda i: (i, 0)),
-            per_head, per_head,
+            resident, resident, resident,
             pl.BlockSpec((BLOCK // CHUNK, N, width), lambda i: (i, 0, 0)),
             whole((PAY, width)), whole((slots, rows, N)), whole((8, width)),
             smem,
         ],
         out_shape=[
-            jax.ShapeDtypeStruct((span, channels), BF16),
-            jax.ShapeDtypeStruct((heads, span), F32),
-            jax.ShapeDtypeStruct((heads, span), F32),
+            pltpu.VMEM((span, channels), BF16),
+            pltpu.VMEM((heads, span), F32),
+            pltpu.VMEM((heads, span), F32),
             jax.ShapeDtypeStruct((chunks, N, width), BF16),
             jax.ShapeDtypeStruct((PAY, width), BF16),
             jax.ShapeDtypeStruct((slots, rows, N), BF16),
@@ -460,7 +465,7 @@
             pltpu.VMEM((1 + BLOCK // CHUNK,) + move.shape, BF16),
             pltpu.SMEM((owners,), jnp.int32),
         ],
-        compiler_params=params(),
+        compiler_params=params(18),
         cost_estimate=pl.CostEstimate(
             flops=2 * span * width * N * 2, bytes_accessed=40 << 20, transcendentals=span * channels
         ),
@@ -480,17 +485,17 @@
             grid_spec=prefetch(
                 grid=(last - first,),
                 in_specs=[
-                    pl.BlockSpec((BLOCK, channels), lambda i, *_: (first + i, 0)),
+                    resident,
                     pl.BlockSpec((heads, BLOCK), lambda i, *_: (0, first + i)),
-                    pl.BlockSpec((heads, BLOCK), lambda i, *_: (0, first + i)),
+                    resident,
                     pl.BlockSpec((BLOCK // CHUNK, N, width), lambda i, *_: (first + i, 0, 0)),
                     whole((1, width)), whole((2 * heads, width)),
-                ] + [pl.BlockSpec(memory_space=pl.ANY)] * len(hold),
-                out_specs=pl.BlockSpec((BLOCK, width), lambda i, *_: (first + i, 0)),
+                ] + [resident] * len(hold),
+                out_specs=resident,
             ),
-            out_shape=jax.ShapeDtypeStruct((span, width), BF16),
+            out_shape=pltpu.VMEM((span, width), BF16),
             input_output_aliases={7: 0} if hold else {},
-            compiler_params=params(),
+            compiler_params=params(10),
             cost_estimate=pl.CostEstimate(
                 flops=2 * (last - first) * BLOCK * width * N * 4,
                 bytes_accessed=(last - first) * (4 << 20),
@@ -510,67 +515,66 @@
         in_specs=[smem, whole((PAY, width)), whole((PAY, width))],
         out_specs=whole((PAY, side)),
         out_shape=jax.ShapeDtypeStruct((PAY, side), BF16),
-        compiler_params=pltpu.CompilerParams(vmem_limit_bytes=VMEM),
+        compiler_params=params(8),
         name="pair",
     )(shard, pay, early)
     half, fin = lax.optimization_barrier((half, fin))
-    gathered = lax.all_gather(
-        half[None], "seq", axis=0, tiled=True,
-        axis_index_groups=[list(range(0, count, 2)), list(range(1, count, 2))],
-    )
+    chips = count // 2
+    behind = [shifted(half, "seq", 2 * far) for far in range(chips - 1, 0, -1)]
     got = lax.all_to_all(
         fin.reshape(owners, CAP, rows, N), "stream", split_axis=0, concat_axis=0, tiled=True
     )
     base = outputs(1, steps - 2, base)
-    gathered, base = lax.optimization_barrier((gathered, base))
+    *behind, base = lax.optimization_barrier((*behind, base))
     mine = pl.pallas_call(
         prefix_kernel,
-        in_specs=[smem, whole(gathered.shape)],
+        in_specs=[whole((PAY, side))] * len(behind),
         out_specs=whole((N, side)),
         out_shape=jax.ShapeDtypeStruct((N, side), BF16),
-        scratch_shapes=[pltpu.VMEM((N, side), F32)],
-        compiler_params=pltpu.CompilerParams(vmem_limit_bytes=VMEM),
+        compiler_params=params(8),
         name="prefix",
-    )(shard, gathered)
+    )(*behind)
     other = lax.ppermute(mine, "seq", pairs)
     base = outputs(steps - 2, steps, base)
-    other, base = lax.optimization_barrier((other, base))
-    carried, send = pl.pallas_call(
+    other, base, got = lax.optimization_barrier((other, base, got))
+    carried, *send = pl.pallas_call(
         carry_kernel,
-        in_specs=[smem, smem, whole((N, side)), whole((N, side)), whole((PAY, width)), whole((8, width))],
-        out_specs=[whole((N, width)), whole((owners, width, N))],
-        out_shape=[
-            jax.ShapeDtypeStruct((N, width), BF16),
-            jax.ShapeDtypeStruct((owners, width, N), BF16),
-        ],
-        compiler_params=pltpu.CompilerParams(vmem_limit_bytes=VMEM),
+        in_specs=[smem, smem, smem, whole((N, side)), whole((N, side)), whole((PAY, width)), whole((8, width))],
+        out_specs=[whole((N, width))] + [whole((width, N))] * owners,
+        out_shape=[jax.ShapeDtypeStruct((N, width), BF16)]
+        + [jax.ShapeDtypeStruct((width, N), BF16)] * owners,
+        compiler_params=params(8),
         name="carry",
-    )(shard, meta, mine, other, early, first)
-    more = lax.all_to_all(send, "stream", split_axis=0, concat_axis=0, tiled=True)
+    )(shard, stream, meta, mine, other, early, first)
+    more = [send[0]]
+    for apart in range(1, owners):
+        swap = [(index, index ^ apart) for index in range(owners)]
+        more.append(lax.ppermute(send[apart], "stream", swap))
 
     out = pl.pallas_call(
         correct_kernel,
         grid_spec=prefetch(
             grid=(steps,),
             in_specs=[
-                pl.BlockSpec((BLOCK, width), lambda i, *_: (i, 0)),
-                pl.BlockSpec((BLOCK, N), lambda i, *_: (i, width // N + 1)),
-                per_head,
+                resident, resident, resident,
                 whole((N, width)), whole((2 * heads, width)),
             ],
             out_specs=pl.BlockSpec((BLOCK, width), lambda i, *_: (i, 0)),
         ),
         out_shape=jax.ShapeDtypeStruct((span, width), BF16),
-        input_output_aliases={1: 0},
-        compiler_params=params(),
+        compiler_params=params(10),
         cost_estimate=pl.CostEstimate(
             flops=2 * span * width * N, bytes_accessed=18 << 20, transcendentals=0
         ),
         name="correct",
     )(meta, base, act, carry, carried, rep16)
 
-    more = jnp.concatenate([more[:, None], jnp.zeros((owners, CAP - 1, width, N), BF16)], axis=1)
-    ssm = got[:, :, :width].astype(F32) + more.astype(F32)
+    apart = (jnp.arange(owners) ^ stream)[:, None, None]
+    extra = jnp.zeros((owners, width, N), F32)
+    for index in range(owners):
+        extra = jnp.where(apart == index, more[index][None].astype(F32), extra)
+    ranks = jnp.arange(CAP)[None, :, None, None]
+    ssm = got[:, :, :width].astype(F32) + jnp.where(ranks == 0, extra[:, None], 0.0)
     ssm = ssm.reshape(1, 1, owners, CAP, heads, P_SIZE, N)
     tiles = channels // N
     conv = got[:, :, width : width + 3 * tiles].reshape(owners, CAP, tiles, 3, N)

time: 153 us -> 150 us (0.980)
  the two profiles are of different devices: /device:TPU:0 before, /device:TPU:3 now
where the time goes in v4:
time: 150 us; the launch traced here: 149 us
  Pallas kernels  61.1 us (41%)
  local copies, waits for them, and re-layouts  55 us (37%)
  starting transfers between devices  26.7 us (18%)
  other arithmetic  4.61 us (3%)
    unnamed x52, local copies, waits for them, and re-layouts  51.8 us
    pallas_call x1, Pallas kernels, on_device(): pl.pallas_call(states_kernel, grid=(steps,), in_specs=[smem, smem, smem,...  32.9 us
    pallas_call x3, Pallas kernels, outputs(): pl.pallas_call(functools.partial(output_kernel, first, bool(hold)), grid_...  19 us
    ppermute x4, starting transfers between devices, shifted(): lax.ppermute(value, axis, [(source, source + steps) for source in range(l...  13.6 us
    pallas_call x1, Pallas kernels, on_device(): pl.pallas_call(correct_kernel, grid_spec=prefetch(grid=(steps,), in_specs...  8.21 us
    all_to_all x1, starting transfers between devices, on_device(): lax.all_to_all(fin.reshape(owners, CAP, rows, N), 'stream', split_axis=0,...  6.01 us
    add x1, other arithmetic, on_device(): got[:, :, :width].astype(F32) + jnp.where(ranks == 0, extra[:, None], 0.0)  4.1 us
    ppermute x1, starting transfers between devices, on_device(): early = lax.ppermute(pay, 'seq', pairs)  3.73 us
  transfers between devices with their start and end apart: 10, of which 1 were waited for; matrix products, arithmetic and copies ran while one was open for 2% of the time, Pallas kernels for 18%

profile of v4, /device:TPU:3, one launch (start us, length us, event | category | flops | bytes accessed | tf_op | source)
XLA Modules:
  0.0 148.6 jit_solution(6017265531621731655)
XLA Ops:
  1.4 3.8 %collective-permute-start = (bf16[16,1280]{1,0:T(8,128)(2,1)S(1)}, bf16[16,1280]{1,0:T(8,128)(2,1)S(1)}, u32[]{:S(2)}, u32[]{:S(2)}) collective-permute-start(bf16[16,1280]{1,0:T(8,128)(2,1)S(1)} %slice_bitcast_fusion), channel_id=1, source_target_pairs={{0,1},{1,2},{2,3},{3,4},{4,5},{5,6},{6,7},{8,9},{9,10},{10,11},{11... | collective-permute-start | bytes 122888 | tf_op jit(solution)/shard_map/ppermute | solution.py:30
  6.3 4.0 %copy-done.12 = bf16[1,4096,1280]{2,1,0:T(8,128)(2,1)S(1)} copy-done((bf16[1,4096,1280]{2,1,0:T(8,128)(2,1)S(1)}, bf16[1,4096,1280]{2,1,0:T(8,128)(2,1)}, u32[]{:S(2)}) %copy-start.12) | copy-done | bytes 10485784
  18.5 32.9 %states.1 = (bf16[4096,1280]{1,0:T(8,128)(2,1)S(1)}, f32[16,4096]{1,0:T(8,128)S(1)}, f32[16,4096]{1,0:T(8,128)S(1)}, bf16[32,128,1024]{2,1,0:T(8,128)(2,1)S(1)},...) custom-call(s32[1]{0:T(128)} %bitcast.shard_ref, ...), custom_call_target="tpu_custom_call" | custom-call | flops 2147483648 | bytes 41943040 | tf_op jit(solution)/shard_map/states/pallas_call | solution.py:431
  51.4 4.0 %copy-done = bf16[4096,1280]{1,0:T(8,128)(2,1)} copy-done((bf16[4096,1280]{1,0:T(8,128)(2,1)}, bf16[4096,1280]{1,0:T(8,128)(2,1)S(1)}, u32[]{:S(2)}) %copy-start) | copy-done | bytes 10485784
  55.4 3.4 %copy-done.9 = bf16[32,128,1024]{2,1,0:T(8,128)(2,1)} copy-done((bf16[32,128,1024]{2,1,0:T(8,128)(2,1)}, bf16[32,128,1024]{2,1,0:T(8,128)(2,1)S(1)}, u32[]{:S(2)}) %copy-start.9) | copy-done | bytes 8388632
  58.8 3.7 %collective-permute-start.1 = (bf16[144,1024]{1,0:T(8,128)(2,1)S(1)}, bf16[144,1024]{1,0:T(8,128)(2,1)S(1)}, u32[]{:S(2)}, u32[]{:S(2)}) collective-permute-start(bf16[144,1024]{1,0:T(8,128)(2,1)S(1)} %get-tuple-element.28.own_ref), channel_id=1, source_target_pairs={{0,1},{1,0},{2,3},{3,2},{4,5},{5,4},{6,7},{7,6},{8,9},{9,8},{10,11... | collective-permute-start | bytes 884744 | tf_op jit(solution)/shard_map/ppermute | solution.py:510
  62.7 4.0 %copy-done.1 = bf16[4096,1280]{1,0:T(8,128)(2,1)S(1)} copy-done((bf16[4096,1280]{1,0:T(8,128)(2,1)S(1)}, bf16[4096,1280]{1,0:T(8,128)(2,1)}, u32[]{:S(2)}) %copy-start.1) | copy-done | bytes 10485784
  66.7 3.4 %copy-done.10 = bf16[32,128,1024]{2,1,0:T(8,128)(2,1)S(1)} copy-done((bf16[32,128,1024]{2,1,0:T(8,128)(2,1)S(1)}, bf16[32,128,1024]{2,1,0:T(8,128)(2,1)}, u32[]{:S(2)}) %copy-start.10) | copy-done | bytes 8388632
  70.1 2.7 %outputs.3.refs_0_ = bf16[4096,1024]{1,0:T(8,128)(2,1)S(1)} custom-call(s32[16]{0:T(128)S(1)} %get-tuple-element.27.meta, bf16[4096,1280]{1,0:T(8,128)(2,1)S(1)} %copy-done.1, f32[16,4096]{1,0:T(8,128)S(1)} %bitcast.17, f32[16,4096]{1,0:T(8,128)S(1)} %get-tuple-element.30.cum_ref, bf16[32,128,1024]{2,1,0:T(8,128)(2,1)S(1)} %copy-done.10, ...), custom_call_target="tpu_custom_call" | custom-call | flops 536870912 | bytes 4194304 | tf_op jit(solution)/shard_map/outputs/pallas_call | solution.py:483
  72.8 3.3 %copy-done.5 = bf16[4096,1024]{1,0:T(8,128)(2,1)} copy-done((bf16[4096,1024]{1,0:T(8,128)(2,1)}, bf16[4096,1024]{1,0:T(8,128)(2,1)S(1)}, u32[]{:S(2)}) %copy-start.5) | copy-done | bytes 8388632
  76.1 6.0 %all-to-all-start = ((bf16[4,2,1056,128]{3,2,1,0:T(8,128)(2,1)}), bf16[4,2,1056,128]{3,2,1,0:T(8,128)(2,1)}, u32[]{:S(2)}, u32[]{:S(2)}) async-start(bf16[4,2,1056,128]{3,2,1,0:T(8,128)(2,1)} %bitcast.5), calls=%async_computation | async-start | bytes 4325376 | tf_op jit(solution)/shard_map/all_to_all | solution.py:524
  82.1 6.2 %collective-permute-start.2 = (bf16[144,512]{1,0:T(8,128)(2,1)S(1)}, bf16[144,512]{1,0:T(8,128)(2,1)S(1)}, u32[]{:S(2)}, u32[]{:S(2)}) collective-permute-start(bf16[144,512]{1,0:T(8,128)(2,1)S(1)} %pair.1), channel_id=1, source_target_pairs={{0,6},{1,7},{8,14},{9,15},{16,22},{17,23},{24,30},{25,31}} | collective-permute-start | bytes 442376 | tf_op jit(solution)/shard_map/ppermute | solution.py:30
  89.6 2.4 %collective-permute-start.4 = (bf16[144,512]{1,0:T(8,128)(2,1)S(1)}, bf16[144,512]{1,0:T(8,128)(2,1)S(1)}, u32[]{:S(2)}, u32[]{:S(2)}) collective-permute-start(bf16[144,512]{1,0:T(8,128)(2,1)S(1)} %pair.1), channel_id=1, source_target_pairs={{0,2},{1,3},{2,4},{3,5},{4,6},{5,7},{8,10},{9,11},{10,12},{11,13},... | collective-permute-start | bytes 442376 | tf_op jit(solution)/shard_map/ppermute | solution.py:30
  92.0 4.0 %copy-done.2 = bf16[4096,1280]{1,0:T(8,128)(2,1)S(1)} copy-done((bf16[4096,1280]{1,0:T(8,128)(2,1)S(1)}, bf16[4096,1280]{1,0:T(8,128)(2,1)}, u32[]{:S(2)}) %copy-start.2) | copy-done | bytes 10485784
  96.0 3.4 %copy-done.6 = bf16[4096,1024]{1,0:T(8,128)(2,1)S(1)} copy-done((bf16[4096,1024]{1,0:T(8,128)(2,1)S(1)}, bf16[4096,1024]{1,0:T(8,128)(2,1)}, u32[]{:S(2)}) %copy-start.6) | copy-done | bytes 8388632
  99.3 3.4 %copy-done.11 = bf16[32,128,1024]{2,1,0:T(8,128)(2,1)S(1)} copy-done((bf16[32,128,1024]{2,1,0:T(8,128)(2,1)S(1)}, bf16[32,128,1024]{2,1,0:T(8,128)(2,1)}, u32[]{:S(2)}) %copy-start.11) | copy-done | bytes 8388632
  102.7 11.2 %outputs.4.refs_0_ = bf16[4096,1024]{1,0:T(8,128)(2,1)S(1)} custom-call(s32[16]{0:T(128)S(1)} %get-tuple-element.27.meta, bf16[4096,1280]{1,0:T(8,128)(2,1)S(1)} %copy-done.2, f32[16,4096]{1,0:T(8,128)S(1)} %bitcast.18, f32[16,4096]{1,0:T(8,128)S(1)} %get-tuple-element.30.cum_ref, ...), custom_call_target="tpu_custom_call", output_to_operand_aliasing={{}: (7, {})} | custom-call | flops 2684354560 | bytes 20971520 | tf_op jit(solution)/shard_map/outputs/pallas_call | solution.py:483
  114.7 5.1 %outputs.5.base_ref = bf16[4096,1024]{1,0:T(8,128)(2,1)S(1)} custom-call(s32[16]{0:T(128)S(1)} %get-tuple-element.27.meta, bf16[4096,1280]{1,0:T(8,128)(2,1)S(1)} %copy-done.3, f32[16,4096]{1,0:T(8,128)S(1)} %bitcast.19, f32[16,4096]{1,0:T(8,128)S(1)} %get-tuple-element.30.cum_ref, ...), custom_call_target="tpu_custom_call", output_to_operand_aliasing={{}: (7, {})} | custom-call | flops 1073741824 | bytes 8388608 | tf_op jit(solution)/shard_map/outputs/pallas_call | solution.py:483
  119.8 3.4 %copy-done.7 = bf16[4096,1024]{1,0:T(8,128)(2,1)} copy-done((bf16[4096,1024]{1,0:T(8,128)(2,1)}, bf16[4096,1024]{1,0:T(8,128)(2,1)S(1)}, u32[]{:S(2)}) %copy-start.7) | copy-done | bytes 8388632
  124.4 2.4 %collective-permute-start.6 = (bf16[1024,128]{1,0:T(8,128)(2,1)S(1)}, bf16[1024,128]{1,0:T(8,128)(2,1)S(1)}, u32[]{:S(2)}, u32[]{:S(2)}) collective-permute-start(bf16[1024,128]{1,0:T(8,128)(2,1)S(1)} %get-tuple-element.47), channel_id=1, source_target_pairs={{0,24},{8,16},{16,8},{24,0},{1,25},{9,17},{17,9},{25,1},{2,26},{10... | collective-permute-start | bytes 786440 | tf_op jit(solution)/shard_map/ppermute | solution.py:552
  128.4 4.0 %copy-done.4 = bf16[4096,1280]{1,0:T(8,128)(2,1)S(1)} copy-done((bf16[4096,1280]{1,0:T(8,128)(2,1)S(1)}, bf16[4096,1280]{1,0:T(8,128)(2,1)}, u32[]{:S(2)}) %copy-start.4) | copy-done | bytes 10485784
  132.4 3.4 %copy-done.8 = bf16[4096,1024]{1,0:T(8,128)(2,1)S(1)} copy-done((bf16[4096,1024]{1,0:T(8,128)(2,1)S(1)}, bf16[4096,1024]{1,0:T(8,128)(2,1)}, u32[]{:S(2)}) %copy-start.8) | copy-done | bytes 8388632
  135.8 8.2 %correct.1 = bf16[4096,1024]{1,0:T(8,128)(2,1)} custom-call(s32[16]{0:T(128)S(1)} %get-tuple-element.27.meta, bf16[4096,1024]{1,0:T(8,128)(2,1)S(1)} %copy-done.8, bf16[4096,1280]{1,0:T(8,128)(2,1)S(1)} %copy-done.4, f32[16,4096]{1,0:T(8,128)S(1)} %get-tuple-element.42.carry_ref, bf16[128,1024]{1,0:T(8,128)(2,1)S(1)} %get-tuple-element.45.carried_ref, ...), custom_call_target="tpu_custom_call" | custom-call | flops 1073741824 | bytes 18874368 | tf_op jit(solution)/shard_map/correct/pallas_call | solution.py:554
  144.5 4.1 %select_add_fusion = f32[4,2,1024,128]{3,2,1,0:T(8,128)} fusion(f32[4,1024,128]{2,1,0:T(8,128)S(1)} %select_select_fusion, bf16[4,2,1056,128]{3,2,1,0:T(8,128)(2,1)} %all-to-all-done, pred[2]{0:T(512)(128)(4,1)S(1)} %iota_compare_fusion), kind=kLoop, calls=%fused_computation | loop fusion | flops 3145728 | bytes 8388610 | tf_op jit(solution)/shard_map/add | solution.py:577
  (73 shorter events, 15.6 us)
Async XLA Ops:
  1.4 4.8 %collective-permute-start = (bf16[16,1280]{1,0:T(8,128)(2,1)S(1)}, bf16[16,1280]{1,0:T(8,128)(2,1)S(1)}, u32[]{:S(2)}, u32[]{:S(2)}) collective-permute-start(bf16[16,1280]{1,0:T(8,128)(2,1)S(1)} %slice_bitcast_fusion), channel_id=1, source_target_pairs={{0,1},{1,2},{2,3},{3,4},{4,5},{5,6},{6,7},{8,9},{9,10},{10,11},{11... | collective-permute-start | bytes 122888 | tf_op jit(solution)/shard_map/ppermute | solution.py:30
  6.3 4.0 %copy-start.12 = (bf16[1,4096,1280]{2,1,0:T(8,128)(2,1)S(1)}, bf16[1,4096,1280]{2,1,0:T(8,128)(2,1)}, u32[]{:S(2)}) copy-start(bf16[1,4096,1280]{2,1,0:T(8,128)(2,1)} %param.13) | copy-start | bytes 31457284
  18.5 44.1 %copy-start.25 = (f32[16]{0:T(128)S(1)}, f32[16]{0:T(128)}, u32[]{:S(2)}) copy-start(f32[16]{0:T(128)} %param.18) | copy-start | bytes 196
  18.5 44.2 %copy-start.14 = (f32[1,16,4096]{2,1,0:T(8,128)S(1)}, f32[1,16,4096]{2,1,0:T(8,128)}, u32[]{:S(2)}) copy-start(f32[1,16,4096]{2,1,0:T(8,128)} %param.16) | copy-start | bytes 786436
  18.5 44.2 %copy-start.16 = (bf16[32,1024]{1,0:T(8,128)(2,1)S(1)}, bf16[32,1024]{1,0:T(8,128)(2,1)}, u32[]{:S(2)}) copy-start(bf16[32,1024]{1,0:T(8,128)(2,1)} %constant.31.clone.rep16_ref) | copy-start | bytes 196612
  51.4 4.0 %copy-start = (bf16[4096,1280]{1,0:T(8,128)(2,1)}, bf16[4096,1280]{1,0:T(8,128)(2,1)S(1)}, u32[]{:S(2)}) copy-start(bf16[4096,1280]{1,0:T(8,128)(2,1)S(1)} %get-tuple-element.29.act_ref) | copy-start | bytes 31457284
  55.4 3.4 %copy-start.9 = (bf16[32,128,1024]{2,1,0:T(8,128)(2,1)}, bf16[32,128,1024]{2,1,0:T(8,128)(2,1)S(1)}, u32[]{:S(2)}) copy-start(bf16[32,128,1024]{2,1,0:T(8,128)(2,1)S(1)} %get-tuple-element.31.sin_ref) | copy-start | bytes 25165828
  58.8 17.2 %collective-permute-start.1 = (bf16[144,1024]{1,0:T(8,128)(2,1)S(1)}, bf16[144,1024]{1,0:T(8,128)(2,1)S(1)}, u32[]{:S(2)}, u32[]{:S(2)}) collective-permute-start(bf16[144,1024]{1,0:T(8,128)(2,1)S(1)} %get-tuple-element.28.own_ref), channel_id=1, source_target_pairs={{0,1},{1,0},{2,3},{3,2},{4,5},{5,4},{6,7},{7,6},{8,9},{9,8},{10,11... | collective-permute-start | bytes 884744 | tf_op jit(solution)/shard_map/ppermute | solution.py:510
  62.7 4.0 %copy-start.1 = (bf16[4096,1280]{1,0:T(8,128)(2,1)S(1)}, bf16[4096,1280]{1,0:T(8,128)(2,1)}, u32[]{:S(2)}) copy-start(bf16[4096,1280]{1,0:T(8,128)(2,1)} %copy-done) | copy-start | bytes 31457284
  66.7 3.4 %copy-start.10 = (bf16[32,128,1024]{2,1,0:T(8,128)(2,1)S(1)}, bf16[32,128,1024]{2,1,0:T(8,128)(2,1)}, u32[]{:S(2)}) copy-start(bf16[32,128,1024]{2,1,0:T(8,128)(2,1)} %copy-done.9) | copy-start | bytes 25165828
  76.1 47.1 %all-to-all-start = ((bf16[4,2,1056,128]{3,2,1,0:T(8,128)(2,1)}), bf16[4,2,1056,128]{3,2,1,0:T(8,128)(2,1)}, u32[]{:S(2)}, u32[]{:S(2)}) async-start(bf16[4,2,1056,128]{3,2,1,0:T(8,128)(2,1)} %bitcast.5), calls=%async_computation | async-start | bytes 4325376 | tf_op jit(solution)/shard_map/all_to_all | solution.py:524
  82.1 31.9 %collective-permute-start.2 = (bf16[144,512]{1,0:T(8,128)(2,1)S(1)}, bf16[144,512]{1,0:T(8,128)(2,1)S(1)}, u32[]{:S(2)}, u32[]{:S(2)}) collective-permute-start(bf16[144,512]{1,0:T(8,128)(2,1)S(1)} %pair.1), channel_id=1, source_target_pairs={{0,6},{1,7},{8,14},{9,15},{16,22},{17,23},{24,30},{25,31}} | collective-permute-start | bytes 442376 | tf_op jit(solution)/shard_map/ppermute | solution.py:30
  88.3 25.7 %collective-permute-start.3 = (bf16[144,512]{1,0:T(8,128)(2,1)S(1)}, bf16[144,512]{1,0:T(8,128)(2,1)S(1)}, u32[]{:S(2)}, u32[]{:S(2)}) collective-permute-start(bf16[144,512]{1,0:T(8,128)(2,1)S(1)} %pair.1), channel_id=1, source_target_pairs={{0,4},{1,5},{2,6},{3,7},{8,12},{9,13},{10,14},{11,15},{16,20},{17,... | collective-permute-start | bytes 442376 | tf_op jit(solution)/shard_map/ppermute | solution.py:30
  89.6 24.4 %collective-permute-start.4 = (bf16[144,512]{1,0:T(8,128)(2,1)S(1)}, bf16[144,512]{1,0:T(8,128)(2,1)S(1)}, u32[]{:S(2)}, u32[]{:S(2)}) collective-permute-start(bf16[144,512]{1,0:T(8,128)(2,1)S(1)} %pair.1), channel_id=1, source_target_pairs={{0,2},{1,3},{2,4},{3,5},{4,6},{5,7},{8,10},{9,11},{10,12},{11,13},... | collective-permute-start | bytes 442376 | tf_op jit(solution)/shard_map/ppermute | solution.py:30
  92.0 4.0 %copy-start.2 = (bf16[4096,1280]{1,0:T(8,128)(2,1)S(1)}, bf16[4096,1280]{1,0:T(8,128)(2,1)}, u32[]{:S(2)}) copy-start(bf16[4096,1280]{1,0:T(8,128)(2,1)} %copy-done) | copy-start | bytes 31457284
  96.0 3.4 %copy-start.6 = (bf16[4096,1024]{1,0:T(8,128)(2,1)S(1)}, bf16[4096,1024]{1,0:T(8,128)(2,1)}, u32[]{:S(2)}) copy-start(bf16[4096,1024]{1,0:T(8,128)(2,1)} %copy-done.5) | copy-start | bytes 25165828
  99.3 3.4 %copy-start.11 = (bf16[32,128,1024]{2,1,0:T(8,128)(2,1)S(1)}, bf16[32,128,1024]{2,1,0:T(8,128)(2,1)}, u32[]{:S(2)}) copy-start(bf16[32,128,1024]{2,1,0:T(8,128)(2,1)} %copy-done.9) | copy-start | bytes 25165828
  102.7 12.0 %copy-start.3 = (bf16[4096,1280]{1,0:T(8,128)(2,1)S(1)}, bf16[4096,1280]{1,0:T(8,128)(2,1)}, u32[]{:S(2)}) copy-start(bf16[4096,1280]{1,0:T(8,128)(2,1)} %copy-done) | copy-start | bytes 31457284
  114.1 9.1 %collective-permute-start.5 = (bf16[128,512]{1,0:T(8,128)(2,1)S(1)}, bf16[128,512]{1,0:T(8,128)(2,1)S(1)}, u32[]{:S(2)}, u32[]{:S(2)}) collective-permute-start(bf16[128,512]{1,0:T(8,128)(2,1)S(1)} %prefix.1.mine_ref), channel_id=1, source_target_pairs={{0,1},{1,0},{2,3},{3,2},{4,5},{5,4},{6,7},{7,6},{8,9},{9,8},{10,11... | collective-permute-start | bytes 393224 | tf_op jit(solution)/shard_map/ppermute | solution.py:537
  119.8 3.4 %copy-start.7 = (bf16[4096,1024]{1,0:T(8,128)(2,1)}, bf16[4096,1024]{1,0:T(8,128)(2,1)S(1)}, u32[]{:S(2)}) copy-start(bf16[4096,1024]{1,0:T(8,128)(2,1)S(1)} %outputs.5.base_ref) | copy-start | bytes 25165828
  124.1 19.9 %collective-permute-start.8 = (bf16[1024,128]{1,0:T(8,128)(2,1)S(1)}, bf16[1024,128]{1,0:T(8,128)(2,1)S(1)}, u32[]{:S(2)}, u32[]{:S(2)}) collective-permute-start(bf16[1024,128]{1,0:T(8,128)(2,1)S(1)} %get-tuple-element.49), channel_id=1, source_target_pairs={{0,8},{8,0},{16,24},{24,16},{1,9},{9,1},{17,25},{25,17},{2,10},{10... | collective-permute-start | bytes 786440 | tf_op jit(solution)/shard_map/ppermute | solution.py:552
  124.1 19.9 %collective-permute-start.7 = (bf16[1024,128]{1,0:T(8,128)(2,1)S(1)}, bf16[1024,128]{1,0:T(8,128)(2,1)S(1)}, u32[]{:S(2)}, u32[]{:S(2)}) collective-permute-start(bf16[1024,128]{1,0:T(8,128)(2,1)S(1)} %get-tuple-element.48), channel_id=1, source_target_pairs={{0,16},{8,24},{16,0},{24,8},{1,17},{9,25},{17,1},{25,9},{2,18},{10... | collective-permute-start | bytes 786440 | tf_op jit(solution)/shard_map/ppermute | solution.py:552
  124.4 19.7 %collective-permute-start.6 = (bf16[1024,128]{1,0:T(8,128)(2,1)S(1)}, bf16[1024,128]{1,0:T(8,128)(2,1)S(1)}, u32[]{:S(2)}, u32[]{:S(2)}) collective-permute-start(bf16[1024,128]{1,0:T(8,128)(2,1)S(1)} %get-tuple-element.47), channel_id=1, source_target_pairs={{0,24},{8,16},{16,8},{24,0},{1,25},{9,17},{17,9},{25,1},{2,26},{10... | collective-permute-start | bytes 786440 | tf_op jit(solution)/shard_map/ppermute | solution.py:552
  128.4 4.0 %copy-start.4 = (bf16[4096,1280]{1,0:T(8,128)(2,1)S(1)}, bf16[4096,1280]{1,0:T(8,128)(2,1)}, u32[]{:S(2)}) copy-start(bf16[4096,1280]{1,0:T(8,128)(2,1)} %copy-done) | copy-start | bytes 31457284
  (12 other events, 14.9 us)

commit v5 on v3

--- a/solution.py
+++ b/solution.py
@@ -18,7 +18,7 @@
 LOG2E = 1.4426950408889634
 PAY = 144
 TAIL = 32
-VMEM = 56 * 1024 * 1024
+MIB = 1024 * 1024
 
 F32 = jnp.float32
 BF16 = jnp.bfloat16
@@ -106,29 +106,106 @@
     meta[0] = start - anchor
 
 
-def conv_rows(x_ref, edge16, moves, weights, act_ref, part, choice):
-    low = part * CHUNK
-    rows = slice(low, low + CHUNK)
-    pick = moves[choice]
-    for tile in range(x_ref.shape[1] // 256):
-        cols = slice(tile * 256, tile * 256 + 256)
-        if part:
-            wide = x_ref[low - 16 : low + CHUNK, cols]
-        else:
-            wide = jnp.concatenate([edge16[:, cols], x_ref[rows, cols]], axis=0)
-        moved = jnp.dot(pick, wide, preferred_element_type=F32)
-        moved = moved.reshape(CHUNK // 8, 3, 8, 256)
-        mixed = weights[4:5, cols] + weights[0:1, cols] * x_ref[rows, cols].astype(F32)
-        for lag in range(1, 4):
-            mixed = mixed + weights[lag : lag + 1, cols] * moved[:, lag - 1].reshape(CHUNK, 256)
-        act_ref[rows, cols] = (mixed + mixed * jnp.tanh(mixed)).astype(BF16)
+def conv_kernel(
+    shard_ref, bounds, owners, x_ref, rim_ref, w_ref, bias_ref, move_ref, slot_ref,
+    act_ref, tail_ref, meta,
+    edge16, weights, moves, count,
+):
+    step = pl.program_id(0)
+    span = pl.num_programs(0) * BLOCK
+    parts = BLOCK // CHUNK
+    first = step * BLOCK
+
+    @pl.when(step == 0)
+    def _():
+        read_docs(bounds, owners, meta, count, shard_ref[0] * span, span)
+        tail_ref[...] = jnp.zeros_like(tail_ref)
+        edge16[...] = rim_ref[...]
+        weights[0:4] = 0.5 * w_ref[...]
+        weights[4:5] = 0.5 * bias_ref[...]
+        moves[0] = move_ref[...]
+
+    choices = []
+    for part in range(parts):
+        begin = first + part * CHUNK
+        near = (meta[0] > begin - 3) & (meta[0] < begin + CHUNK)
+        for slot in range(EMAX):
+            near = near | ((meta[1 + slot] > begin - 3) & (meta[1 + slot] < begin + CHUNK))
+
+        @pl.when(near)
+        def _():
+            tick = slot_ref[...] // 4 + begin
+            kept = (tick - starts_of(meta, tick) >= slot_ref[...] % 4).astype(F32)
+            moves[1 + part, :, :128] = (kept * move_ref[:, :128].astype(F32)).astype(BF16)
+            moves[1 + part, :, 128:] = (kept[:, :16] * move_ref[:, 128:].astype(F32)).astype(BF16)
+
+        choices.append(jnp.where(near, 1 + part, 0))
+
+    for part in range(parts):
+        low = part * CHUNK
+        rows = slice(low, low + CHUNK)
+        pick = moves[choices[part]]
+        for tile in range(x_ref.shape[1] // 256):
+            cols = slice(tile * 256, tile * 256 + 256)
+            if part:
+                wide = x_ref[low - 16 : low + CHUNK, cols]
+            else:
+                wide = jnp.concatenate([edge16[:, cols], x_ref[rows, cols]], axis=0)
+            moved = jnp.dot(pick, wide, preferred_element_type=F32)
+            moved = moved.reshape(CHUNK // 8, 3, 8, 256)
+            mixed = weights[4:5, cols] + weights[0:1, cols] * x_ref[rows, cols].astype(F32)
+            for lag in range(1, 4):
+                mixed = mixed + weights[lag : lag + 1, cols] * moved[:, lag - 1].reshape(CHUNK, 256)
+            act_ref[rows, cols] = (mixed + mixed * jnp.tanh(mixed)).astype(BF16)
+
+    def finish(slot, _):
+        end = meta[1 + slot]
+        start = jnp.where(slot > 0, meta[jnp.maximum(slot, 1)], meta[0])
+        low = pl.multiple_of((end - 1 - first) // CHUNK * CHUNK, CHUNK)
+        begin = first + low
+        target = meta[5 + slot]
+        tail = jnp.zeros((TAIL, 128), F32)
+        row = iota((TAIL, CHUNK), 0)
+        col = iota((TAIL, CHUNK), 1) + begin
+        row16 = iota((TAIL, 16), 0)
+        col16 = iota((TAIL, 16), 1) + begin - 16
+        before = pl.multiple_of(jnp.maximum(low - 16, 0), 16)
+        for tile in range(x_ref.shape[1] // 128):
+            cols = slice(tile * 128, tile * 128 + 128)
+            mine = (row >= 3 * tile) & (row < 3 * tile + 3)
+            pick = (col == end - 3 + row - 3 * tile) & (col >= start) & mine
+            mine16 = (row16 >= 3 * tile) & (row16 < 3 * tile + 3)
+            pick16 = (col16 == end - 3 + row16 - 3 * tile) & (col16 >= start) & mine16
+            rim = jnp.where(low > 0, x_ref[pl.ds(before, 16), cols].astype(F32), edge16[:, cols].astype(F32))
+            tail = tail + jnp.dot(
+                pick.astype(F32).astype(BF16), x_ref[pl.ds(low, CHUNK), cols], preferred_element_type=F32
+            ) + jnp.dot(
+                pick16.astype(F32).astype(BF16), rim.astype(BF16), preferred_element_type=F32
+            )
+
+        @pl.when(target >= 0)
+        def _():
+            tail_ref[target] = tail.astype(BF16)
+
+        return 0
+
+    lax.fori_loop(*ended(meta, first), finish, 0)
+    edge16[...] = x_ref[BLOCK - 16 :, :]
+
+
+def ended(meta, first):
+    done = jnp.int32(0)
+    upto = jnp.int32(0)
+    for slot in range(EMAX):
+        done = done + (meta[1 + slot] <= first).astype(jnp.int32)
+        upto = upto + (meta[1 + slot] <= first + BLOCK).astype(jnp.int32)
+    return done, upto
 
 
 def states_kernel(
-    shard_ref, bounds, owners, x_ref, rim_ref, dt_ref, ld_ref, w_ref, bias_ref,
-    rep_ref, rep16_ref, tri_ref, move_ref, slot_ref,
-    act_ref, cum_ref, carry_ref, sin_ref, pay_ref, fin_ref, first_ref, meta,
-    state, edge16, total, totals, weights, moves, count,
+    meta, act_ref, dt_ref, ld_ref, rep_ref, rep16_ref, tri_ref, tail_ref,
+    cum_ref, carry_ref, sin_ref, pay_ref, fin_ref, first_ref,
+    state, total, totals,
 ):
     step = pl.program_id(0)
     heads = dt_ref.shape[0]
@@ -139,40 +216,17 @@
 
     @pl.when(step == 0)
     def _():
-        read_docs(bounds, owners, meta, count, shard_ref[0] * span, span)
         state[...] = jnp.zeros_like(state)
         total[...] = jnp.zeros_like(total)
-        fin_ref[...] = jnp.zeros_like(fin_ref)
+        fin_ref[:, :width] = jnp.zeros_like(fin_ref[:, :width])
+        fin_ref[:, width:] = tail_ref[...]
         first_ref[...] = jnp.zeros_like(first_ref)
-        edge16[...] = rim_ref[...]
-        weights[0:4] = 0.5 * w_ref[...]
-        weights[4:5] = 0.5 * bias_ref[...]
-        moves[0] = move_ref[...]
-
-    choices = []
-    for part in range(parts):
-        begin = first + part * CHUNK
-        near = (meta[0] > begin - 3) & (meta[0] < begin + CHUNK)
-        for slot in range(EMAX):
-            near = near | ((meta[1 + slot] > begin - 3) & (meta[1 + slot] < begin + CHUNK))
-
-        @pl.when(near)
-        def _():
-            tick = slot_ref[...] // 4 + begin
-            kept = (tick - starts_of(meta, tick) >= slot_ref[...] % 4).astype(F32)
-            moves[1 + part, :, :128] = (kept * move_ref[:, :128].astype(F32)).astype(BF16)
-            moves[1 + part, :, 128:] = (kept[:, :16] * move_ref[:, 128:].astype(F32)).astype(BF16)
-
-        choices.append(jnp.where(near, 1 + part, 0))
-
-    conv_rows(x_ref, edge16, moves, weights, act_ref, 0, choices[0])
+
     running = total[...]
     for part in range(parts):
         low = part * CHUNK
         rows = slice(low, low + CHUNK)
         begin = first + low
-        if part + 1 < parts:
-            conv_rows(x_ref, edge16, moves, weights, act_ref, part + 1, choices[part + 1])
         summed = jnp.dot(
             thirds(ld_ref[:, rows] * LOG2E), tri_ref[...], preferred_element_type=F32
         )
@@ -223,48 +277,22 @@
         def _():
             first_ref[...] = jnp.broadcast_to(spread_row(opened, rep_ref[...]), first_ref.shape)
 
-        tail = jnp.zeros((TAIL, 128), F32)
-        row = iota((TAIL, CHUNK), 0)
-        col = iota((TAIL, CHUNK), 1) + begin
-        row16 = iota((TAIL, 16), 0)
-        col16 = iota((TAIL, 16), 1) + begin - 16
-        before = pl.multiple_of(jnp.maximum(low - 16, 0), 16)
-        for tile in range(x_ref.shape[1] // 128):
-            cols = slice(tile * 128, tile * 128 + 128)
-            mine = (row >= 3 * tile) & (row < 3 * tile + 3)
-            pick = (col == end - 3 + row - 3 * tile) & (col >= start) & mine
-            mine16 = (row16 >= 3 * tile) & (row16 < 3 * tile + 3)
-            pick16 = (col16 == end - 3 + row16 - 3 * tile) & (col16 >= start) & mine16
-            rim = jnp.where(low > 0, x_ref[pl.ds(before, 16), cols].astype(F32), edge16[:, cols].astype(F32))
-            tail = tail + jnp.dot(
-                pick.astype(F32).astype(BF16), x_ref[pl.ds(low, CHUNK), cols], preferred_element_type=F32
-            ) + jnp.dot(
-                pick16.astype(F32).astype(BF16), rim.astype(BF16), preferred_element_type=F32
-            )
-
         @pl.when(target >= 0)
         def _():
             fin_ref[target, :width] = final.T.astype(BF16)
-            fin_ref[target, width : width + TAIL] = tail.astype(BF16)
 
         return 0
 
-    done = jnp.int32(0)
-    upto = jnp.int32(0)
-    for slot in range(EMAX):
-        done = done + (meta[1 + slot] <= first).astype(jnp.int32)
-        upto = upto + (meta[1 + slot] <= first + BLOCK).astype(jnp.int32)
-    lax.fori_loop(done, upto, finish, 0)
-    edge16[...] = x_ref[BLOCK - 16 :, :]
+    lax.fori_loop(*ended(meta, first), finish, 0)
 
     @pl.when(step == pl.num_programs(0) - 1)
     def _():
         start = last_start(meta, span - 1)
         gate = spread_row(jnp.where(start < 0, jnp.exp2(total[:, :1]), 0.0), rep_ref[...])
-        gate = jnp.broadcast_to(gate, (16, width))
+        gate = jnp.broadcast_to(gate, (PAY - N, width))
         high = gate.astype(BF16).astype(F32)
         pay_ref[:N] = state[...].astype(BF16)
-        pay_ref[N:] = jnp.where(iota((16, width), 0) == 0, high, gate - high).astype(BF16)
+        pay_ref[N:] = jnp.where(iota((PAY - N, width), 0) == 0, high, gate - high).astype(BF16)
 
 
 def output_kernel(origin, held, meta, act_ref, dt_ref, cum_ref, sin_ref, gain_ref, rep16_ref, *refs):
@@ -272,10 +300,10 @@
     step = origin + pl.program_id(0)
     heads = dt_ref.shape[0]
     width = out_ref.shape[1]
-    for part in range(BLOCK // CHUNK):
-        low = part * CHUNK
-        rows = slice(low, low + CHUNK)
-        begin = step * BLOCK + low
+    parts = BLOCK // CHUNK
+    for part in range(parts):
+        begin = step * BLOCK + part * CHUNK
+        rows = slice(part * CHUNK, part * CHUNK + CHUNK)
         cum = cum_ref[:, rows]
         back = cum - jnp.log2(dt_ref[:, rows])
         ahead = cum.T
@@ -337,19 +365,16 @@
         join(got_ref, own_ref, slice(side, 2 * side))
 
 
-def prefix_kernel(shard_ref, gathered, prefix_ref, held):
-    held[...] = jnp.zeros_like(held)
-
-    def one(index, _):
-        gates = gathered[index, N:].astype(F32)
-        held[...] = (gates[0:1] + gates[1:2]) * held[...] + gathered[index, :N].astype(F32)
-        return 0
-
-    lax.fori_loop(0, shard_ref[0] // 2, one, 0)
-    prefix_ref[...] = held[...].astype(BF16)
-
-
-def carry_kernel(shard_ref, meta, mine_ref, other_ref, early_ref, first_ref, carried_ref, send_ref):
+def prefix_kernel(*refs):
+    prefix_ref = refs[-1]
+    side = prefix_ref.shape[1]
+    total = jnp.zeros((N, side), F32)
+    for ref in refs[:-1]:
+        total = gates_of(ref, slice(0, side)) * total + ref[:N].astype(F32)
+    prefix_ref[...] = total.astype(BF16)
+
+
+def carry_kernel(shard_ref, stream_ref, meta, mine_ref, other_ref, early_ref, first_ref, carried_ref, *sends):
     side = mine_ref.shape[1]
     lower, upper = slice(0, side), slice(side, 2 * side)
 
@@ -365,19 +390,20 @@
                 early_ref[:N, cols].astype(F32) + gates_of(early_ref, cols) * part[...].astype(F32)
             ).astype(BF16)
 
-    send_ref[...] = jnp.zeros_like(send_ref)
-    send_ref[meta[5] // CAP] = (first_ref[0:1] * carried_ref[...].astype(F32)).T.astype(BF16)
+    value = (first_ref[0:1] * carried_ref[...].astype(F32)).T.astype(BF16)
+    apart = (meta[5] // CAP) ^ stream_ref[0]
+    for index, ref in enumerate(sends):
+        ref[...] = jnp.where(apart == index, value, jnp.zeros_like(value))
 
 
 def correct_kernel(meta, base_ref, c_ref, carry_ref, carried_ref, rep16_ref, out_ref):
-    step = pl.program_id(0)
-    touched = (meta[0] < 0) & (meta[1] > step * BLOCK)
+    width = out_ref.shape[1]
+    touched = (meta[0] < 0) & (meta[1] > pl.program_id(0) * BLOCK)
 
     @pl.when(touched)
     def _():
         entry = carry_ref[...]
         entry = jnp.concatenate([entry, entry - entry.astype(BF16).astype(F32)], axis=0).T.astype(BF16)
-        width = out_ref.shape[1]
         for tile in range(width // 256):
             cols = slice(tile * 256, tile * 256 + 256)
             outer = jnp.dot(c_ref[...], carried_ref[:, cols], preferred_element_type=F32)
@@ -389,8 +415,8 @@
         out_ref[...] = base_ref[...]
 
 
-def params():
-    return pltpu.CompilerParams(vmem_limit_bytes=VMEM, dimension_semantics=("arbitrary",))
+def params(mib):
+    return pltpu.CompilerParams(vmem_limit_bytes=mib * MIB)
 
 
 def whole(shape):
@@ -421,57 +447,71 @@
     move = (source[None, :] - 16 == (tick - lag)[:, None]).astype(BF16)
     slot = np.broadcast_to((4 * tick + lag)[:, None], (3 * CHUNK, 128)).astype(np.int32)
     smem = pl.BlockSpec(memory_space=pltpu.SMEM)
+    stream = lax.axis_index("stream").astype(jnp.int32).reshape(1)
     per_head = pl.BlockSpec((heads, BLOCK), lambda i, *_: (0, i))
-    act, cum, carry, sin, pay, fin, first, meta = pl.pallas_call(
-        states_kernel,
+    prefetch = functools.partial(pltpu.PrefetchScalarGridSpec, num_scalar_prefetch=1)
+    by_rows = pl.BlockSpec((BLOCK, channels), lambda i, *_: (i, 0))
+    act, tails, meta = pl.pallas_call(
+        conv_kernel,
         grid=(steps,),
         in_specs=[
-            smem, smem, smem,
-            pl.BlockSpec((BLOCK, channels), lambda i: (i, 0)),
-            whole((16, channels)),
-            per_head, per_head,
-            whole((4, channels)), whole((1, channels)),
-            whole((heads, width)), whole((2 * heads, width)), whole((CHUNK, CHUNK)),
-            whole(move.shape), whole(slot.shape),
+            smem, smem, smem, by_rows, whole((16, channels)),
+            whole((4, channels)), whole((1, channels)), whole(move.shape), whole(slot.shape),
         ],
-        out_specs=[
-            pl.BlockSpec((BLOCK, channels), lambda i: (i, 0)),
-            per_head, per_head,
-            pl.BlockSpec((BLOCK // CHUNK, N, width), lambda i: (i, 0, 0)),
-            whole((PAY, width)), whole((slots, rows, N)), whole((8, width)),
-            smem,
-        ],
+        out_specs=[by_rows, whole((slots, TAIL, N)), smem],
         out_shape=[
             jax.ShapeDtypeStruct((span, channels), BF16),
+            jax.ShapeDtypeStruct((slots, TAIL, N), BF16),
+            jax.ShapeDtypeStruct((16,), jnp.int32),
+        ],
+        scratch_shapes=[
+            pltpu.VMEM((16, channels), BF16),
+            pltpu.VMEM((8, channels), F32),
+            pltpu.VMEM((1 + BLOCK // CHUNK,) + move.shape, BF16),
+            pltpu.SMEM((owners,), jnp.int32),
+        ],
+        compiler_params=params(48),
+        cost_estimate=pl.CostEstimate(
+            flops=2 * span * channels * 400, bytes_accessed=21 << 20, transcendentals=span * channels
+        ),
+        name="conv",
+    )(shard, doc_bounds, doc_owner, rows_in, rim, conv_weight, conv_bias[None], move, slot)
+    cum, carry, sin, pay, fin, first = pl.pallas_call(
+        states_kernel,
+        grid_spec=prefetch(
+            grid=(steps,),
+            in_specs=[
+                by_rows, per_head, per_head,
+                whole((heads, width)), whole((2 * heads, width)), whole((CHUNK, CHUNK)),
+                whole((slots, TAIL, N)),
+            ],
+            out_specs=[
+                per_head, per_head,
+                pl.BlockSpec((BLOCK // CHUNK, N, width), lambda i, *_: (i, 0, 0)),
+                whole((PAY, width)), whole((slots, rows, N)), whole((8, width)),
+            ],
+            scratch_shapes=[
+                pltpu.VMEM((N, width), F32),
+                pltpu.VMEM((heads, CHUNK), F32),
+                pltpu.VMEM((BLOCK // CHUNK, heads, CHUNK), F32),
+            ],
+        ),
+        out_shape=[
             jax.ShapeDtypeStruct((heads, span), F32),
             jax.ShapeDtypeStruct((heads, span), F32),
             jax.ShapeDtypeStruct((chunks, N, width), BF16),
             jax.ShapeDtypeStruct((PAY, width), BF16),
             jax.ShapeDtypeStruct((slots, rows, N), BF16),
             jax.ShapeDtypeStruct((8, width), F32),
-            jax.ShapeDtypeStruct((16,), jnp.int32),
         ],
-        scratch_shapes=[
-            pltpu.VMEM((N, width), F32),
-            pltpu.VMEM((16, channels), BF16),
-            pltpu.VMEM((heads, CHUNK), F32),
-            pltpu.VMEM((BLOCK // CHUNK, heads, CHUNK), F32),
-            pltpu.VMEM((8, channels), F32),
-            pltpu.VMEM((1 + BLOCK // CHUNK,) + move.shape, BF16),
-            pltpu.SMEM((owners,), jnp.int32),
-        ],
-        compiler_params=params(),
+        compiler_params=params(48),
         cost_estimate=pl.CostEstimate(
-            flops=2 * span * width * N * 2, bytes_accessed=40 << 20, transcendentals=span * channels
+            flops=2 * span * width * N * 2, bytes_accessed=22 << 20, transcendentals=span * heads
         ),
         name="states",
-    )(
-        shard, doc_bounds, doc_owner, rows_in, rim, step_size[0], log_decay[0],
-        conv_weight, conv_bias[None], rep, rep16, tri, move, slot,
-    )
+    )(meta, act, step_size[0], log_decay[0], rep, rep16, tri, tails)
 
     gain = jnp.repeat(skip_gain, P_SIZE)[None]
-    prefetch = functools.partial(pltpu.PrefetchScalarGridSpec, num_scalar_prefetch=1)
 
     def outputs(first, last, base):
         hold = [] if base is None else [base]
@@ -490,7 +530,7 @@
             ),
             out_shape=jax.ShapeDtypeStruct((span, width), BF16),
             input_output_aliases={7: 0} if hold else {},
-            compiler_params=params(),
+            compiler_params=params(48),
             cost_estimate=pl.CostEstimate(
                 flops=2 * (last - first) * BLOCK * width * N * 4,
                 bytes_accessed=(last - first) * (4 << 20),
@@ -510,43 +550,41 @@
         in_specs=[smem, whole((PAY, width)), whole((PAY, width))],
         out_specs=whole((PAY, side)),
         out_shape=jax.ShapeDtypeStruct((PAY, side), BF16),
-        compiler_params=pltpu.CompilerParams(vmem_limit_bytes=VMEM),
+        compiler_params=params(48),
         name="pair",
     )(shard, pay, early)
     half, fin = lax.optimization_barrier((half, fin))
-    gathered = lax.all_gather(
-        half[None], "seq", axis=0, tiled=True,
-        axis_index_groups=[list(range(0, count, 2)), list(range(1, count, 2))],
-    )
+    chips = count // 2
+    behind = [shifted(half, "seq", 2 * far) for far in range(chips - 1, 0, -1)]
     got = lax.all_to_all(
         fin.reshape(owners, CAP, rows, N), "stream", split_axis=0, concat_axis=0, tiled=True
     )
     base = outputs(1, steps - 2, base)
-    gathered, base = lax.optimization_barrier((gathered, base))
+    *behind, base = lax.optimization_barrier((*behind, base))
     mine = pl.pallas_call(
         prefix_kernel,
-        in_specs=[smem, whole(gathered.shape)],
+        in_specs=[whole((PAY, side))] * len(behind),
         out_specs=whole((N, side)),
         out_shape=jax.ShapeDtypeStruct((N, side), BF16),
-        scratch_shapes=[pltpu.VMEM((N, side), F32)],
-        compiler_params=pltpu.CompilerParams(vmem_limit_bytes=VMEM),
+        compiler_params=params(48),
         name="prefix",
-    )(shard, gathered)
+    )(*behind)
     other = lax.ppermute(mine, "seq", pairs)
     base = outputs(steps - 2, steps, base)
-    other, base = lax.optimization_barrier((other, base))
-    carried, send = pl.pallas_call(
+    other, base, got = lax.optimization_barrier((other, base, got))
+    carried, *send = pl.pallas_call(
         carry_kernel,
-        in_specs=[smem, smem, whole((N, side)), whole((N, side)), whole((PAY, width)), whole((8, width))],
-        out_specs=[whole((N, width)), whole((owners, width, N))],
-        out_shape=[
-            jax.ShapeDtypeStruct((N, width), BF16),
-            jax.ShapeDtypeStruct((owners, width, N), BF16),
-        ],
-        compiler_params=pltpu.CompilerParams(vmem_limit_bytes=VMEM),
+        in_specs=[smem, smem, smem, whole((N, side)), whole((N, side)), whole((PAY, width)), whole((8, width))],
+        out_specs=[whole((N, width))] + [whole((width, N))] * owners,
+        out_shape=[jax.ShapeDtypeStruct((N, width), BF16)]
+        + [jax.ShapeDtypeStruct((width, N), BF16)] * owners,
+        compiler_params=params(48),
         name="carry",
-    )(shard, meta, mine, other, early, first)
-    more = lax.all_to_all(send, "stream", split_axis=0, concat_axis=0, tiled=True)
+    )(shard, stream, meta, mine, other, early, first)
+    more = [send[0]]
+    for apart in range(1, owners):
+        swap = [(index, index ^ apart) for index in range(owners)]
+        more.append(lax.ppermute(send[apart], "stream", swap))
 
     out = pl.pallas_call(
         correct_kernel,
@@ -562,15 +600,19 @@
         ),
         out_shape=jax.ShapeDtypeStruct((span, width), BF16),
         input_output_aliases={1: 0},
-        compiler_params=params(),
+        compiler_params=params(48),
         cost_estimate=pl.CostEstimate(
             flops=2 * span * width * N, bytes_accessed=18 << 20, transcendentals=0
         ),
         name="correct",
     )(meta, base, act, carry, carried, rep16)
 
-    more = jnp.concatenate([more[:, None], jnp.zeros((owners, CAP - 1, width, N), BF16)], axis=1)
-    ssm = got[:, :, :width].astype(F32) + more.astype(F32)
+    apart = (jnp.arange(owners) ^ stream)[:, None, None]
+    extra = jnp.zeros((owners, width, N), F32)
+    for index in range(owners):
+        extra = jnp.where(apart == index, more[index][None].astype(F32), extra)
+    ranks = jnp.arange(CAP)[None, :, None, None]
+    ssm = got[:, :, :width].astype(F32) + jnp.where(ranks == 0, extra[:, None], 0.0)
     ssm = ssm.reshape(1, 1, owners, CAP, heads, P_SIZE, N)
     tiles = channels // N
     conv = got[:, :, width : width + 3 * tiles].reshape(owners, CAP, tiles, 3, N)

time: 153 us -> 115 us (0.75); the launches traced: 153 us -> 113 us
  blocking collectives: 40.1 us -> 0 us
  starting transfers between devices: 6.04 us -> 20.3 us
  waiting for transfers between devices: 14.6 us -> 1.46 us
  other arithmetic: 0.28 us -> 4.61 us
  Pallas kernels: 83.2 us -> 78.9 us
    all_to_all x1 -> x0, blocking collectives: 22.3 us -> none  [on_device(): lax.all_to_all(send, 'stream', split_axis=0, concat_axis=0, tiled=True)]
    all_gather x1 -> x0, blocking collectives: 17.8 us -> none  [on_device(): lax.all_gather(half[None], 'seq', axis=0, tiled=True, axis_index_groups=[...]
    all_to_all x1, waiting for transfers between devices: 14.6 us -> 0.01 us  [on_device(): lax.all_to_all(fin.reshape(owners, CAP, rows, N), 'stream', split_axis=0,...]
    ppermute x1 -> x4, starting transfers between devices: 2.35 us -> 9.97 us  [shifted(): lax.ppermute(value, axis, [(source, source + steps) for source in range(l...]
    add x1, other arithmetic: 0.28 us -> 4.1 us  [on_device(): got[:, :, :width].astype(F32) + jnp.where(ranks == 0, extra[:, None], 0.0)]
    ppermute x0 -> x3, starting transfers between devices: none -> 3.57 us  [on_device(): more.append(lax.ppermute(send[apart], 'stream', swap))]
    ppermute x1, starting transfers between devices: 0.07 us -> 2.22 us  [on_device(): early = lax.ppermute(pay, 'seq', pairs)]
    pallas_call x1, Pallas kernels: 1.76 us -> 0.06 us  [on_device(): pl.pallas_call(pair_kernel, in_specs=[smem, whole((PAY, width)), whole((P...]
  transfers between devices with their start and end apart: 4 -> 10, of which waited for: 1 -> 2; matrix products, arithmetic and copies ran while one was open for 1% -> 2% of each run, Pallas kernels for 15% -> 32%
where the time goes in v5:
time: 115 us; the launch traced here: 113 us
  Pallas kernels  78.9 us (69%)
  starting transfers between devices  20.3 us (18%)
  local copies, waits for them, and re-layouts  7.14 us (6%)
  other arithmetic  4.61 us (4%)
  waiting for transfers between devices  1.46 us (1%)
    pallas_call x3, Pallas kernels, outputs(): pl.pallas_call(functools.partial(output_kernel, first, bool(hold)), grid_...  26.5 us
    pallas_call x1, Pallas kernels, on_device(): pl.pallas_call(states_kernel, grid_spec=prefetch(grid=(steps,), in_specs=...  24.2 us
    pallas_call x1, Pallas kernels, on_device(): pl.pallas_call(conv_kernel, grid=(steps,), in_specs=[smem, smem, smem, by...  17.7 us
    ppermute x4, starting transfers between devices, shifted(): lax.ppermute(value, axis, [(source, source + steps) for source in range(l...  9.97 us
    pallas_call x1, Pallas kernels, on_device(): pl.pallas_call(correct_kernel, grid_spec=prefetch(grid=(steps,), in_specs...  9.58 us
    all_to_all x1, starting transfers between devices, on_device(): lax.all_to_all(fin.reshape(owners, CAP, rows, N), 'stream', split_axis=0,...  4.48 us
    add x1, other arithmetic, on_device(): got[:, :, :width].astype(F32) + jnp.where(ranks == 0, extra[:, None], 0.0)  4.1 us
    unnamed x22, local copies, waits for them, and re-layouts  3.92 us
  transfers between devices with their start and end apart: 10, of which 2 were waited for; matrix products, arithmetic and copies ran while one was open for 2% of the time, Pallas kernels for 32%

profile of v5, /device:TPU:0, one launch (start us, length us, event | category | flops | bytes accessed | tf_op | source)
XLA Modules:
  0.0 113.3 jit_solution(15944778923026584225)
XLA Ops:
  0.6 0.8 slice_bitcast_fusion
  1.4 2.3 %collective-permute-start = (bf16[16,1280]{1,0:T(8,128)(2,1)S(1)}, bf16[16,1280]{1,0:T(8,128)(2,1)S(1)}, u32[]{:S(2)}, u32[]{:S(2)}) collective-permute-start(bf16[16,1280]{1,0:T(8,128)(2,1)S(1)} %slice_bitcast_fusion), channel_id=1, source_target_pairs={{0,1},{1,2},{2,3},{3,4},{4,5},{5,6},{6,7},{8,9},{9,10},{10,11},{11... | collective-permute-start | bytes 122888 | tf_op jit(solution)/shard_map/ppermute | solution.py:30
  3.8 0.7 broadcast_in_dim.85.bias_ref
  4.6 0.7 copy-done.5
  6.7 0.9 copy-done.8
  7.6 0.9 copy-done.9
  8.5 17.7 %conv.1 = (bf16[4096,1280]{1,0:T(8,128)(2,1)}, bf16[8,32,128]{2,1,0:T(8,128)(2,1)S(1)}, s32[16]{0:T(128)S(1)}) custom-call(s32[1]{0:T(128)} %bitcast.shard_ref, s32[1,32]{1,0:T(1,128)S(1)} %copy-done.6, s32[1,32]{1,0:T(1,128)S(1)} %copy-done.7, bf16[4096,1280]{1,0:T(8,128)(2,1)} %bitcast.23, bf16[16,1280]{1,0:T(8,128)(2,1)S(1)} %collective-permute-done.rim_ref, ...), custom_call_target="tpu_custom_call" | custom-call | flops 4194304000 | bytes 22020096 | tf_op jit(solution)/shard_map/conv/pallas_call | solution.py:454
  26.3 24.2 %states.1 = (f32[16,4096]{1,0:T(8,128)S(1)}, f32[16,4096]{1,0:T(8,128)S(1)}, bf16[32,128,1024]{2,1,0:T(8,128)(2,1)}, bf16[144,1024]{1,0:T(8,128)(2,1)S(1)}, bf16...) custom-call(s32[16]{0:T(128)S(1)} %get-tuple-element.28.meta, bf16[4096,1280]{1,0:T(8,128)(2,1)} %get-tuple-element.29.act_ref.c_ref, ...), custom_call_target="tpu_custom_call" | custom-call | flops 2147483648 | bytes 23068672 | tf_op jit(solution)/shard_map/states/pallas_call | solution.py:479
  50.5 2.2 %collective-permute-start.1 = (bf16[144,1024]{1,0:T(8,128)(2,1)S(1)}, bf16[144,1024]{1,0:T(8,128)(2,1)S(1)}, u32[]{:S(2)}, u32[]{:S(2)}) collective-permute-start(bf16[144,1024]{1,0:T(8,128)(2,1)S(1)} %get-tuple-element.31.own_ref), channel_id=1, source_target_pairs={{0,1},{1,0},{2,3},{3,2},{4,5},{5,4},{6,7},{7,6},{8,9},{9,8},{10,11... | collective-permute-start | bytes 884744 | tf_op jit(solution)/shard_map/ppermute | solution.py:545
  52.9 5.3 %outputs.3.refs_0_ = bf16[4096,1024]{1,0:T(8,128)(2,1)} custom-call(s32[16]{0:T(128)S(1)} %get-tuple-element.28.meta, bf16[4096,1280]{1,0:T(8,128)(2,1)} %get-tuple-element.29.act_ref.c_ref, f32[16,4096]{1,0:T(8,128)S(1)} %bitcast.16, f32[16,4096]{1,0:T(8,128)S(1)} %get-tuple-element.32.cum_ref, bf16[32,128,1024]{2,1,0:T(8,128)(2,1)} %get-tuple-element.33.sin_ref, ...), custom_call_target="tpu_custom_call" | custom-call | flops 536870912 | bytes 4194304 | tf_op jit(solution)/shard_map/outputs/pallas_call | solution.py:518
  58.2 4.5 %all-to-all-start = ((bf16[4,2,1056,128]{3,2,1,0:T(8,128)(2,1)}), bf16[4,2,1056,128]{3,2,1,0:T(8,128)(2,1)}, u32[]{:S(2)}, u32[]{:S(2)}) async-start(bf16[4,2,1056,128]{3,2,1,0:T(8,128)(2,1)} %bitcast.5), calls=%async_computation | async-start | bytes 4325376 | tf_op jit(solution)/shard_map/all_to_all | solution.py:559
  62.7 3.9 %collective-permute-start.2 = (bf16[144,512]{1,0:T(8,128)(2,1)S(1)}, bf16[144,512]{1,0:T(8,128)(2,1)S(1)}, u32[]{:S(2)}, u32[]{:S(2)}) collective-permute-start(bf16[144,512]{1,0:T(8,128)(2,1)S(1)} %pair.1), channel_id=1, source_target_pairs={{0,6},{1,7},{8,14},{9,15},{16,22},{17,23},{24,30},{25,31}} | collective-permute-start | bytes 442376 | tf_op jit(solution)/shard_map/ppermute | solution.py:30
  66.6 1.3 %collective-permute-start.3 = (bf16[144,512]{1,0:T(8,128)(2,1)S(1)}, bf16[144,512]{1,0:T(8,128)(2,1)S(1)}, u32[]{:S(2)}, u32[]{:S(2)}) collective-permute-start(bf16[144,512]{1,0:T(8,128)(2,1)S(1)} %pair.1), channel_id=1, source_target_pairs={{0,4},{1,5},{2,6},{3,7},{8,12},{9,13},{10,14},{11,15},{16,20},{17,... | collective-permute-start | bytes 442376 | tf_op jit(solution)/shard_map/ppermute | solution.py:30
  67.9 2.5 %collective-permute-start.4 = (bf16[144,512]{1,0:T(8,128)(2,1)S(1)}, bf16[144,512]{1,0:T(8,128)(2,1)S(1)}, u32[]{:S(2)}, u32[]{:S(2)}) collective-permute-start(bf16[144,512]{1,0:T(8,128)(2,1)S(1)} %pair.1), channel_id=1, source_target_pairs={{0,2},{1,3},{2,4},{3,5},{4,6},{5,7},{8,10},{9,11},{10,12},{11,13},... | collective-permute-start | bytes 442376 | tf_op jit(solution)/shard_map/ppermute | solution.py:30
  70.3 13.8 %outputs.4.refs_0_ = bf16[4096,1024]{1,0:T(8,128)(2,1)} custom-call(s32[16]{0:T(128)S(1)} %get-tuple-element.28.meta, bf16[4096,1280]{1,0:T(8,128)(2,1)} %get-tuple-element.29.act_ref.c_ref, f32[16,4096]{1,0:T(8,128)S(1)} %bitcast.17, f32[16,4096]{1,0:T(8,128)S(1)} %get-tuple-element.32.cum_ref, ...), custom_call_target="tpu_custom_call", output_to_operand_aliasing={{}: (7, {})} | custom-call | flops 2684354560 | bytes 20971520 | tf_op jit(solution)/shard_map/outputs/pallas_call | solution.py:518
  84.4 7.4 %outputs.5.base_ref = bf16[4096,1024]{1,0:T(8,128)(2,1)} custom-call(s32[16]{0:T(128)S(1)} %get-tuple-element.28.meta, bf16[4096,1280]{1,0:T(8,128)(2,1)} %get-tuple-element.29.act_ref.c_ref, f32[16,4096]{1,0:T(8,128)S(1)} %bitcast.18, f32[16,4096]{1,0:T(8,128)S(1)} %get-tuple-element.32.cum_ref, ...), custom_call_target="tpu_custom_call", output_to_operand_aliasing={{}: (7, {})} | custom-call | flops 1073741824 | bytes 8388608 | tf_op jit(solution)/shard_map/outputs/pallas_call | solution.py:518
  91.8 0.8 carry.1
  92.6 2.0 %collective-permute-start.8 = (bf16[1024,128]{1,0:T(8,128)(2,1)S(1)}, bf16[1024,128]{1,0:T(8,128)(2,1)S(1)}, u32[]{:S(2)}, u32[]{:S(2)}) collective-permute-start(bf16[1024,128]{1,0:T(8,128)(2,1)S(1)} %get-tuple-element.51), channel_id=1, source_target_pairs={{0,8},{8,0},{16,24},{24,16},{1,9},{9,1},{17,25},{25,17},{2,10},{10... | collective-permute-start | bytes 786440 | tf_op jit(solution)/shard_map/ppermute | solution.py:587
  94.6 1.5 %collective-permute-start.7 = (bf16[1024,128]{1,0:T(8,128)(2,1)S(1)}, bf16[1024,128]{1,0:T(8,128)(2,1)S(1)}, u32[]{:S(2)}, u32[]{:S(2)}) collective-permute-start(bf16[1024,128]{1,0:T(8,128)(2,1)S(1)} %get-tuple-element.50), channel_id=1, source_target_pairs={{0,16},{8,24},{16,0},{24,8},{1,17},{9,25},{17,1},{25,9},{2,18},{10... | collective-permute-start | bytes 786440 | tf_op jit(solution)/shard_map/ppermute | solution.py:587
  96.2 0.9 slice.15
  97.1 0.7 reshape.66
  97.8 9.6 %correct.1 = bf16[4096,1024]{1,0:T(8,128)(2,1)} custom-call(s32[16]{0:T(128)S(1)} %get-tuple-element.28.meta, bf16[4096,1024]{1,0:T(8,128)(2,1)} %outputs.5.base_ref, bf16[4096,1280]{1,0:T(8,128)(2,1)} %get-tuple-element.29.act_ref.c_ref, f32[16,4096]{1,0:T(8,128)S(1)} %get-tuple-element.44.carry_ref, ...), custom_call_target="tpu_custom_call", output_to_operand_aliasing={{}: (1, {})} | custom-call | flops 1073741824 | bytes 18874368 | tf_op jit(solution)/shard_map/correct/pallas_call | solution.py:589
  107.4 1.3 %collective-permute-done.7 = bf16[1024,128]{1,0:T(8,128)(2,1)S(1)} collective-permute-done((bf16[1024,128]{1,0:T(8,128)(2,1)S(1)}, bf16[1024,128]{1,0:T(8,128)(2,1)S(1)}, u32[]{:S(2)}, u32[]{:S(2)}) %collective-permute-start.7) | collective-permute-done | bytes 262176 | tf_op jit(solution)/shard_map/ppermute | solution.py:587
  109.1 4.1 %select_add_fusion = f32[4,2,1024,128]{3,2,1,0:T(8,128)} fusion(f32[4,1024,128]{2,1,0:T(8,128)S(1)} %select_select_fusion, bf16[4,2,1056,128]{3,2,1,0:T(8,128)(2,1)} %all-to-all-done, pred[2]{0:T(512)(128)(4,1)S(1)} %iota_compare_fusion), kind=kLoop, calls=%fused_computation | loop fusion | flops 3145728 | bytes 8388610 | tf_op jit(solution)/shard_map/add | solution.py:615
  (44 shorter events, 2.5 us)
Async XLA Ops:
  1.4 3.2 %collective-permute-start = (bf16[16,1280]{1,0:T(8,128)(2,1)S(1)}, bf16[16,1280]{1,0:T(8,128)(2,1)S(1)}, u32[]{:S(2)}, u32[]{:S(2)}) collective-permute-start(bf16[16,1280]{1,0:T(8,128)(2,1)S(1)} %slice_bitcast_fusion), channel_id=1, source_target_pairs={{0,1},{1,2},{2,3},{3,4},{4,5},{5,6},{6,7},{8,9},{9,10},{10,11},{11... | collective-permute-start | bytes 122888 | tf_op jit(solution)/shard_map/ppermute | solution.py:30
  4.6 0.7 copy-start.5
  5.3 0.7 copy-start.6
  6.0 0.7 copy-start.7
  6.7 0.9 copy-start.8
  7.6 0.9 copy-start.9
  8.5 17.7 %copy-start = (f32[1,16,4096]{2,1,0:T(8,128)S(1)}, f32[1,16,4096]{2,1,0:T(8,128)}, u32[]{:S(2)}) copy-start(f32[1,16,4096]{2,1,0:T(8,128)} %param.16) | copy-start | bytes 786436
  8.5 17.7 %copy-start.1 = (bf16[32,1024]{1,0:T(8,128)(2,1)S(1)}, bf16[32,1024]{1,0:T(8,128)(2,1)}, u32[]{:S(2)}) copy-start(bf16[32,1024]{1,0:T(8,128)(2,1)} %constant.33.clone.rep16_ref) | copy-start | bytes 196612
  8.5 17.7 %copy-start.2 = (f32[1,16,4096]{2,1,0:T(8,128)S(1)}, f32[1,16,4096]{2,1,0:T(8,128)}, u32[]{:S(2)}) copy-start(f32[1,16,4096]{2,1,0:T(8,128)} %param.17) | copy-start | bytes 786436
  8.5 17.8 %copy-start.3 = (f32[16,1024]{1,0:T(8,128)S(1)}, f32[16,1024]{1,0:T(8,128)}, u32[]{:S(2)}) copy-start(f32[16,1024]{1,0:T(8,128)} %constant.32.clone.rep_ref) | copy-start | bytes 196612
  8.5 17.8 %copy-start.4 = (bf16[128,128]{1,0:T(8,128)(2,1)S(1)}, bf16[128,128]{1,0:T(8,128)(2,1)}, u32[]{:S(2)}) copy-start(bf16[128,128]{1,0:T(8,128)(2,1)} %constant.34.clone.tri_ref) | copy-start | bytes 98308
  26.3 26.4 %copy-start.10 = (f32[16]{0:T(128)S(1)}, f32[16]{0:T(128)}, u32[]{:S(2)}) copy-start(f32[16]{0:T(128)} %param.18) | copy-start | bytes 196
  50.5 7.6 %collective-permute-start.1 = (bf16[144,1024]{1,0:T(8,128)(2,1)S(1)}, bf16[144,1024]{1,0:T(8,128)(2,1)S(1)}, u32[]{:S(2)}, u32[]{:S(2)}) collective-permute-start(bf16[144,1024]{1,0:T(8,128)(2,1)S(1)} %get-tuple-element.31.own_ref), channel_id=1, source_target_pairs={{0,1},{1,0},{2,3},{3,2},{4,5},{5,4},{6,7},{7,6},{8,9},{9,8},{10,11... | collective-permute-start | bytes 884744 | tf_op jit(solution)/shard_map/ppermute | solution.py:545
  58.2 33.6 %all-to-all-start = ((bf16[4,2,1056,128]{3,2,1,0:T(8,128)(2,1)}), bf16[4,2,1056,128]{3,2,1,0:T(8,128)(2,1)}, u32[]{:S(2)}, u32[]{:S(2)}) async-start(bf16[4,2,1056,128]{3,2,1,0:T(8,128)(2,1)} %bitcast.5), calls=%async_computation | async-start | bytes 4325376 | tf_op jit(solution)/shard_map/all_to_all | solution.py:559
  62.7 21.5 %collective-permute-start.2 = (bf16[144,512]{1,0:T(8,128)(2,1)S(1)}, bf16[144,512]{1,0:T(8,128)(2,1)S(1)}, u32[]{:S(2)}, u32[]{:S(2)}) collective-permute-start(bf16[144,512]{1,0:T(8,128)(2,1)S(1)} %pair.1), channel_id=1, source_target_pairs={{0,6},{1,7},{8,14},{9,15},{16,22},{17,23},{24,30},{25,31}} | collective-permute-start | bytes 442376 | tf_op jit(solution)/shard_map/ppermute | solution.py:30
  66.6 17.6 %collective-permute-start.3 = (bf16[144,512]{1,0:T(8,128)(2,1)S(1)}, bf16[144,512]{1,0:T(8,128)(2,1)S(1)}, u32[]{:S(2)}, u32[]{:S(2)}) collective-permute-start(bf16[144,512]{1,0:T(8,128)(2,1)S(1)} %pair.1), channel_id=1, source_target_pairs={{0,4},{1,5},{2,6},{3,7},{8,12},{9,13},{10,14},{11,15},{16,20},{17,... | collective-permute-start | bytes 442376 | tf_op jit(solution)/shard_map/ppermute | solution.py:30
  67.9 16.3 %collective-permute-start.4 = (bf16[144,512]{1,0:T(8,128)(2,1)S(1)}, bf16[144,512]{1,0:T(8,128)(2,1)S(1)}, u32[]{:S(2)}, u32[]{:S(2)}) collective-permute-start(bf16[144,512]{1,0:T(8,128)(2,1)S(1)} %pair.1), channel_id=1, source_target_pairs={{0,2},{1,3},{2,4},{3,5},{4,6},{5,7},{8,10},{9,11},{10,12},{11,13},... | collective-permute-start | bytes 442376 | tf_op jit(solution)/shard_map/ppermute | solution.py:30
  84.3 7.5 %collective-permute-start.5 = (bf16[128,512]{1,0:T(8,128)(2,1)S(1)}, bf16[128,512]{1,0:T(8,128)(2,1)S(1)}, u32[]{:S(2)}, u32[]{:S(2)}) collective-permute-start(bf16[128,512]{1,0:T(8,128)(2,1)S(1)} %prefix.1.mine_ref), channel_id=1, source_target_pairs={{0,1},{1,0},{2,3},{3,2},{4,5},{5,4},{6,7},{7,6},{8,9},{9,8},{10,11... | collective-permute-start | bytes 393224 | tf_op jit(solution)/shard_map/ppermute | solution.py:572
  92.6 14.8 %collective-permute-start.8 = (bf16[1024,128]{1,0:T(8,128)(2,1)S(1)}, bf16[1024,128]{1,0:T(8,128)(2,1)S(1)}, u32[]{:S(2)}, u32[]{:S(2)}) collective-permute-start(bf16[1024,128]{1,0:T(8,128)(2,1)S(1)} %get-tuple-element.51), channel_id=1, source_target_pairs={{0,8},{8,0},{16,24},{24,16},{1,9},{9,1},{17,25},{25,17},{2,10},{10... | collective-permute-start | bytes 786440 | tf_op jit(solution)/shard_map/ppermute | solution.py:587
  94.6 14.1 %collective-permute-start.7 = (bf16[1024,128]{1,0:T(8,128)(2,1)S(1)}, bf16[1024,128]{1,0:T(8,128)(2,1)S(1)}, u32[]{:S(2)}, u32[]{:S(2)}) collective-permute-start(bf16[1024,128]{1,0:T(8,128)(2,1)S(1)} %get-tuple-element.50), channel_id=1, source_target_pairs={{0,16},{8,24},{16,0},{24,8},{1,17},{9,25},{17,1},{25,9},{2,18},{10... | collective-permute-start | bytes 786440 | tf_op jit(solution)/shard_map/ppermute | solution.py:587
  96.1 12.7 %collective-permute-start.6 = (bf16[1024,128]{1,0:T(8,128)(2,1)S(1)}, bf16[1024,128]{1,0:T(8,128)(2,1)S(1)}, u32[]{:S(2)}, u32[]{:S(2)}) collective-permute-start(bf16[1024,128]{1,0:T(8,128)(2,1)S(1)} %get-tuple-element.49), channel_id=1, source_target_pairs={{0,24},{8,16},{16,8},{24,0},{1,25},{9,17},{17,9},{25,1},{2,26},{10... | collective-permute-start | bytes 786440 | tf_op jit(solution)/shard_map/ppermute | solution.py:587
